TPU v7x, 256 devices: a whole 4x4x8 slice. The times are simulated.
256 devices in a mesh: dp: 16 (over z, core), row: 4 (over y), col: 4 (over x).
Axes of the slice: x: 4, y: 4, z: 8, core: 2. Of those that a mesh axis runs over, the one named last changes fastest.
Arguments:
- grad_parts: bfloat16 [16, 16, 256, 10240], P('dp', None, 'row', 'col'), may hold values from -64 to 64
- row_old: float32 [16, 256], P('dp', 'row'), may hold values from 0.1 to 2
- col_old: float32 [10240], P('col'), may hold values from 0.1 to 2
Outputs:
- update: float32 [16, 256, 10240], P('dp', 'row', 'col')
- row_new: float32 [16, 256], P('dp', 'row')
- col_new: float32 [10240], P('col')
- update_rms: float32 [], replicated
All inputs are finite; a program needn't handle non-finite values.
Results may differ from a plain program's by a relative error of at most 0.0003.
Values sent between devices are 32-bit elements; how exact they have to be, the bound alone decides.
No kernel may reach another device: no remote copies, remote signals or barrier semaphores. Data moves between devices by JAX's collectives and lax.ppermute only.
A program may use at most 64 MiB of HBM per device.

v0:
```python
import jax
import jax.numpy as jnp
from jax import lax
from jax.sharding import PartitionSpec as P

D = 4096
FF = 10240


def on_device(grad_parts, row_old, col_old):
    terms = grad_parts[0].astype(jnp.float32)
    grad = lax.psum_scatter(terms, "dp", scatter_dimension=0, tiled=True)
    square = grad * grad + 1e-30
    row_part = jnp.sum(square, axis=2)
    col_part = jnp.sum(square, axis=(0, 1))
    row_total = lax.psum(row_part, "col")
    col_total = lax.psum(col_part, ("dp", "row"))
    row_new = 0.8 * row_old + 0.2 * row_total / FF
    col_new = 0.8 * col_old + 0.2 * col_total / D
    row_mean = lax.psum(jnp.sum(row_new), ("dp", "row")) / D
    scaled = grad * jnp.sqrt(row_mean / (row_new[:, :, None] * col_new[None, None, :]))
    total = lax.psum(jnp.sum(scaled * scaled), ("dp", "row", "col"))
    update_rms = jnp.sqrt(total / (D * FF))
    update = scaled / jnp.maximum(1.0, update_rms)
    return (update, row_new, col_new, update_rms)


def solution(mesh):
    return jax.shard_map(
        on_device,
        mesh=mesh,
        in_specs=(P("dp", None, "row", "col"), P("dp", "row"), P("col")),
        out_specs=(P("dp", "row", "col"), P("dp", "row"), P("col"), P()),
        check_vma=False,
    )
```

profile of v0, /device:TPU:1, one launch (start us, length us, event | category | flops | bytes accessed | tf_op | source)
XLA Modules:
  0.0 438.6 jit_solution(11287304878155187438)
XLA Ops:
  7.2 0.0 copy-start.3
  7.2 0.0 copy-start.1
  7.2 0.0 reduce-scatter.2.cloned.1.call-start
  7.2 7.9 %bitcast_convert_fusion = f32[16,64,2560]{2,1,0:T(8,128)} fusion(bf16[1,16,64,2560]{3,2,1,0:T(8,128)(2,1)} %param.3), kind=kLoop, calls=%fused_computation | loop fusion | flops 2621440 | bytes 15728640 | tf_op jit(solution)/shard_map/convert_element_type | solution.py:11
  15.2 0.0 reduce-scatter.2.cloned.1.call-update
  15.2 76.4 %reduce-scatter.2.cloned.1.call-done = f32[1,64,2560]{2,1,0:T(8,128)} async-done(((f32[16,64,2560]{2,1,0:T(8,128)}), f32[1,64,2560]{2,1,0:T(8,128)}) %reduce-scatter.2.cloned.1.call-update) | async-done | bytes 655376 | tf_op jit(solution)/shard_map/reduce_scatter | solution.py:12
  91.5 1.3 fusion.1
  92.8 8.5 %psum.28 = f32[1,64]{1,0:T(1,128)S(1)} all-reduce(f32[1,64]{1,0:T(1,128)S(1)} %bitcast.7), channel_id=1, replica_groups=mesh['dp'=16,'row'=4,'col'=4] {'col'}, use_global_device_ids=true, to_apply=%region_2.0 | all-reduce | flops 64 | bytes 512 | tf_op jit(solution)/shard_map/psum | solution.py:16
  101.3 0.0 copy-done.3
  101.3 0.6 fusion.2
  101.9 0.0 copy-start.2
  101.9 247.6 %all-reduce = (f32[2560]{0:T(1024)S(1)}, f32[]{:T(128)}) all-reduce(f32[2560]{0:T(1024)S(1)} %get-tuple-element.5, f32[]{:T(128)} %get-tuple-element.8), channel_id=1, replica_groups=mesh['dp'=16,'row'=4,'col'=4] {'dp','row'}, use_global_device_ids=true, to_apply=%region_6.0 | all-reduce | flops 2561 | bytes 20488 | tf_op jit(solution)/shard_map/psum | solution.py:17
  350.2 0.0 copy-done.1
  350.2 0.0 copy-start
  350.2 2.1 multiply_reduce_fusion
  352.3 75.4 %psum.31 = f32[]{:T(128)} all-reduce(f32[]{:T(128)} %multiply_reduce_fusion), channel_id=1, replica_groups=mesh['dp'=16,'row'=4,'col'=4] {'dp','row','col'}, use_global_device_ids=true, to_apply=%region_8.0 | all-reduce | flops 1 | bytes 8 | tf_op jit(solution)/shard_map/psum | solution.py:22
  428.4 2.3 broadcast_divide_fusion
  430.7 0.0 copy-done.2
  430.7 0.0 copy-done
  (1 shorter events, 0.0 us)
Async XLA Ops:
  7.2 94.2 %copy-start.3 = (f32[1,64]{1,0:T(1,128)S(1)}, f32[1,64]{1,0:T(1,128)}, u32[]{:S(2)}) copy-start(f32[1,64]{1,0:T(1,128)} %param.4) | copy-start | bytes 772
  7.2 343.0 %copy-start.1 = (f32[2560]{0:T(1024)S(1)}, f32[2560]{0:T(1024)}, u32[]{:S(2)}) copy-start(f32[2560]{0:T(1024)} %param.5) | copy-start | bytes 30724
  7.2 84.4 %reduce-scatter.2.cloned.1.call-start = ((), (), s32[]{:S(2)}) async-start(), calls=%async_computation.1 | async-start | bytes 11141120 | tf_op jit(solution)/shard_map/reduce_scatter | solution.py:12
  101.9 328.7 %copy-start.2 = (f32[1,64]{1,0:T(1,128)}, f32[1,64]{1,0:T(1,128)S(1)}, u32[]{:S(2)}) copy-start(f32[1,64]{1,0:T(1,128)S(1)} %get-tuple-element.9) | copy-start | bytes 772
  350.2 80.4 %copy-start = (f32[2560]{0:T(1024)}, f32[2560]{0:T(1024)S(1)}, u32[]{:S(2)}) copy-start(f32[2560]{0:T(1024)S(1)} %multiply_add_fusion.1) | copy-start | bytes 30724
Sparse Core Ops, SparseCore 0:
  15.3 76.1 reduce-scatter.1
where the time goes:
time: 439 us
  blocking collectives  332 us (76%)
  waiting for transfers between devices  76.4 us (17%)
  between operations  16.6 us (4%)
  other arithmetic  14.1 us (3%)
    psum x1, blocking collectives, on_device(): col_total = lax.psum(col_part, ('dp', 'row'))  248 us
    reduce_scatter x1, waiting for transfers between devices, on_device(): grad = lax.psum_scatter(terms, 'dp', scatter_dimension=0, tiled=True)  76.4 us
    psum x1, blocking collectives, on_device(): total = lax.psum(jnp.sum(scaled * scaled), ('dp', 'row', 'col'))  75.4 us
  transfers between devices with their start and end apart: 1, of which 1 were waited for; matrix products, arithmetic and copies ran while one was open for 0% of the time, Pallas kernels for 0%

commit v1 on v0

v1 whole, which is shorter than its diff:
```python
import functools

import jax
import jax.numpy as jnp
from jax import lax
from jax.experimental import pallas as pl
from jax.experimental.pallas import tpu as pltpu
from jax.sharding import PartitionSpec as P

D = 4096
FF = 10240
HALF = 32
ROWS = 64
COLS = 2560
ORDER = (2, 3, 1)

SWAP = [(i, i ^ 1) for i in range(16)]
UP = [(i, (i + 2) % 16) for i in range(16)]
DOWN = [(i, (i - 2) % 16) for i in range(16)]

VMEM = pl.BlockSpec(memory_space=pltpu.VMEM)
HBM = pl.BlockSpec(memory_space=pltpu.HBM)
ANY = pl.BlockSpec(memory_space=pl.ANY)
PARAMS = pltpu.CompilerParams(vmem_limit_bytes=8 * 1024 * 1024)


def told(micros):
    return pl.CostEstimate(flops=int(micros * 1.15e9), bytes_accessed=0, transcendentals=0)


def fetch_kernel(ks, n_in, parts, *refs):
    own, sent, buf, own_sems, sems = refs[n_in:]
    me = lax.axis_index("dp")
    core = jnp.bitwise_and(me, 1)
    own_copies, copies = [], []
    for i, k in enumerate(ks):
        dest = 2 * jnp.bitwise_and(lax.shift_right_logical(me, 1) + (k + 8), 7)
        copies.append(pltpu.make_async_copy(parts.at[dest + 1 - core], buf.at[i], sems.at[i]))
        own_copies.append(pltpu.make_async_copy(parts.at[dest + core], own.at[i], own_sems.at[i]))
    for copy in copies + own_copies:
        copy.start()
    for i, copy in enumerate(copies):
        copy.wait()
        sent[i] = buf[i].astype(jnp.float32)
    for copy in own_copies:
        copy.wait()


def fetch(ks, parts, *after, micros=0):
    n = len(ks)
    own, sent = pl.pallas_call(
        functools.partial(fetch_kernel, ks, len(after)),
        out_shape=[
            jax.ShapeDtypeStruct((n, ROWS, COLS), jnp.bfloat16),
            jax.ShapeDtypeStruct((n, ROWS, COLS), jnp.float32),
        ],
        in_specs=[HBM] + [ANY] * len(after),
        out_specs=[VMEM, VMEM],
        scratch_shapes=[
            pltpu.VMEM((n, ROWS, COLS), jnp.bfloat16),
            pltpu.SemaphoreType.DMA((n,)),
            pltpu.SemaphoreType.DMA((n,)),
        ],
        compiler_params=PARAMS,
        cost_estimate=told(micros),
    )(parts, *after)
    return own, lax.ppermute(sent, "dp", SWAP)


def add_kernel(terms, n_in, own, sib, *refs):
    outs = refs[n_in:]
    for i, (block, half, has_state) in enumerate(terms):
        rows = slice(half * HALF, (half + 1) * HALF)
        total = own[block, rows].astype(jnp.float32) + sib[block, rows]
        if has_state:
            total = total + refs[i][...]
        outs[i][...] = total


def add(blocks, terms, states=(), after=(), micros=40):
    return pl.pallas_call(
        functools.partial(add_kernel, [(*t, bool(states)) for t in terms], len(states) + len(after)),
        out_shape=[jax.ShapeDtypeStruct((HALF, COLS), jnp.float32)] * len(terms),
        in_specs=[VMEM] * (2 + len(states)) + [ANY] * len(after),
        out_specs=[VMEM] * len(terms),
        compiler_params=PARAMS,
        cost_estimate=told(micros),
    )(*blocks, *states, *after)


def final_kernel(scaled, row_sum, total, out, rms, buf, sems):
    row_mean = jnp.sum(row_sum[...], keepdims=True) / D
    update_rms = jnp.sqrt(row_mean * jnp.sum(total[...], keepdims=True) / (D * FF))
    rms[...] = update_rms
    factor = jnp.sqrt(row_mean) / jnp.maximum(1.0, update_rms)
    copies = []
    for i in range(4):
        rows = pl.ds(16 * i, 16)
        buf[rows] = scaled[rows] * factor
        copies.append(pltpu.make_async_copy(buf.at[rows], out.at[rows], sems.at[i]))
        copies[i].start()
    for copy in copies:
        copy.wait()


def final(scaled, row_sum, total):
    return pl.pallas_call(
        final_kernel,
        out_shape=[
            jax.ShapeDtypeStruct((ROWS, COLS), jnp.float32),
            jax.ShapeDtypeStruct((1, 1), jnp.float32),
        ],
        in_specs=[VMEM, VMEM, VMEM],
        out_specs=[HBM, VMEM],
        scratch_shapes=[pltpu.VMEM((ROWS, COLS), jnp.float32), pltpu.SemaphoreType.DMA((4,))],
        compiler_params=PARAMS,
        cost_estimate=told(1),
    )(scaled, row_sum, total)


def places():
    return [(z, c, y, x) for z in range(8) for c in range(2) for y in range(4) for x in range(4)]


def number(z, c, y, x):
    return ((2 * z + c) * 4 + y) * 4 + x


def exchange(v, mask, idle=None):
    pairs = []
    for z, c, y, x in places():
        dz, dy, dx = mask if c == 1 or idle is None else idle
        pairs.append((number(z, c, y, x), number(z ^ dz, c, y ^ dy, x ^ dx)))
    return lax.ppermute(v, ("dp", "row", "col"), pairs)


def sum_four(v, axis, idle=None):
    unit = [0, 0, 0]
    got = {}
    for mask in ORDER:
        unit[axis] = mask
        got[mask] = exchange(v, tuple(unit), idle)
    return (got[2] + got[3]) + (got[1] + v)


def on_device(grad_parts, row_old, col_old):
    parts = pltpu.with_memory_space_constraint(grad_parts[0], pltpu.HBM)
    core_one = jnp.bitwise_and(lax.axis_index("dp"), 1) == 1

    def up(x):
        return lax.ppermute(x, "dp", UP)

    def down(x):
        return lax.ppermute(x, "dp", DOWN)

    far = fetch((4,), parts)
    third = fetch((3, -3), parts, far[0], micros=40)
    a, b = add(far, ((0, 0), (0, 1)), after=(third[0],))
    after = a
    a, b = up(a), down(b)
    c, d = add(third, ((0, 1), (1, 0)), after=(after,))
    second = fetch((2, -2), parts, c)
    near = fetch((1, -1, 0), parts, second[0])
    c, d = up(c), down(d)
    a, b = add(third, ((0, 0), (1, 1)), (a, b), after=(near[0],))
    after = a
    a, b = up(a), down(b)
    c, d = add(second, ((0, 1), (1, 0)), (c, d), after=(after,))
    after = c
    c, d = up(c), down(d)
    a, b = add(second, ((0, 0), (1, 1)), (a, b), after=(after,))
    after = a
    a, b = up(a), down(b)
    c, d = add(near, ((0, 1), (1, 0)), (c, d), after=(after,))
    after = c
    c, d = up(c), down(d)
    a, b = add(near, ((0, 0), (1, 1)), (a, b), after=(after,))
    after = a
    a, b = up(a), down(b)
    upper, lower = add(near, ((2, 0), (2, 1)), (d, c), after=(after,))
    grad = jnp.concatenate([upper + a, lower + b], axis=0)

    square = grad * grad
    row_part = jnp.sum(square + 1e-30, axis=1)
    col_part = jnp.sum(square + 1e-30, axis=0)
    row_total = sum_four(row_part, 2)
    row_new = 0.8 * row_old[0] + 0.2 * row_total / FF
    weighted = jnp.sum(square * (1.0 / row_new)[:, None], axis=0)
    packed = jnp.concatenate([col_part, weighted, row_new, jnp.zeros((64,), jnp.float32)])

    packed = packed + lax.ppermute(packed, "dp", SWAP)
    packed = sum_four(packed, 0, (0, 0, 1))
    packed = packed + exchange(packed, (7, 0, 0), (0, 0, 1))
    packed = sum_four(packed, 1, (0, 0, 1))
    col_new = 0.8 * col_old + 0.2 * packed[:COLS] / D
    total = jnp.sum((packed[COLS:2 * COLS] / col_new).reshape(20, 128), axis=0)
    total = sum_four(total, 2, (0, 1, 0))
    core_one = jnp.bitwise_and(lax.axis_index("dp"), 1) == 1

    packed = jnp.concatenate([col_new, packed[2 * COLS:], total])
    packed = jnp.where(core_one, packed, lax.ppermute(packed, "dp", SWAP))
    col_new, row_sum, total = packed[:COLS], packed[COLS:COLS + 128], packed[COLS + 128:]
    scaled = grad * lax.rsqrt(row_new[:, None] * col_new[None, :])
    update, update_rms = final(scaled, row_sum.reshape(1, 128), total.reshape(1, 128))
    return (update[None], row_new[None], col_new, update_rms.reshape(()))


def solution(mesh):
    return jax.shard_map(
        on_device,
        mesh=mesh,
        in_specs=(P("dp", None, "row", "col"), P("dp", "row"), P("col")),
        out_specs=(P("dp", "row", "col"), P("dp", "row"), P("col"), P()),
        check_vma=False,
    )
```

time: 439 us -> 97 us (0.22)
  blocking collectives: 332 us -> 0 us
  starting transfers between devices: 0.04 us -> 46 us
  waiting for transfers between devices: 76.4 us -> 41.5 us
  between operations: 16.6 us -> 1.04 us
  other arithmetic: 14.1 us -> 0.63 us
  Pallas kernels: 0 us -> 7.52 us
    psum x3 -> x0, blocking collectives: 332 us -> none  [the longest x1 248 us: on_device(): col_total = lax.psum(col_part, ('dp', 'row'))]
    reduce_scatter x1 -> x0, waiting for transfers between devices: 76.4 us -> none  [on_device(): grad = lax.psum_scatter(terms, 'dp', scatter_dimension=0, tiled=True)]
    ppermute x0 -> x33, starting transfers between devices: none -> 46 us  [the longest x7 21.4 us: down(): return lax.ppermute(x, 'dp', DOWN)]
    ppermute x0 -> x33, waiting for transfers between devices: none -> 41.5 us  [the longest x7 22 us: up(): return lax.ppermute(x, 'dp', UP)]
    convert_element_type x1 -> x0, other arithmetic: 7.92 us -> none  [on_device(): terms = grad_parts[0].astype(jnp.float32)]
    pallas_call x0 -> x13, Pallas kernels: none -> 7.52 us  [the longest x4 5.26 us: fetch(): pl.pallas_call(functools.partial(fetch_kernel, ks, len(after)), out_shape...]
  transfers between devices with their start and end apart: 1 -> 33, of which waited for: 1 -> 20; matrix products, arithmetic and copies ran while one was open for 0% -> 0% of each run, Pallas kernels for 0% -> 5%
where the time goes in v1:
time: 97 us; the launch traced here: 96.8 us
  starting transfers between devices  46 us (47%)
  waiting for transfers between devices  41.5 us (43%)
  Pallas kernels  7.52 us (8%)
  between operations  1.04 us (1%)
    ppermute x7, waiting for transfers between devices, up(): return lax.ppermute(x, 'dp', UP)  22 us
    ppermute x7, starting transfers between devices, down(): return lax.ppermute(x, 'dp', DOWN)  21.4 us
    ppermute x13, starting transfers between devices, exchange(): return lax.ppermute(v, ('dp', 'row', 'col'), pairs)  15.6 us
    ppermute x13, waiting for transfers between devices, exchange(): return lax.ppermute(v, ('dp', 'row', 'col'), pairs)  13.4 us
    ppermute x4, starting transfers between devices, fetch(): return (own, lax.ppermute(sent, 'dp', SWAP))  5.55 us
    pallas_call x4, Pallas kernels, fetch(): pl.pallas_call(functools.partial(fetch_kernel, ks, len(after)), out_shape...  5.26 us
    ppermute x7, waiting for transfers between devices, down(): return lax.ppermute(x, 'dp', DOWN)  3.7 us
    ppermute x1, starting transfers between devices, on_device(): packed = packed + lax.ppermute(packed, 'dp', SWAP)  2.81 us
  transfers between devices with their start and end apart: 33, of which 20 were waited for; matrix products, arithmetic and copies ran while one was open for 0% of the time, Pallas kernels for 5%

profile of v1, /device:TPU:1, one launch (start us, length us, event | category | flops | bytes accessed | tf_op | source)
XLA Modules:
  0.0 96.8 jit_solution(16666664798428709769)
XLA Ops:
  1.7 3.3 %collective-permute-start.1 = (f32[1,64,2560]{2,1,0:T(8,128)S(1)}, f32[1,64,2560]{2,1,0:T(8,128)S(1)}, u32[]{:S(2)}, u32[]{:S(2)}) collective-permute-start(f32[1,64,2560]{2,1,0:T(8,128)S(1)} %get-tuple-element.33), channel_id=1, source_target_pairs={{0,16},{16,0},{32,48},{48,32},{64,80},{80,64},{96,112},{112,96},{1... | collective-permute-start | bytes 1966088 | tf_op jit(solution)/shard_map/ppermute | solution.py:67
  6.9 3.9 %collective-permute-start.7 = (f32[32,2560]{1,0:T(8,128)S(1)}, f32[32,2560]{1,0:T(8,128)S(1)}, u32[]{:S(2)}, u32[]{:S(2)}) collective-permute-start(f32[32,2560]{1,0:T(8,128)S(1)} %get-tuple-element.41), channel_id=1, source_target_pairs={{0,224},{16,240},{32,0},{48,16},{64,32},{80,48},{96,64},{112,80},{... | collective-permute-start | bytes 983048 | tf_op jit(solution)/shard_map/ppermute | solution.py:154
  14.6 2.9 %collective-permute-start.5 = (f32[32,2560]{1,0:T(8,128)S(1)}, f32[32,2560]{1,0:T(8,128)S(1)}, u32[]{:S(2)}, u32[]{:S(2)}) collective-permute-start(f32[32,2560]{1,0:T(8,128)S(1)} %get-tuple-element.40), channel_id=1, source_target_pairs={{0,224},{16,240},{32,0},{48,16},{64,32},{80,48},{96,64},{112,80},{... | collective-permute-start | bytes 983048 | tf_op jit(solution)/shard_map/ppermute | solution.py:154
  18.8 2.7 %collective-permute-start.11 = (f32[32,2560]{1,0:T(8,128)S(1)}, f32[32,2560]{1,0:T(8,128)S(1)}, u32[]{:S(2)}, u32[]{:S(2)}) collective-permute-start(f32[32,2560]{1,0:T(8,128)S(1)} %get-tuple-element.45), channel_id=1, source_target_pairs={{0,224},{16,240},{32,0},{48,16},{64,32},{80,48},{96,64},{112,80},{... | collective-permute-start | bytes 983048 | tf_op jit(solution)/shard_map/ppermute | solution.py:154
  21.4 4.2 %collective-permute-done.4.refs_0_ = f32[32,2560]{1,0:T(8,128)S(1)} collective-permute-done((f32[32,2560]{1,0:T(8,128)S(1)}, f32[32,2560]{1,0:T(8,128)S(1)}, u32[]{:S(2)}, u32[]{:S(2)}) %collective-permute-start.4) | collective-permute-done | bytes 327712 | tf_op jit(solution)/shard_map/ppermute | solution.py:151
  27.1 2.7 %collective-permute-start.9 = (f32[32,2560]{1,0:T(8,128)S(1)}, f32[32,2560]{1,0:T(8,128)S(1)}, u32[]{:S(2)}, u32[]{:S(2)}) collective-permute-start(f32[32,2560]{1,0:T(8,128)S(1)} %get-tuple-element.44), channel_id=1, source_target_pairs={{0,224},{16,240},{32,0},{48,16},{64,32},{80,48},{96,64},{112,80},{... | collective-permute-start | bytes 983048 | tf_op jit(solution)/shard_map/ppermute | solution.py:154
  29.8 2.8 %collective-permute-done.10.refs_0_ = f32[32,2560]{1,0:T(8,128)S(1)} collective-permute-done((f32[32,2560]{1,0:T(8,128)S(1)}, f32[32,2560]{1,0:T(8,128)S(1)}, u32[]{:S(2)}, u32[]{:S(2)}) %collective-permute-start.10) | collective-permute-done | bytes 327712 | tf_op jit(solution)/shard_map/ppermute | solution.py:151
  32.8 3.1 %collective-permute-start.15 = (f32[32,2560]{1,0:T(8,128)S(1)}, f32[32,2560]{1,0:T(8,128)S(1)}, u32[]{:S(2)}, u32[]{:S(2)}) collective-permute-start(f32[32,2560]{1,0:T(8,128)S(1)} %get-tuple-element.49), channel_id=1, source_target_pairs={{0,224},{16,240},{32,0},{48,16},{64,32},{80,48},{96,64},{112,80},{... | collective-permute-start | bytes 983048 | tf_op jit(solution)/shard_map/ppermute | solution.py:154
  35.9 3.8 %collective-permute-done.8.refs_0_ = f32[32,2560]{1,0:T(8,128)S(1)} collective-permute-done((f32[32,2560]{1,0:T(8,128)S(1)}, f32[32,2560]{1,0:T(8,128)S(1)}, u32[]{:S(2)}, u32[]{:S(2)}) %collective-permute-start.8) | collective-permute-done | bytes 327712 | tf_op jit(solution)/shard_map/ppermute | solution.py:151
  39.7 3.1 %collective-permute-start.12 = (f32[32,2560]{1,0:T(8,128)S(1)}, f32[32,2560]{1,0:T(8,128)S(1)}, u32[]{:S(2)}, u32[]{:S(2)}) collective-permute-start(f32[32,2560]{1,0:T(8,128)S(1)} %get-tuple-element.47), channel_id=1, source_target_pairs={{0,224},{16,240},{32,0},{48,16},{64,32},{80,48},{96,64},{112,80},{... | collective-permute-start | bytes 983048 | tf_op jit(solution)/shard_map/ppermute | solution.py:154
  42.8 3.8 %collective-permute-done.14.refs_0_ = f32[32,2560]{1,0:T(8,128)S(1)} collective-permute-done((f32[32,2560]{1,0:T(8,128)S(1)}, f32[32,2560]{1,0:T(8,128)S(1)}, u32[]{:S(2)}, u32[]{:S(2)}) %collective-permute-start.14) | collective-permute-done | bytes 327712 | tf_op jit(solution)/shard_map/ppermute | solution.py:151
  46.8 3.1 %collective-permute-start.17 = (f32[32,2560]{1,0:T(8,128)S(1)}, f32[32,2560]{1,0:T(8,128)S(1)}, u32[]{:S(2)}, u32[]{:S(2)}) collective-permute-start(f32[32,2560]{1,0:T(8,128)S(1)} %get-tuple-element.53), channel_id=1, source_target_pairs={{0,224},{16,240},{32,0},{48,16},{64,32},{80,48},{96,64},{112,80},{... | collective-permute-start | bytes 983048 | tf_op jit(solution)/shard_map/ppermute | solution.py:154
  49.9 3.3 %collective-permute-done.12.refs_0_ = f32[32,2560]{1,0:T(8,128)S(1)} collective-permute-done((f32[32,2560]{1,0:T(8,128)S(1)}, f32[32,2560]{1,0:T(8,128)S(1)}, u32[]{:S(2)}, u32[]{:S(2)}) %collective-permute-start.12) | collective-permute-done | bytes 327712 | tf_op jit(solution)/shard_map/ppermute | solution.py:154
  53.4 6.5 %collective-permute-done.16 = f32[32,2560]{1,0:T(8,128)S(1)} collective-permute-done((f32[32,2560]{1,0:T(8,128)S(1)}, f32[32,2560]{1,0:T(8,128)S(1)}, u32[]{:S(2)}, u32[]{:S(2)}) %collective-permute-start.16) | collective-permute-done | bytes 327712 | tf_op jit(solution)/shard_map/ppermute | solution.py:151
  60.5 2.8 %collective-permute-start.18 = (f32[64]{0:T(128)S(1)}, f32[64]{0:T(128)S(1)}, u32[]{:S(2)}, u32[]{:S(2)}) collective-permute-start(f32[64]{0:T(128)S(1)} %add_reduce_fusion.1), channel_id=1, source_target_pairs={{0,2},{1,3},{2,0},{3,1},{4,6},{5,7},{6,4},{7,5},{8,10},{9,11},{10,... | collective-permute-start | bytes 776 | tf_op jit(solution)/shard_map/ppermute | solution.py:134
  64.5 2.5 %collective-permute-done.19 = f32[64]{0:T(128)S(1)} collective-permute-done((f32[64]{0:T(128)S(1)}, f32[64]{0:T(128)S(1)}, u32[]{:S(2)}, u32[]{:S(2)}) %collective-permute-start.19) | collective-permute-done | bytes 288 | tf_op jit(solution)/shard_map/ppermute | solution.py:134
  67.2 2.8 %collective-permute-start.21 = (f32[5248]{0:T(1024)S(1)}, f32[5248]{0:T(1024)S(1)}, u32[]{:S(2)}, u32[]{:S(2)}) collective-permute-start(f32[5248]{0:T(1024)S(1)} %concatenate.10), channel_id=1, source_target_pairs={{0,16},{16,0},{32,48},{48,32},{64,80},{80,64},{96,112},{112,96},{1... | collective-permute-start | bytes 62984 | tf_op jit(solution)/shard_map/ppermute | solution.py:191
  70.9 1.8 %collective-permute-start.22 = (f32[5248]{0:T(1024)S(1)}, f32[5248]{0:T(1024)S(1)}, u32[]{:S(2)}, u32[]{:S(2)}) collective-permute-start(f32[5248]{0:T(1024)S(1)} %add.65), channel_id=1, source_target_pairs={{0,1},{1,0},{2,3},{3,2},{4,5},{5,4},{6,7},{7,6},{8,9},{9,8},{10,11... | collective-permute-start | bytes 62984 | tf_op jit(solution)/shard_map/ppermute | solution.py:134
  72.7 2.5 %collective-permute-start.23 = (f32[5248]{0:T(1024)S(1)}, f32[5248]{0:T(1024)S(1)}, u32[]{:S(2)}, u32[]{:S(2)}) collective-permute-start(f32[5248]{0:T(1024)S(1)} %add.65), channel_id=1, source_target_pairs={{0,1},{1,0},{2,3},{3,2},{4,5},{5,4},{6,7},{7,6},{8,9},{9,8},{10,11... | collective-permute-start | bytes 62984 | tf_op jit(solution)/shard_map/ppermute | solution.py:134
  75.4 1.8 %collective-permute-done.23 = f32[5248]{0:T(1024)S(1)} collective-permute-done((f32[5248]{0:T(1024)S(1)}, f32[5248]{0:T(1024)S(1)}, u32[]{:S(2)}, u32[]{:S(2)}) %collective-permute-start.23) | collective-permute-done | bytes 21024 | tf_op jit(solution)/shard_map/ppermute | solution.py:134
  78.8 3.0 %collective-permute-done.25 = f32[5248]{0:T(1024)S(1)} collective-permute-done((f32[5248]{0:T(1024)S(1)}, f32[5248]{0:T(1024)S(1)}, u32[]{:S(2)}, u32[]{:S(2)}) %collective-permute-start.25) | collective-permute-done | bytes 21024 | tf_op jit(solution)/shard_map/ppermute | solution.py:134
  81.8 2.9 %collective-permute-start.26 = (f32[5248]{0:T(1024)S(1)}, f32[5248]{0:T(1024)S(1)}, u32[]{:S(2)}, u32[]{:S(2)}) collective-permute-start(f32[5248]{0:T(1024)S(1)} %add.69), channel_id=1, source_target_pairs={{0,1},{1,0},{2,3},{3,2},{4,5},{5,4},{6,7},{7,6},{8,9},{9,8},{10,11... | collective-permute-start | bytes 62984 | tf_op jit(solution)/shard_map/ppermute | solution.py:134
  86.0 2.6 %collective-permute-done.27 = f32[5248]{0:T(1024)S(1)} collective-permute-done((f32[5248]{0:T(1024)S(1)}, f32[5248]{0:T(1024)S(1)}, u32[]{:S(2)}, u32[]{:S(2)}) %collective-permute-start.27) | collective-permute-done | bytes 21024 | tf_op jit(solution)/shard_map/ppermute | solution.py:134
  95.0 1.5 %shard_map.78 = (f32[64,2560]{1,0:T(8,128)}, f32[1,1]{1,0:T(1,128)}) custom-call(f32[64,2560]{1,0:T(8,128)S(1)} %rsqrt_multiply_fusion.scaled, f32[1,128]{1,0:T(1,128)S(1)} %get-tuple-element.63.row_sum, f32[1,128]{1,0:T(1,128)S(1)} %get-tuple-element.62.total), custom_call_target="tpu_custom_call" | custom-call | flops 1150000000 | tf_op jit(solution)/shard_map/pallas_call | solution.py:107
  (81 shorter events, 22.3 us)
Async XLA Ops:
  1.7 5.1 %collective-permute-start.1 = (f32[1,64,2560]{2,1,0:T(8,128)S(1)}, f32[1,64,2560]{2,1,0:T(8,128)S(1)}, u32[]{:S(2)}, u32[]{:S(2)}) collective-permute-start(f32[1,64,2560]{2,1,0:T(8,128)S(1)} %get-tuple-element.33), channel_id=1, source_target_pairs={{0,16},{16,0},{32,48},{48,32},{64,80},{80,64},{96,112},{112,96},{1... | collective-permute-start | bytes 1966088 | tf_op jit(solution)/shard_map/ppermute | solution.py:67
  6.4 4.5 %collective-permute-start = (f32[2,64,2560]{2,1,0:T(8,128)S(1)}, f32[2,64,2560]{2,1,0:T(8,128)S(1)}, u32[]{:S(2)}, u32[]{:S(2)}) collective-permute-start(f32[2,64,2560]{2,1,0:T(8,128)S(1)} %get-tuple-element.32), channel_id=1, source_target_pairs={{0,16},{16,0},{32,48},{48,32},{64,80},{80,64},{96,112},{112,96},{1... | collective-permute-start | bytes 3932168 | tf_op jit(solution)/shard_map/ppermute | solution.py:67
  6.9 11.7 %collective-permute-start.6 = (f32[32,2560]{1,0:T(8,128)S(1)}, f32[32,2560]{1,0:T(8,128)S(1)}, u32[]{:S(2)}, u32[]{:S(2)}) collective-permute-start(f32[32,2560]{1,0:T(8,128)S(1)} %get-tuple-element.34.refs_0_), channel_id=1, source_target_pairs={{0,32},{16,48},{32,64},{48,80},{64,96},{80,112},{96,128},{112,144}... | collective-permute-start | bytes 983048 | tf_op jit(solution)/shard_map/ppermute | solution.py:151
  6.9 11.6 %collective-permute-start.7 = (f32[32,2560]{1,0:T(8,128)S(1)}, f32[32,2560]{1,0:T(8,128)S(1)}, u32[]{:S(2)}, u32[]{:S(2)}) collective-permute-start(f32[32,2560]{1,0:T(8,128)S(1)} %get-tuple-element.41), channel_id=1, source_target_pairs={{0,224},{16,240},{32,0},{48,16},{64,32},{80,48},{96,64},{112,80},{... | collective-permute-start | bytes 983048 | tf_op jit(solution)/shard_map/ppermute | solution.py:154
  12.3 13.3 %collective-permute-start.4 = (f32[32,2560]{1,0:T(8,128)S(1)}, f32[32,2560]{1,0:T(8,128)S(1)}, u32[]{:S(2)}, u32[]{:S(2)}) collective-permute-start(f32[32,2560]{1,0:T(8,128)S(1)} %get-tuple-element.35.refs_0_), channel_id=1, source_target_pairs={{0,32},{16,48},{32,64},{48,80},{64,96},{80,112},{96,128},{112,144}... | collective-permute-start | bytes 983048 | tf_op jit(solution)/shard_map/ppermute | solution.py:151
  13.9 13.0 %collective-permute-start.3 = (f32[2,64,2560]{2,1,0:T(8,128)S(1)}, f32[2,64,2560]{2,1,0:T(8,128)S(1)}, u32[]{:S(2)}, u32[]{:S(2)}) collective-permute-start(f32[2,64,2560]{2,1,0:T(8,128)S(1)} %get-tuple-element.39), channel_id=1, source_target_pairs={{0,16},{16,0},{32,48},{48,32},{64,80},{80,64},{96,112},{112,96},{1... | collective-permute-start | bytes 3932168 | tf_op jit(solution)/shard_map/ppermute | solution.py:67
  14.6 12.3 %collective-permute-start.5 = (f32[32,2560]{1,0:T(8,128)S(1)}, f32[32,2560]{1,0:T(8,128)S(1)}, u32[]{:S(2)}, u32[]{:S(2)}) collective-permute-start(f32[32,2560]{1,0:T(8,128)S(1)} %get-tuple-element.40), channel_id=1, source_target_pairs={{0,224},{16,240},{32,0},{48,16},{64,32},{80,48},{96,64},{112,80},{... | collective-permute-start | bytes 983048 | tf_op jit(solution)/shard_map/ppermute | solution.py:154
  18.7 13.9 %collective-permute-start.10 = (f32[32,2560]{1,0:T(8,128)S(1)}, f32[32,2560]{1,0:T(8,128)S(1)}, u32[]{:S(2)}, u32[]{:S(2)}) collective-permute-start(f32[32,2560]{1,0:T(8,128)S(1)} %get-tuple-element.42.refs_2_), channel_id=1, source_target_pairs={{0,32},{16,48},{32,64},{48,80},{64,96},{80,112},{96,128},{112,144}... | collective-permute-start | bytes 983048 | tf_op jit(solution)/shard_map/ppermute | solution.py:151
  18.8 13.8 %collective-permute-start.11 = (f32[32,2560]{1,0:T(8,128)S(1)}, f32[32,2560]{1,0:T(8,128)S(1)}, u32[]{:S(2)}, u32[]{:S(2)}) collective-permute-start(f32[32,2560]{1,0:T(8,128)S(1)} %get-tuple-element.45), channel_id=1, source_target_pairs={{0,224},{16,240},{32,0},{48,16},{64,32},{80,48},{96,64},{112,80},{... | collective-permute-start | bytes 983048 | tf_op jit(solution)/shard_map/ppermute | solution.py:154
  25.6 14.1 %collective-permute-start.2 = (f32[3,64,2560]{2,1,0:T(8,128)S(1)}, f32[3,64,2560]{2,1,0:T(8,128)S(1)}, u32[]{:S(2)}, u32[]{:S(2)}) collective-permute-start(f32[3,64,2560]{2,1,0:T(8,128)S(1)} %get-tuple-element.38), channel_id=1, source_target_pairs={{0,16},{16,0},{32,48},{48,32},{64,80},{80,64},{96,112},{112,96},{1... | collective-permute-start | bytes 5898248 | tf_op jit(solution)/shard_map/ppermute | solution.py:67
  27.0 12.6 %collective-permute-start.8 = (f32[32,2560]{1,0:T(8,128)S(1)}, f32[32,2560]{1,0:T(8,128)S(1)}, u32[]{:S(2)}, u32[]{:S(2)}) collective-permute-start(f32[32,2560]{1,0:T(8,128)S(1)} %get-tuple-element.43.refs_2_), channel_id=1, source_target_pairs={{0,32},{16,48},{32,64},{48,80},{64,96},{80,112},{96,128},{112,144}... | collective-permute-start | bytes 983048 | tf_op jit(solution)/shard_map/ppermute | solution.py:151
  27.1 12.5 %collective-permute-start.9 = (f32[32,2560]{1,0:T(8,128)S(1)}, f32[32,2560]{1,0:T(8,128)S(1)}, u32[]{:S(2)}, u32[]{:S(2)}) collective-permute-start(f32[32,2560]{1,0:T(8,128)S(1)} %get-tuple-element.44), channel_id=1, source_target_pairs={{0,224},{16,240},{32,0},{48,16},{64,32},{80,48},{96,64},{112,80},{... | collective-permute-start | bytes 983048 | tf_op jit(solution)/shard_map/ppermute | solution.py:154
  32.7 13.9 %collective-permute-start.14 = (f32[32,2560]{1,0:T(8,128)S(1)}, f32[32,2560]{1,0:T(8,128)S(1)}, u32[]{:S(2)}, u32[]{:S(2)}) collective-permute-start(f32[32,2560]{1,0:T(8,128)S(1)} %get-tuple-element.46.refs_2_), channel_id=1, source_target_pairs={{0,32},{16,48},{32,64},{48,80},{64,96},{80,112},{96,128},{112,144}... | collective-permute-start | bytes 983048 | tf_op jit(solution)/shard_map/ppermute | solution.py:151
  32.8 13.9 %collective-permute-start.15 = (f32[32,2560]{1,0:T(8,128)S(1)}, f32[32,2560]{1,0:T(8,128)S(1)}, u32[]{:S(2)}, u32[]{:S(2)}) collective-permute-start(f32[32,2560]{1,0:T(8,128)S(1)} %get-tuple-element.49), channel_id=1, source_target_pairs={{0,224},{16,240},{32,0},{48,16},{64,32},{80,48},{96,64},{112,80},{... | collective-permute-start | bytes 983048 | tf_op jit(solution)/shard_map/ppermute | solution.py:154
  39.7 13.5 %collective-permute-start.12 = (f32[32,2560]{1,0:T(8,128)S(1)}, f32[32,2560]{1,0:T(8,128)S(1)}, u32[]{:S(2)}, u32[]{:S(2)}) collective-permute-start(f32[32,2560]{1,0:T(8,128)S(1)} %get-tuple-element.47), channel_id=1, source_target_pairs={{0,224},{16,240},{32,0},{48,16},{64,32},{80,48},{96,64},{112,80},{... | collective-permute-start | bytes 983048 | tf_op jit(solution)/shard_map/ppermute | solution.py:154
  42.8 10.5 %collective-permute-start.13 = (f32[32,2560]{1,0:T(8,128)S(1)}, f32[32,2560]{1,0:T(8,128)S(1)}, u32[]{:S(2)}, u32[]{:S(2)}) collective-permute-start(f32[32,2560]{1,0:T(8,128)S(1)} %get-tuple-element.48.refs_2_), channel_id=1, source_target_pairs={{0,32},{16,48},{32,64},{48,80},{64,96},{80,112},{96,128},{112,144}... | collective-permute-start | bytes 983048 | tf_op jit(solution)/shard_map/ppermute | solution.py:151
  46.7 13.1 %collective-permute-start.16 = (f32[32,2560]{1,0:T(8,128)S(1)}, f32[32,2560]{1,0:T(8,128)S(1)}, u32[]{:S(2)}, u32[]{:S(2)}) collective-permute-start(f32[32,2560]{1,0:T(8,128)S(1)} %get-tuple-element.50.refs_2_), channel_id=1, source_target_pairs={{0,32},{16,48},{32,64},{48,80},{64,96},{80,112},{96,128},{112,144}... | collective-permute-start | bytes 983048 | tf_op jit(solution)/shard_map/ppermute | solution.py:151
  46.8 13.4 %collective-permute-start.17 = (f32[32,2560]{1,0:T(8,128)S(1)}, f32[32,2560]{1,0:T(8,128)S(1)}, u32[]{:S(2)}, u32[]{:S(2)}) collective-permute-start(f32[32,2560]{1,0:T(8,128)S(1)} %get-tuple-element.53), channel_id=1, source_target_pairs={{0,224},{16,240},{32,0},{48,16},{64,32},{80,48},{96,64},{112,80},{... | collective-permute-start | bytes 983048 | tf_op jit(solution)/shard_map/ppermute | solution.py:154
  60.5 4.0 %collective-permute-start.18 = (f32[64]{0:T(128)S(1)}, f32[64]{0:T(128)S(1)}, u32[]{:S(2)}, u32[]{:S(2)}) collective-permute-start(f32[64]{0:T(128)S(1)} %add_reduce_fusion.1), channel_id=1, source_target_pairs={{0,2},{1,3},{2,0},{3,1},{4,6},{5,7},{6,4},{7,5},{8,10},{9,11},{10,... | collective-permute-start | bytes 776 | tf_op jit(solution)/shard_map/ppermute | solution.py:134
  70.9 4.5 %collective-permute-start.22 = (f32[5248]{0:T(1024)S(1)}, f32[5248]{0:T(1024)S(1)}, u32[]{:S(2)}, u32[]{:S(2)}) collective-permute-start(f32[5248]{0:T(1024)S(1)} %add.65), channel_id=1, source_target_pairs={{0,1},{1,0},{2,3},{3,2},{4,5},{5,4},{6,7},{7,6},{8,9},{9,8},{10,11... | collective-permute-start | bytes 62984 | tf_op jit(solution)/shard_map/ppermute | solution.py:134
  72.7 4.5 %collective-permute-start.23 = (f32[5248]{0:T(1024)S(1)}, f32[5248]{0:T(1024)S(1)}, u32[]{:S(2)}, u32[]{:S(2)}) collective-permute-start(f32[5248]{0:T(1024)S(1)} %add.65), channel_id=1, source_target_pairs={{0,1},{1,0},{2,3},{3,2},{4,5},{5,4},{6,7},{7,6},{8,9},{9,8},{10,11... | collective-permute-start | bytes 62984 | tf_op jit(solution)/shard_map/ppermute | solution.py:134
  77.8 4.0 %collective-permute-start.25 = (f32[5248]{0:T(1024)S(1)}, f32[5248]{0:T(1024)S(1)}, u32[]{:S(2)}, u32[]{:S(2)}) collective-permute-start(f32[5248]{0:T(1024)S(1)} %add_add_fusion.1), channel_id=1, source_target_pairs={{0,1},{1,0},{2,3},{3,2},{4,5},{5,4},{6,7},{7,6},{8,9},{9,8},{10,11... | collective-permute-start | bytes 62984 | tf_op jit(solution)/shard_map/ppermute | solution.py:134
  81.8 4.2 %collective-permute-start.26 = (f32[5248]{0:T(1024)S(1)}, f32[5248]{0:T(1024)S(1)}, u32[]{:S(2)}, u32[]{:S(2)}) collective-permute-start(f32[5248]{0:T(1024)S(1)} %add.69), channel_id=1, source_target_pairs={{0,1},{1,0},{2,3},{3,2},{4,5},{5,4},{6,7},{7,6},{8,9},{9,8},{10,11... | collective-permute-start | bytes 62984 | tf_op jit(solution)/shard_map/ppermute | solution.py:134
  88.7 4.0 %collective-permute-start.29 = (f32[128]{0:T(128)S(1)}, f32[128]{0:T(128)S(1)}, u32[]{:S(2)}, u32[]{:S(2)}) collective-permute-start(f32[128]{0:T(128)S(1)} %get-tuple-element.58), channel_id=1, source_target_pairs={{0,4},{1,5},{2,6},{3,7},{4,0},{5,1},{6,2},{7,3},{8,12},{9,13},{10,... | collective-permute-start | bytes 1544 | tf_op jit(solution)/shard_map/ppermute | solution.py:134
  (13 other events, 94.1 us)

commit v2 on v1

--- a/solution.py
+++ b/solution.py
@@ -15,8 +15,8 @@
 ORDER = (2, 3, 1)
 
 SWAP = [(i, i ^ 1) for i in range(16)]
-UP = [(i, (i + 2) % 16) for i in range(16)]
-DOWN = [(i, (i - 2) % 16) for i in range(16)]
+UP = [(2 * z + c, 2 * ((z + 1 - 2 * c) % 8) + c) for z in range(8) for c in range(2)]
+DOWN = [(j, i) for i, j in UP]
 
 VMEM = pl.BlockSpec(memory_space=pltpu.VMEM)
 HBM = pl.BlockSpec(memory_space=pltpu.HBM)
@@ -32,11 +32,14 @@
     own, sent, buf, own_sems, sems = refs[n_in:]
     me = lax.axis_index("dp")
     core = jnp.bitwise_and(me, 1)
+    z = lax.shift_right_logical(me, 1) + 8
     own_copies, copies = [], []
     for i, k in enumerate(ks):
-        dest = 2 * jnp.bitwise_and(lax.shift_right_logical(me, 1) + (k + 8), 7)
-        copies.append(pltpu.make_async_copy(parts.at[dest + 1 - core], buf.at[i], sems.at[i]))
-        own_copies.append(pltpu.make_async_copy(parts.at[dest + core], own.at[i], own_sems.at[i]))
+        step = k * (1 - 2 * core)
+        here = 2 * jnp.bitwise_and(z + step, 7) + core
+        there = 2 * jnp.bitwise_and(z - step, 7) + 1 - core
+        copies.append(pltpu.make_async_copy(parts.at[there], buf.at[i], sems.at[i]))
+        own_copies.append(pltpu.make_async_copy(parts.at[here], own.at[i], own_sems.at[i]))
     for copy in copies + own_copies:
         copy.start()
     for i, copy in enumerate(copies):

time: 97 us -> 96.1 us (level)
  starting transfers between devices: 46 us -> 40.2 us
  waiting for transfers between devices: 41.5 us -> 46.5 us
    ppermute x7, waiting for transfers between devices: 3.7 us -> 22.6 us  [down(): return lax.ppermute(x, 'dp', DOWN)]
    ppermute x7, starting transfers between devices: 21.4 us -> 4.33 us  [down(): return lax.ppermute(x, 'dp', DOWN)]
    ppermute x7, waiting for transfers between devices: 22 us -> 10.8 us  [up(): return lax.ppermute(x, 'dp', UP)]
    ppermute x7, starting transfers between devices: 0.51 us -> 11.7 us  [up(): return lax.ppermute(x, 'dp', UP)]
    ppermute x13, waiting for transfers between devices: 13.4 us -> 11.1 us  [exchange(): return lax.ppermute(v, ('dp', 'row', 'col'), pairs)]
    ppermute x4, starting transfers between devices: 5.55 us -> 3.96 us  [fetch(): return (own, lax.ppermute(sent, 'dp', SWAP))]
    ppermute x1, starting transfers between devices: 0.09 us -> 1.33 us  [on_device(): packed = jnp.where(core_one, packed, lax.ppermute(packed, 'dp', SWAP))]
  transfers between devices with their start and end apart: 33 -> 33, of which waited for: 20 -> 24; matrix products, arithmetic and copies ran while one was open for 0% -> 0% of each run, Pallas kernels for 5% -> 5%
where the time goes in v2:
time: 96.1 us; the launch traced here: 96 us
  waiting for transfers between devices  46.5 us (48%)
  starting transfers between devices  40.2 us (42%)
  Pallas kernels  7.51 us (8%)
  between operations  1.01 us (1%)
    ppermute x7, waiting for transfers between devices, down(): return lax.ppermute(x, 'dp', DOWN)  22.6 us
    ppermute x13, starting transfers between devices, exchange(): return lax.ppermute(v, ('dp', 'row', 'col'), pairs)  15.7 us
    ppermute x7, starting transfers between devices, up(): return lax.ppermute(x, 'dp', UP)  11.7 us
    ppermute x13, waiting for transfers between devices, exchange(): return lax.ppermute(v, ('dp', 'row', 'col'), pairs)  11.1 us
    ppermute x7, waiting for transfers between devices, up(): return lax.ppermute(x, 'dp', UP)  10.8 us
    pallas_call x4, Pallas kernels, fetch(): pl.pallas_call(functools.partial(fetch_kernel, ks, len(after)), out_shape...  5.24 us
    ppermute x7, starting transfers between devices, down(): return lax.ppermute(x, 'dp', DOWN)  4.33 us
    ppermute x4, starting transfers between devices, fetch(): return (own, lax.ppermute(sent, 'dp', SWAP))  3.96 us
  transfers between devices with their start and end apart: 33, of which 24 were waited for; matrix products, arithmetic and copies ran while one was open for 0% of the time, Pallas kernels for 5%

profile of v2, /device:TPU:1, one launch (start us, length us, event | category | flops | bytes accessed | tf_op | source)
XLA Modules:
  0.0 96.0 jit_solution(15660647283040024916)
XLA Ops:
  1.7 3.3 %collective-permute-start.1 = (f32[1,64,2560]{2,1,0:T(8,128)S(1)}, f32[1,64,2560]{2,1,0:T(8,128)S(1)}, u32[]{:S(2)}, u32[]{:S(2)}) collective-permute-start(f32[1,64,2560]{2,1,0:T(8,128)S(1)} %get-tuple-element.33), channel_id=1, source_target_pairs={{0,16},{16,0},{32,48},{48,32},{64,80},{80,64},{96,112},{112,96},{1... | collective-permute-start | bytes 1966088 | tf_op jit(solution)/shard_map/ppermute | solution.py:70
  6.9 3.9 %collective-permute-start.6 = (f32[32,2560]{1,0:T(8,128)S(1)}, f32[32,2560]{1,0:T(8,128)S(1)}, u32[]{:S(2)}, u32[]{:S(2)}) collective-permute-start(f32[32,2560]{1,0:T(8,128)S(1)} %get-tuple-element.34.refs_0_), channel_id=1, source_target_pairs={{0,32},{16,240},{32,64},{48,16},{64,96},{80,48},{96,128},{112,80},... | collective-permute-start | bytes 983048 | tf_op jit(solution)/shard_map/ppermute | solution.py:154
  12.2 2.7 %collective-permute-start.4 = (f32[32,2560]{1,0:T(8,128)S(1)}, f32[32,2560]{1,0:T(8,128)S(1)}, u32[]{:S(2)}, u32[]{:S(2)}) collective-permute-start(f32[32,2560]{1,0:T(8,128)S(1)} %get-tuple-element.35.refs_0_), channel_id=1, source_target_pairs={{0,32},{16,240},{32,64},{48,16},{64,96},{80,48},{96,128},{112,80},... | collective-permute-start | bytes 983048 | tf_op jit(solution)/shard_map/ppermute | solution.py:154
  14.9 1.5 %shard_map.71 = (bf16[3,64,2560]{2,1,0:T(8,128)(2,1)S(1)}, f32[3,64,2560]{2,1,0:T(8,128)S(1)}) custom-call(bf16[16,64,2560]{2,1,0:T(8,128)(2,1)} %bitcast.19, bf16[2,64,2560]{2,1,0:T(8,128)(2,1)S(1)} %get-tuple-element.36.refs_0_.own), custom_call_target="tpu_custom_call" | custom-call | tf_op jit(solution)/shard_map/pallas_call | solution.py:54
  17.4 4.4 %collective-permute-done.7.refs_1_ = f32[32,2560]{1,0:T(8,128)S(1)} collective-permute-done((f32[32,2560]{1,0:T(8,128)S(1)}, f32[32,2560]{1,0:T(8,128)S(1)}, u32[]{:S(2)}, u32[]{:S(2)}) %collective-permute-start.7) | collective-permute-done | bytes 327712 | tf_op jit(solution)/shard_map/ppermute | solution.py:157
  22.0 1.5 %collective-permute-start.11 = (f32[32,2560]{1,0:T(8,128)S(1)}, f32[32,2560]{1,0:T(8,128)S(1)}, u32[]{:S(2)}, u32[]{:S(2)}) collective-permute-start(f32[32,2560]{1,0:T(8,128)S(1)} %get-tuple-element.45), channel_id=1, source_target_pairs={{32,0},{240,16},{64,32},{16,48},{96,64},{48,80},{128,96},{80,112},... | collective-permute-start | bytes 983048 | tf_op jit(solution)/shard_map/ppermute | solution.py:157
  24.8 3.7 %collective-permute-done.5.refs_1_ = f32[32,2560]{1,0:T(8,128)S(1)} collective-permute-done((f32[32,2560]{1,0:T(8,128)S(1)}, f32[32,2560]{1,0:T(8,128)S(1)}, u32[]{:S(2)}, u32[]{:S(2)}) %collective-permute-start.5) | collective-permute-done | bytes 327712 | tf_op jit(solution)/shard_map/ppermute | solution.py:157
  31.4 4.1 %collective-permute-done.11.refs_1_ = f32[32,2560]{1,0:T(8,128)S(1)} collective-permute-done((f32[32,2560]{1,0:T(8,128)S(1)}, f32[32,2560]{1,0:T(8,128)S(1)}, u32[]{:S(2)}, u32[]{:S(2)}) %collective-permute-start.11) | collective-permute-done | bytes 327712 | tf_op jit(solution)/shard_map/ppermute | solution.py:157
  35.7 1.5 %collective-permute-start.15 = (f32[32,2560]{1,0:T(8,128)S(1)}, f32[32,2560]{1,0:T(8,128)S(1)}, u32[]{:S(2)}, u32[]{:S(2)}) collective-permute-start(f32[32,2560]{1,0:T(8,128)S(1)} %get-tuple-element.49), channel_id=1, source_target_pairs={{32,0},{240,16},{64,32},{16,48},{96,64},{48,80},{128,96},{80,112},... | collective-permute-start | bytes 983048 | tf_op jit(solution)/shard_map/ppermute | solution.py:157
  38.5 4.1 %collective-permute-done.9.refs_1_ = f32[32,2560]{1,0:T(8,128)S(1)} collective-permute-done((f32[32,2560]{1,0:T(8,128)S(1)}, f32[32,2560]{1,0:T(8,128)S(1)}, u32[]{:S(2)}, u32[]{:S(2)}) %collective-permute-start.9) | collective-permute-done | bytes 327712 | tf_op jit(solution)/shard_map/ppermute | solution.py:157
  42.8 2.7 %collective-permute-start.13 = (f32[32,2560]{1,0:T(8,128)S(1)}, f32[32,2560]{1,0:T(8,128)S(1)}, u32[]{:S(2)}, u32[]{:S(2)}) collective-permute-start(f32[32,2560]{1,0:T(8,128)S(1)} %get-tuple-element.48.refs_2_), channel_id=1, source_target_pairs={{0,32},{16,240},{32,64},{48,16},{64,96},{80,48},{96,128},{112,80},... | collective-permute-start | bytes 983048 | tf_op jit(solution)/shard_map/ppermute | solution.py:154
  45.5 1.9 %collective-permute-done.15.refs_1_ = f32[32,2560]{1,0:T(8,128)S(1)} collective-permute-done((f32[32,2560]{1,0:T(8,128)S(1)}, f32[32,2560]{1,0:T(8,128)S(1)}, u32[]{:S(2)}, u32[]{:S(2)}) %collective-permute-start.15) | collective-permute-done | bytes 327712 | tf_op jit(solution)/shard_map/ppermute | solution.py:157
  47.5 1.9 %collective-permute-start.16 = (f32[32,2560]{1,0:T(8,128)S(1)}, f32[32,2560]{1,0:T(8,128)S(1)}, u32[]{:S(2)}, u32[]{:S(2)}) collective-permute-start(f32[32,2560]{1,0:T(8,128)S(1)} %get-tuple-element.50.refs_2_), channel_id=1, source_target_pairs={{0,32},{16,240},{32,64},{48,16},{64,96},{80,48},{96,128},{112,80},... | collective-permute-start | bytes 983048 | tf_op jit(solution)/shard_map/ppermute | solution.py:154
  49.4 4.0 %collective-permute-done.12.refs_0_ = f32[32,2560]{1,0:T(8,128)S(1)} collective-permute-done((f32[32,2560]{1,0:T(8,128)S(1)}, f32[32,2560]{1,0:T(8,128)S(1)}, u32[]{:S(2)}, u32[]{:S(2)}) %collective-permute-start.12) | collective-permute-done | bytes 327712 | tf_op jit(solution)/shard_map/ppermute | solution.py:157
  53.5 6.6 %collective-permute-done.16 = f32[32,2560]{1,0:T(8,128)S(1)} collective-permute-done((f32[32,2560]{1,0:T(8,128)S(1)}, f32[32,2560]{1,0:T(8,128)S(1)}, u32[]{:S(2)}, u32[]{:S(2)}) %collective-permute-start.16) | collective-permute-done | bytes 327712 | tf_op jit(solution)/shard_map/ppermute | solution.py:154
  60.6 2.8 %collective-permute-start.18 = (f32[64]{0:T(128)S(1)}, f32[64]{0:T(128)S(1)}, u32[]{:S(2)}, u32[]{:S(2)}) collective-permute-start(f32[64]{0:T(128)S(1)} %add_reduce_fusion.1), channel_id=1, source_target_pairs={{0,2},{1,3},{2,0},{3,1},{4,6},{5,7},{6,4},{7,5},{8,10},{9,11},{10,... | collective-permute-start | bytes 776 | tf_op jit(solution)/shard_map/ppermute | solution.py:137
  64.6 2.5 %collective-permute-done.19 = f32[64]{0:T(128)S(1)} collective-permute-done((f32[64]{0:T(128)S(1)}, f32[64]{0:T(128)S(1)}, u32[]{:S(2)}, u32[]{:S(2)}) %collective-permute-start.19) | collective-permute-done | bytes 288 | tf_op jit(solution)/shard_map/ppermute | solution.py:137
  67.3 3.2 %collective-permute-start.21 = (f32[5248]{0:T(1024)S(1)}, f32[5248]{0:T(1024)S(1)}, u32[]{:S(2)}, u32[]{:S(2)}) collective-permute-start(f32[5248]{0:T(1024)S(1)} %concatenate.10), channel_id=1, source_target_pairs={{0,16},{16,0},{32,48},{48,32},{64,80},{80,64},{96,112},{112,96},{1... | collective-permute-start | bytes 62984 | tf_op jit(solution)/shard_map/ppermute | solution.py:194
  71.4 1.4 %collective-permute-start.23 = (f32[5248]{0:T(1024)S(1)}, f32[5248]{0:T(1024)S(1)}, u32[]{:S(2)}, u32[]{:S(2)}) collective-permute-start(f32[5248]{0:T(1024)S(1)} %add.65), channel_id=1, source_target_pairs={{0,1},{1,0},{2,3},{3,2},{4,5},{5,4},{6,7},{7,6},{8,9},{9,8},{10,11... | collective-permute-start | bytes 62984 | tf_op jit(solution)/shard_map/ppermute | solution.py:137
  76.0 2.9 %collective-permute-start.25 = (f32[5248]{0:T(1024)S(1)}, f32[5248]{0:T(1024)S(1)}, u32[]{:S(2)}, u32[]{:S(2)}) collective-permute-start(f32[5248]{0:T(1024)S(1)} %add_add_fusion.1), channel_id=1, source_target_pairs={{0,1},{1,0},{2,3},{3,2},{4,5},{5,4},{6,7},{7,6},{8,9},{9,8},{10,11... | collective-permute-start | bytes 62984 | tf_op jit(solution)/shard_map/ppermute | solution.py:137
  80.1 2.9 %collective-permute-start.26 = (f32[5248]{0:T(1024)S(1)}, f32[5248]{0:T(1024)S(1)}, u32[]{:S(2)}, u32[]{:S(2)}) collective-permute-start(f32[5248]{0:T(1024)S(1)} %add.69), channel_id=1, source_target_pairs={{0,1},{1,0},{2,3},{3,2},{4,5},{5,4},{6,7},{7,6},{8,9},{9,8},{10,11... | collective-permute-start | bytes 62984 | tf_op jit(solution)/shard_map/ppermute | solution.py:137
  84.3 2.6 %collective-permute-done.27 = f32[5248]{0:T(1024)S(1)} collective-permute-done((f32[5248]{0:T(1024)S(1)}, f32[5248]{0:T(1024)S(1)}, u32[]{:S(2)}, u32[]{:S(2)}) %collective-permute-start.27) | collective-permute-done | bytes 21024 | tf_op jit(solution)/shard_map/ppermute | solution.py:137
  91.9 1.3 %collective-permute-start.32 = (f32[2816]{0:T(1024)S(1)}, f32[2816]{0:T(1024)S(1)}, u32[]{:S(2)}, u32[]{:S(2)}) collective-permute-start(f32[2816]{0:T(1024)S(1)} %pad_maximum_fusion.1), channel_id=1, source_target_pairs={{0,16},{16,0},{32,48},{48,32},{64,80},{80,64},{96,112},{112,96},{1... | collective-permute-start | bytes 33800 | tf_op jit(solution)/shard_map/ppermute | solution.py:204
  94.2 1.5 %shard_map.78 = (f32[64,2560]{1,0:T(8,128)}, f32[1,1]{1,0:T(1,128)}) custom-call(f32[64,2560]{1,0:T(8,128)S(1)} %rsqrt_multiply_fusion.scaled, f32[1,128]{1,0:T(1,128)S(1)} %get-tuple-element.63.row_sum, f32[1,128]{1,0:T(1,128)S(1)} %get-tuple-element.62.total), custom_call_target="tpu_custom_call" | custom-call | flops 1150000000 | tf_op jit(solution)/shard_map/pallas_call | solution.py:110
  (81 shorter events, 26.0 us)
Async XLA Ops:
  1.7 5.1 %collective-permute-start.1 = (f32[1,64,2560]{2,1,0:T(8,128)S(1)}, f32[1,64,2560]{2,1,0:T(8,128)S(1)}, u32[]{:S(2)}, u32[]{:S(2)}) collective-permute-start(f32[1,64,2560]{2,1,0:T(8,128)S(1)} %get-tuple-element.33), channel_id=1, source_target_pairs={{0,16},{16,0},{32,48},{48,32},{64,80},{80,64},{96,112},{112,96},{1... | collective-permute-start | bytes 1966088 | tf_op jit(solution)/shard_map/ppermute | solution.py:70
  6.4 4.4 %collective-permute-start = (f32[2,64,2560]{2,1,0:T(8,128)S(1)}, f32[2,64,2560]{2,1,0:T(8,128)S(1)}, u32[]{:S(2)}, u32[]{:S(2)}) collective-permute-start(f32[2,64,2560]{2,1,0:T(8,128)S(1)} %get-tuple-element.32), channel_id=1, source_target_pairs={{0,16},{16,0},{32,48},{48,32},{64,80},{80,64},{96,112},{112,96},{1... | collective-permute-start | bytes 3932168 | tf_op jit(solution)/shard_map/ppermute | solution.py:70
  6.9 10.5 %collective-permute-start.6 = (f32[32,2560]{1,0:T(8,128)S(1)}, f32[32,2560]{1,0:T(8,128)S(1)}, u32[]{:S(2)}, u32[]{:S(2)}) collective-permute-start(f32[32,2560]{1,0:T(8,128)S(1)} %get-tuple-element.34.refs_0_), channel_id=1, source_target_pairs={{0,32},{16,240},{32,64},{48,16},{64,96},{80,48},{96,128},{112,80},... | collective-permute-start | bytes 983048 | tf_op jit(solution)/shard_map/ppermute | solution.py:154
  10.8 11.0 %collective-permute-start.7 = (f32[32,2560]{1,0:T(8,128)S(1)}, f32[32,2560]{1,0:T(8,128)S(1)}, u32[]{:S(2)}, u32[]{:S(2)}) collective-permute-start(f32[32,2560]{1,0:T(8,128)S(1)} %get-tuple-element.41), channel_id=1, source_target_pairs={{32,0},{240,16},{64,32},{16,48},{96,64},{48,80},{128,96},{80,112},... | collective-permute-start | bytes 983048 | tf_op jit(solution)/shard_map/ppermute | solution.py:157
  12.2 12.2 %collective-permute-start.4 = (f32[32,2560]{1,0:T(8,128)S(1)}, f32[32,2560]{1,0:T(8,128)S(1)}, u32[]{:S(2)}, u32[]{:S(2)}) collective-permute-start(f32[32,2560]{1,0:T(8,128)S(1)} %get-tuple-element.35.refs_0_), channel_id=1, source_target_pairs={{0,32},{16,240},{32,64},{48,16},{64,96},{80,48},{96,128},{112,80},... | collective-permute-start | bytes 983048 | tf_op jit(solution)/shard_map/ppermute | solution.py:154
  16.5 12.1 %collective-permute-start.3 = (f32[2,64,2560]{2,1,0:T(8,128)S(1)}, f32[2,64,2560]{2,1,0:T(8,128)S(1)}, u32[]{:S(2)}, u32[]{:S(2)}) collective-permute-start(f32[2,64,2560]{2,1,0:T(8,128)S(1)} %get-tuple-element.39), channel_id=1, source_target_pairs={{0,16},{16,0},{32,48},{48,32},{64,80},{80,64},{96,112},{112,96},{1... | collective-permute-start | bytes 3932168 | tf_op jit(solution)/shard_map/ppermute | solution.py:70
  16.6 12.0 %collective-permute-start.5 = (f32[32,2560]{1,0:T(8,128)S(1)}, f32[32,2560]{1,0:T(8,128)S(1)}, u32[]{:S(2)}, u32[]{:S(2)}) collective-permute-start(f32[32,2560]{1,0:T(8,128)S(1)} %get-tuple-element.40), channel_id=1, source_target_pairs={{32,0},{240,16},{64,32},{16,48},{96,64},{48,80},{128,96},{80,112},... | collective-permute-start | bytes 983048 | tf_op jit(solution)/shard_map/ppermute | solution.py:157
  21.9 9.6 %collective-permute-start.10 = (f32[32,2560]{1,0:T(8,128)S(1)}, f32[32,2560]{1,0:T(8,128)S(1)}, u32[]{:S(2)}, u32[]{:S(2)}) collective-permute-start(f32[32,2560]{1,0:T(8,128)S(1)} %get-tuple-element.42.refs_2_), channel_id=1, source_target_pairs={{0,32},{16,240},{32,64},{48,16},{64,96},{80,48},{96,128},{112,80},... | collective-permute-start | bytes 983048 | tf_op jit(solution)/shard_map/ppermute | solution.py:154
  22.0 13.6 %collective-permute-start.11 = (f32[32,2560]{1,0:T(8,128)S(1)}, f32[32,2560]{1,0:T(8,128)S(1)}, u32[]{:S(2)}, u32[]{:S(2)}) collective-permute-start(f32[32,2560]{1,0:T(8,128)S(1)} %get-tuple-element.45), channel_id=1, source_target_pairs={{32,0},{240,16},{64,32},{16,48},{96,64},{48,80},{128,96},{80,112},... | collective-permute-start | bytes 983048 | tf_op jit(solution)/shard_map/ppermute | solution.py:157
  24.4 18.2 %collective-permute-start.2 = (f32[3,64,2560]{2,1,0:T(8,128)S(1)}, f32[3,64,2560]{2,1,0:T(8,128)S(1)}, u32[]{:S(2)}, u32[]{:S(2)}) collective-permute-start(f32[3,64,2560]{2,1,0:T(8,128)S(1)} %get-tuple-element.38), channel_id=1, source_target_pairs={{0,16},{16,0},{32,48},{48,32},{64,80},{80,64},{96,112},{112,96},{1... | collective-permute-start | bytes 5898248 | tf_op jit(solution)/shard_map/ppermute | solution.py:70
  28.6 9.8 %collective-permute-start.8 = (f32[32,2560]{1,0:T(8,128)S(1)}, f32[32,2560]{1,0:T(8,128)S(1)}, u32[]{:S(2)}, u32[]{:S(2)}) collective-permute-start(f32[32,2560]{1,0:T(8,128)S(1)} %get-tuple-element.43.refs_2_), channel_id=1, source_target_pairs={{0,32},{16,240},{32,64},{48,16},{64,96},{80,48},{96,128},{112,80},... | collective-permute-start | bytes 983048 | tf_op jit(solution)/shard_map/ppermute | solution.py:154
  28.9 13.7 %collective-permute-start.9 = (f32[32,2560]{1,0:T(8,128)S(1)}, f32[32,2560]{1,0:T(8,128)S(1)}, u32[]{:S(2)}, u32[]{:S(2)}) collective-permute-start(f32[32,2560]{1,0:T(8,128)S(1)} %get-tuple-element.44), channel_id=1, source_target_pairs={{32,0},{240,16},{64,32},{16,48},{96,64},{48,80},{128,96},{80,112},... | collective-permute-start | bytes 983048 | tf_op jit(solution)/shard_map/ppermute | solution.py:157
  35.7 9.8 %collective-permute-start.14 = (f32[32,2560]{1,0:T(8,128)S(1)}, f32[32,2560]{1,0:T(8,128)S(1)}, u32[]{:S(2)}, u32[]{:S(2)}) collective-permute-start(f32[32,2560]{1,0:T(8,128)S(1)} %get-tuple-element.46.refs_2_), channel_id=1, source_target_pairs={{0,32},{16,240},{32,64},{48,16},{64,96},{80,48},{96,128},{112,80},... | collective-permute-start | bytes 983048 | tf_op jit(solution)/shard_map/ppermute | solution.py:154
  35.7 11.6 %collective-permute-start.15 = (f32[32,2560]{1,0:T(8,128)S(1)}, f32[32,2560]{1,0:T(8,128)S(1)}, u32[]{:S(2)}, u32[]{:S(2)}) collective-permute-start(f32[32,2560]{1,0:T(8,128)S(1)} %get-tuple-element.49), channel_id=1, source_target_pairs={{32,0},{240,16},{64,32},{16,48},{96,64},{48,80},{128,96},{80,112},... | collective-permute-start | bytes 983048 | tf_op jit(solution)/shard_map/ppermute | solution.py:157
  42.7 10.7 %collective-permute-start.12 = (f32[32,2560]{1,0:T(8,128)S(1)}, f32[32,2560]{1,0:T(8,128)S(1)}, u32[]{:S(2)}, u32[]{:S(2)}) collective-permute-start(f32[32,2560]{1,0:T(8,128)S(1)} %get-tuple-element.47), channel_id=1, source_target_pairs={{32,0},{240,16},{64,32},{16,48},{96,64},{48,80},{128,96},{80,112},... | collective-permute-start | bytes 983048 | tf_op jit(solution)/shard_map/ppermute | solution.py:157
  42.8 10.6 %collective-permute-start.13 = (f32[32,2560]{1,0:T(8,128)S(1)}, f32[32,2560]{1,0:T(8,128)S(1)}, u32[]{:S(2)}, u32[]{:S(2)}) collective-permute-start(f32[32,2560]{1,0:T(8,128)S(1)} %get-tuple-element.48.refs_2_), channel_id=1, source_target_pairs={{0,32},{16,240},{32,64},{48,16},{64,96},{80,48},{96,128},{112,80},... | collective-permute-start | bytes 983048 | tf_op jit(solution)/shard_map/ppermute | solution.py:154
  47.5 12.6 %collective-permute-start.16 = (f32[32,2560]{1,0:T(8,128)S(1)}, f32[32,2560]{1,0:T(8,128)S(1)}, u32[]{:S(2)}, u32[]{:S(2)}) collective-permute-start(f32[32,2560]{1,0:T(8,128)S(1)} %get-tuple-element.50.refs_2_), channel_id=1, source_target_pairs={{0,32},{16,240},{32,64},{48,16},{64,96},{80,48},{96,128},{112,80},... | collective-permute-start | bytes 983048 | tf_op jit(solution)/shard_map/ppermute | solution.py:154
  49.4 11.0 %collective-permute-start.17 = (f32[32,2560]{1,0:T(8,128)S(1)}, f32[32,2560]{1,0:T(8,128)S(1)}, u32[]{:S(2)}, u32[]{:S(2)}) collective-permute-start(f32[32,2560]{1,0:T(8,128)S(1)} %get-tuple-element.53), channel_id=1, source_target_pairs={{32,0},{240,16},{64,32},{16,48},{96,64},{48,80},{128,96},{80,112},... | collective-permute-start | bytes 983048 | tf_op jit(solution)/shard_map/ppermute | solution.py:157
  60.6 4.0 %collective-permute-start.18 = (f32[64]{0:T(128)S(1)}, f32[64]{0:T(128)S(1)}, u32[]{:S(2)}, u32[]{:S(2)}) collective-permute-start(f32[64]{0:T(128)S(1)} %add_reduce_fusion.1), channel_id=1, source_target_pairs={{0,2},{1,3},{2,0},{3,1},{4,6},{5,7},{6,4},{7,5},{8,10},{9,11},{10,... | collective-permute-start | bytes 776 | tf_op jit(solution)/shard_map/ppermute | solution.py:137
  67.3 4.1 %collective-permute-start.21 = (f32[5248]{0:T(1024)S(1)}, f32[5248]{0:T(1024)S(1)}, u32[]{:S(2)}, u32[]{:S(2)}) collective-permute-start(f32[5248]{0:T(1024)S(1)} %concatenate.10), channel_id=1, source_target_pairs={{0,16},{16,0},{32,48},{48,32},{64,80},{80,64},{96,112},{112,96},{1... | collective-permute-start | bytes 62984 | tf_op jit(solution)/shard_map/ppermute | solution.py:194
  71.4 4.6 %collective-permute-start.23 = (f32[5248]{0:T(1024)S(1)}, f32[5248]{0:T(1024)S(1)}, u32[]{:S(2)}, u32[]{:S(2)}) collective-permute-start(f32[5248]{0:T(1024)S(1)} %add.65), channel_id=1, source_target_pairs={{0,1},{1,0},{2,3},{3,2},{4,5},{5,4},{6,7},{7,6},{8,9},{9,8},{10,11... | collective-permute-start | bytes 62984 | tf_op jit(solution)/shard_map/ppermute | solution.py:137
  76.0 4.1 %collective-permute-start.25 = (f32[5248]{0:T(1024)S(1)}, f32[5248]{0:T(1024)S(1)}, u32[]{:S(2)}, u32[]{:S(2)}) collective-permute-start(f32[5248]{0:T(1024)S(1)} %add_add_fusion.1), channel_id=1, source_target_pairs={{0,1},{1,0},{2,3},{3,2},{4,5},{5,4},{6,7},{7,6},{8,9},{9,8},{10,11... | collective-permute-start | bytes 62984 | tf_op jit(solution)/shard_map/ppermute | solution.py:137
  80.1 4.2 %collective-permute-start.26 = (f32[5248]{0:T(1024)S(1)}, f32[5248]{0:T(1024)S(1)}, u32[]{:S(2)}, u32[]{:S(2)}) collective-permute-start(f32[5248]{0:T(1024)S(1)} %add.69), channel_id=1, source_target_pairs={{0,1},{1,0},{2,3},{3,2},{4,5},{5,4},{6,7},{7,6},{8,9},{9,8},{10,11... | collective-permute-start | bytes 62984 | tf_op jit(solution)/shard_map/ppermute | solution.py:137
  87.0 4.0 %collective-permute-start.29 = (f32[128]{0:T(128)S(1)}, f32[128]{0:T(128)S(1)}, u32[]{:S(2)}, u32[]{:S(2)}) collective-permute-start(f32[128]{0:T(128)S(1)} %get-tuple-element.58), channel_id=1, source_target_pairs={{0,4},{1,5},{2,6},{3,7},{4,0},{5,1},{6,2},{7,3},{8,12},{9,13},{10,... | collective-permute-start | bytes 1544 | tf_op jit(solution)/shard_map/ppermute | solution.py:137
  (13 other events, 92.6 us)

commit v3 on v2

--- a/solution.py
+++ b/solution.py
@@ -183,15 +183,22 @@
     upper, lower = add(near, ((2, 0), (2, 1)), (d, c), after=(after,))
     grad = jnp.concatenate([upper + a, lower + b], axis=0)
 
-    square = grad * grad
-    row_part = jnp.sum(square + 1e-30, axis=1)
-    col_part = jnp.sum(square + 1e-30, axis=0)
-    row_total = sum_four(row_part, 2)
-    row_new = 0.8 * row_old[0] + 0.2 * row_total / FF
-    weighted = jnp.sum(square * (1.0 / row_new)[:, None], axis=0)
-    packed = jnp.concatenate([col_part, weighted, row_new, jnp.zeros((64,), jnp.float32)])
-
-    packed = packed + lax.ppermute(packed, "dp", SWAP)
+    grad = lax.optimization_barrier(grad)
+    row_own = jnp.concatenate([jnp.sum(grad * grad + 1e-30, axis=1), row_old[0]])
+    row_other = lax.ppermute(row_own, "dp", SWAP)
+    grad_other, row_other = lax.optimization_barrier((grad, row_other))
+    grad_other = lax.ppermute(grad_other, "dp", SWAP)
+    row_total = sum_four(jnp.concatenate([row_own[:ROWS], row_other[:ROWS]]), 2, (0, 1, 0))
+    row_new = 0.8 * jnp.concatenate([row_own[ROWS:], row_other[ROWS:]]) + 0.2 * row_total / FF
+    packed = []
+    for weight in (None, 1.0 / row_new):
+        sums = 0.0
+        for g, rows in ((grad, slice(0, ROWS)), (grad_other, slice(ROWS, 2 * ROWS))):
+            term = g * g + 1e-30 if weight is None else g * g * weight[rows, None]
+            sums = sums + jnp.sum(term, axis=0)
+        packed.append(sums)
+    packed = jnp.concatenate([*packed, row_new])
+
     packed = sum_four(packed, 0, (0, 0, 1))
     packed = packed + exchange(packed, (7, 0, 0), (0, 0, 1))
     packed = sum_four(packed, 1, (0, 0, 1))
@@ -200,9 +207,11 @@
     total = sum_four(total, 2, (0, 1, 0))
     core_one = jnp.bitwise_and(lax.axis_index("dp"), 1) == 1
 
-    packed = jnp.concatenate([col_new, packed[2 * COLS:], total])
-    packed = jnp.where(core_one, packed, lax.ppermute(packed, "dp", SWAP))
-    col_new, row_sum, total = packed[:COLS], packed[COLS:COLS + 128], packed[COLS + 128:]
+    packed = jnp.concatenate([col_new, packed[2 * COLS:], total, row_new])
+    other = lax.ppermute(packed, "dp", SWAP)
+    row_new = jnp.where(core_one, packed[-2 * ROWS:-ROWS], other[-ROWS:])
+    packed = jnp.where(core_one, packed, other)
+    col_new, row_sum, total = packed[:COLS], packed[COLS:COLS + 128], packed[COLS + 128:COLS + 256]
     scaled = grad * lax.rsqrt(row_new[:, None] * col_new[None, :])
     update, update_rms = final(scaled, row_sum.reshape(1, 128), total.reshape(1, 128))
     return (update[None], row_new[None], col_new, update_rms.reshape(()))

time: 96.1 us -> 95.1 us (0.990)
  starting transfers between devices: 40.2 us -> 38.1 us
    ppermute x2 -> x3, starting transfers between devices: 4.55 us -> 2.44 us  [the longest x1 1.77 us: on_device(): row_other = lax.ppermute(row_own, 'dp', SWAP)]
  transfers between devices with their start and end apart: 33 -> 34, of which waited for: 24 -> 24; matrix products, arithmetic and copies ran while one was open for 0% -> 1% of each run, Pallas kernels for 5% -> 5%
where the time goes in v3:
time: 95.1 us; the launch traced here: 94.9 us
  waiting for transfers between devices  46.6 us (49%)
  starting transfers between devices  38.1 us (40%)
  Pallas kernels  7.51 us (8%)
  other arithmetic  1.13 us (1%)
  between operations  1.06 us (1%)
    ppermute x7, waiting for transfers between devices, down(): return lax.ppermute(x, 'dp', DOWN)  22.6 us
    ppermute x13, starting transfers between devices, exchange(): return lax.ppermute(v, ('dp', 'row', 'col'), pairs)  15.7 us
    ppermute x7, starting transfers between devices, up(): return lax.ppermute(x, 'dp', UP)  11.7 us
    ppermute x13, waiting for transfers between devices, exchange(): return lax.ppermute(v, ('dp', 'row', 'col'), pairs)  11.2 us
    ppermute x7, waiting for transfers between devices, up(): return lax.ppermute(x, 'dp', UP)  10.8 us
    pallas_call x4, Pallas kernels, fetch(): pl.pallas_call(functools.partial(fetch_kernel, ks, len(after)), out_shape...  5.24 us
    ppermute x7, starting transfers between devices, down(): return lax.ppermute(x, 'dp', DOWN)  4.33 us
    ppermute x4, starting transfers between devices, fetch(): return (own, lax.ppermute(sent, 'dp', SWAP))  3.96 us
  transfers between devices with their start and end apart: 34, of which 24 were waited for; matrix products, arithmetic and copies ran while one was open for 1% of the time, Pallas kernels for 5%

profile of v3, /device:TPU:1, one launch (start us, length us, event | category | flops | bytes accessed | tf_op | source)
XLA Modules:
  0.0 94.9 jit_solution(787048272466332635)
XLA Ops:
  1.7 3.3 %collective-permute-start.1 = (f32[1,64,2560]{2,1,0:T(8,128)S(1)}, f32[1,64,2560]{2,1,0:T(8,128)S(1)}, u32[]{:S(2)}, u32[]{:S(2)}) collective-permute-start(f32[1,64,2560]{2,1,0:T(8,128)S(1)} %get-tuple-element.35), channel_id=1, source_target_pairs={{0,16},{16,0},{32,48},{48,32},{64,80},{80,64},{96,112},{112,96},{1... | collective-permute-start | bytes 1966088 | tf_op jit(solution)/shard_map/ppermute | solution.py:70
  6.9 3.9 %collective-permute-start.6 = (f32[32,2560]{1,0:T(8,128)S(1)}, f32[32,2560]{1,0:T(8,128)S(1)}, u32[]{:S(2)}, u32[]{:S(2)}) collective-permute-start(f32[32,2560]{1,0:T(8,128)S(1)} %get-tuple-element.36.refs_0_), channel_id=1, source_target_pairs={{0,32},{16,240},{32,64},{48,16},{64,96},{80,48},{96,128},{112,80},... | collective-permute-start | bytes 983048 | tf_op jit(solution)/shard_map/ppermute | solution.py:154
  10.9 1.3 %shard_map.70 = (bf16[2,64,2560]{2,1,0:T(8,128)(2,1)S(1)}, f32[2,64,2560]{2,1,0:T(8,128)S(1)}) custom-call(bf16[16,64,2560]{2,1,0:T(8,128)(2,1)} %bitcast.16, f32[32,2560]{1,0:T(8,128)S(1)} %get-tuple-element.37.refs_0_), custom_call_target="tpu_custom_call" | custom-call | tf_op jit(solution)/shard_map/pallas_call | solution.py:54
  12.2 2.7 %collective-permute-start.4 = (f32[32,2560]{1,0:T(8,128)S(1)}, f32[32,2560]{1,0:T(8,128)S(1)}, u32[]{:S(2)}, u32[]{:S(2)}) collective-permute-start(f32[32,2560]{1,0:T(8,128)S(1)} %get-tuple-element.37.refs_0_), channel_id=1, source_target_pairs={{0,32},{16,240},{32,64},{48,16},{64,96},{80,48},{96,128},{112,80},... | collective-permute-start | bytes 983048 | tf_op jit(solution)/shard_map/ppermute | solution.py:154
  14.9 1.5 %shard_map.71 = (bf16[3,64,2560]{2,1,0:T(8,128)(2,1)S(1)}, f32[3,64,2560]{2,1,0:T(8,128)S(1)}) custom-call(bf16[16,64,2560]{2,1,0:T(8,128)(2,1)} %bitcast.17, bf16[2,64,2560]{2,1,0:T(8,128)(2,1)S(1)} %get-tuple-element.38.refs_0_.own), custom_call_target="tpu_custom_call" | custom-call | tf_op jit(solution)/shard_map/pallas_call | solution.py:54
  17.4 4.4 %collective-permute-done.7.refs_1_ = f32[32,2560]{1,0:T(8,128)S(1)} collective-permute-done((f32[32,2560]{1,0:T(8,128)S(1)}, f32[32,2560]{1,0:T(8,128)S(1)}, u32[]{:S(2)}, u32[]{:S(2)}) %collective-permute-start.7) | collective-permute-done | bytes 327712 | tf_op jit(solution)/shard_map/ppermute | solution.py:157
  22.0 1.5 %collective-permute-start.11 = (f32[32,2560]{1,0:T(8,128)S(1)}, f32[32,2560]{1,0:T(8,128)S(1)}, u32[]{:S(2)}, u32[]{:S(2)}) collective-permute-start(f32[32,2560]{1,0:T(8,128)S(1)} %get-tuple-element.47), channel_id=1, source_target_pairs={{32,0},{240,16},{64,32},{16,48},{96,64},{48,80},{128,96},{80,112},... | collective-permute-start | bytes 983048 | tf_op jit(solution)/shard_map/ppermute | solution.py:157
  24.8 3.7 %collective-permute-done.5.refs_1_ = f32[32,2560]{1,0:T(8,128)S(1)} collective-permute-done((f32[32,2560]{1,0:T(8,128)S(1)}, f32[32,2560]{1,0:T(8,128)S(1)}, u32[]{:S(2)}, u32[]{:S(2)}) %collective-permute-start.5) | collective-permute-done | bytes 327712 | tf_op jit(solution)/shard_map/ppermute | solution.py:157
  31.4 4.1 %collective-permute-done.11.refs_1_ = f32[32,2560]{1,0:T(8,128)S(1)} collective-permute-done((f32[32,2560]{1,0:T(8,128)S(1)}, f32[32,2560]{1,0:T(8,128)S(1)}, u32[]{:S(2)}, u32[]{:S(2)}) %collective-permute-start.11) | collective-permute-done | bytes 327712 | tf_op jit(solution)/shard_map/ppermute | solution.py:157
  35.7 1.5 %collective-permute-start.15 = (f32[32,2560]{1,0:T(8,128)S(1)}, f32[32,2560]{1,0:T(8,128)S(1)}, u32[]{:S(2)}, u32[]{:S(2)}) collective-permute-start(f32[32,2560]{1,0:T(8,128)S(1)} %get-tuple-element.51), channel_id=1, source_target_pairs={{32,0},{240,16},{64,32},{16,48},{96,64},{48,80},{128,96},{80,112},... | collective-permute-start | bytes 983048 | tf_op jit(solution)/shard_map/ppermute | solution.py:157
  38.5 4.1 %collective-permute-done.9.refs_1_ = f32[32,2560]{1,0:T(8,128)S(1)} collective-permute-done((f32[32,2560]{1,0:T(8,128)S(1)}, f32[32,2560]{1,0:T(8,128)S(1)}, u32[]{:S(2)}, u32[]{:S(2)}) %collective-permute-start.9) | collective-permute-done | bytes 327712 | tf_op jit(solution)/shard_map/ppermute | solution.py:157
  42.8 2.7 %collective-permute-start.13 = (f32[32,2560]{1,0:T(8,128)S(1)}, f32[32,2560]{1,0:T(8,128)S(1)}, u32[]{:S(2)}, u32[]{:S(2)}) collective-permute-start(f32[32,2560]{1,0:T(8,128)S(1)} %get-tuple-element.50.refs_2_), channel_id=1, source_target_pairs={{0,32},{16,240},{32,64},{48,16},{64,96},{80,48},{96,128},{112,80},... | collective-permute-start | bytes 983048 | tf_op jit(solution)/shard_map/ppermute | solution.py:154
  45.5 1.9 %collective-permute-done.15.refs_1_ = f32[32,2560]{1,0:T(8,128)S(1)} collective-permute-done((f32[32,2560]{1,0:T(8,128)S(1)}, f32[32,2560]{1,0:T(8,128)S(1)}, u32[]{:S(2)}, u32[]{:S(2)}) %collective-permute-start.15) | collective-permute-done | bytes 327712 | tf_op jit(solution)/shard_map/ppermute | solution.py:157
  47.5 1.9 %collective-permute-start.16 = (f32[32,2560]{1,0:T(8,128)S(1)}, f32[32,2560]{1,0:T(8,128)S(1)}, u32[]{:S(2)}, u32[]{:S(2)}) collective-permute-start(f32[32,2560]{1,0:T(8,128)S(1)} %get-tuple-element.52.refs_2_), channel_id=1, source_target_pairs={{0,32},{16,240},{32,64},{48,16},{64,96},{80,48},{96,128},{112,80},... | collective-permute-start | bytes 983048 | tf_op jit(solution)/shard_map/ppermute | solution.py:154
  49.4 4.0 %collective-permute-done.12.refs_0_ = f32[32,2560]{1,0:T(8,128)S(1)} collective-permute-done((f32[32,2560]{1,0:T(8,128)S(1)}, f32[32,2560]{1,0:T(8,128)S(1)}, u32[]{:S(2)}, u32[]{:S(2)}) %collective-permute-start.12) | collective-permute-done | bytes 327712 | tf_op jit(solution)/shard_map/ppermute | solution.py:157
  53.5 6.6 %collective-permute-done.16 = f32[32,2560]{1,0:T(8,128)S(1)} collective-permute-done((f32[32,2560]{1,0:T(8,128)S(1)}, f32[32,2560]{1,0:T(8,128)S(1)}, u32[]{:S(2)}, u32[]{:S(2)}) %collective-permute-start.16) | collective-permute-done | bytes 327712 | tf_op jit(solution)/shard_map/ppermute | solution.py:154
  61.1 1.8 %collective-permute-start.18 = (f32[128]{0:T(128)S(1)}, f32[128]{0:T(128)S(1)}, u32[]{:S(2)}, u32[]{:S(2)}) collective-permute-start(f32[128]{0:T(128)S(1)} %pad_maximum_fusion.3), channel_id=1, source_target_pairs={{0,16},{16,0},{32,48},{48,32},{64,80},{80,64},{96,112},{112,96},{1... | collective-permute-start | bytes 1544 | tf_op jit(solution)/shard_map/ppermute | solution.py:188
  64.2 2.7 %collective-permute-start.19 = (f32[128]{0:T(128)S(1)}, f32[128]{0:T(128)S(1)}, u32[]{:S(2)}, u32[]{:S(2)}) collective-permute-start(f32[128]{0:T(128)S(1)} %pad_maximum_fusion.4), channel_id=1, source_target_pairs={{0,4},{1,5},{2,6},{3,7},{4,0},{5,1},{6,2},{7,3},{8,12},{9,13},{10,... | collective-permute-start | bytes 1544 | tf_op jit(solution)/shard_map/ppermute | solution.py:137
  68.1 2.5 %collective-permute-done.20 = f32[128]{0:T(128)S(1)} collective-permute-done((f32[128]{0:T(128)S(1)}, f32[128]{0:T(128)S(1)}, u32[]{:S(2)}, u32[]{:S(2)}) %collective-permute-start.20) | collective-permute-done | bytes 544 | tf_op jit(solution)/shard_map/ppermute | solution.py:137
  71.2 1.4 %collective-permute-start.24 = (f32[5248]{0:T(1024)S(1)}, f32[5248]{0:T(1024)S(1)}, u32[]{:S(2)}, u32[]{:S(2)}) collective-permute-start(f32[5248]{0:T(1024)S(1)} %pad_maximum_fusion.1), channel_id=1, source_target_pairs={{0,1},{1,0},{2,3},{3,2},{4,5},{5,4},{6,7},{7,6},{8,9},{9,8},{10,11... | collective-permute-start | bytes 62984 | tf_op jit(solution)/shard_map/ppermute | solution.py:137
  75.7 2.9 %collective-permute-start.26 = (f32[5248]{0:T(1024)S(1)}, f32[5248]{0:T(1024)S(1)}, u32[]{:S(2)}, u32[]{:S(2)}) collective-permute-start(f32[5248]{0:T(1024)S(1)} %add_add_fusion.1), channel_id=1, source_target_pairs={{0,1},{1,0},{2,3},{3,2},{4,5},{5,4},{6,7},{7,6},{8,9},{9,8},{10,11... | collective-permute-start | bytes 62984 | tf_op jit(solution)/shard_map/ppermute | solution.py:137
  79.8 2.9 %collective-permute-start.27 = (f32[5248]{0:T(1024)S(1)}, f32[5248]{0:T(1024)S(1)}, u32[]{:S(2)}, u32[]{:S(2)}) collective-permute-start(f32[5248]{0:T(1024)S(1)} %add.77), channel_id=1, source_target_pairs={{0,1},{1,0},{2,3},{3,2},{4,5},{5,4},{6,7},{7,6},{8,9},{9,8},{10,11... | collective-permute-start | bytes 62984 | tf_op jit(solution)/shard_map/ppermute | solution.py:137
  84.0 2.6 %collective-permute-done.28 = f32[5248]{0:T(1024)S(1)} collective-permute-done((f32[5248]{0:T(1024)S(1)}, f32[5248]{0:T(1024)S(1)}, u32[]{:S(2)}, u32[]{:S(2)}) %collective-permute-start.28) | collective-permute-done | bytes 21024 | tf_op jit(solution)/shard_map/ppermute | solution.py:137
  93.2 1.5 %shard_map.78 = (f32[64,2560]{1,0:T(8,128)}, f32[1,1]{1,0:T(1,128)}) custom-call(f32[64,2560]{1,0:T(8,128)S(1)} %rsqrt_multiply_fusion.scaled, f32[1,128]{1,0:T(1,128)S(1)} %get-tuple-element.69.row_sum, f32[1,128]{1,0:T(1,128)S(1)} %get-tuple-element.68.total), custom_call_target="tpu_custom_call" | custom-call | flops 1150000000 | tf_op jit(solution)/shard_map/pallas_call | solution.py:110
  (90 shorter events, 26.4 us)
Async XLA Ops:
  1.7 5.1 %collective-permute-start.1 = (f32[1,64,2560]{2,1,0:T(8,128)S(1)}, f32[1,64,2560]{2,1,0:T(8,128)S(1)}, u32[]{:S(2)}, u32[]{:S(2)}) collective-permute-start(f32[1,64,2560]{2,1,0:T(8,128)S(1)} %get-tuple-element.35), channel_id=1, source_target_pairs={{0,16},{16,0},{32,48},{48,32},{64,80},{80,64},{96,112},{112,96},{1... | collective-permute-start | bytes 1966088 | tf_op jit(solution)/shard_map/ppermute | solution.py:70
  6.4 4.4 %collective-permute-start = (f32[2,64,2560]{2,1,0:T(8,128)S(1)}, f32[2,64,2560]{2,1,0:T(8,128)S(1)}, u32[]{:S(2)}, u32[]{:S(2)}) collective-permute-start(f32[2,64,2560]{2,1,0:T(8,128)S(1)} %get-tuple-element.34), channel_id=1, source_target_pairs={{0,16},{16,0},{32,48},{48,32},{64,80},{80,64},{96,112},{112,96},{1... | collective-permute-start | bytes 3932168 | tf_op jit(solution)/shard_map/ppermute | solution.py:70
  6.9 10.5 %collective-permute-start.6 = (f32[32,2560]{1,0:T(8,128)S(1)}, f32[32,2560]{1,0:T(8,128)S(1)}, u32[]{:S(2)}, u32[]{:S(2)}) collective-permute-start(f32[32,2560]{1,0:T(8,128)S(1)} %get-tuple-element.36.refs_0_), channel_id=1, source_target_pairs={{0,32},{16,240},{32,64},{48,16},{64,96},{80,48},{96,128},{112,80},... | collective-permute-start | bytes 983048 | tf_op jit(solution)/shard_map/ppermute | solution.py:154
  10.8 11.0 %collective-permute-start.7 = (f32[32,2560]{1,0:T(8,128)S(1)}, f32[32,2560]{1,0:T(8,128)S(1)}, u32[]{:S(2)}, u32[]{:S(2)}) collective-permute-start(f32[32,2560]{1,0:T(8,128)S(1)} %get-tuple-element.43), channel_id=1, source_target_pairs={{32,0},{240,16},{64,32},{16,48},{96,64},{48,80},{128,96},{80,112},... | collective-permute-start | bytes 983048 | tf_op jit(solution)/shard_map/ppermute | solution.py:157
  12.2 12.2 %collective-permute-start.4 = (f32[32,2560]{1,0:T(8,128)S(1)}, f32[32,2560]{1,0:T(8,128)S(1)}, u32[]{:S(2)}, u32[]{:S(2)}) collective-permute-start(f32[32,2560]{1,0:T(8,128)S(1)} %get-tuple-element.37.refs_0_), channel_id=1, source_target_pairs={{0,32},{16,240},{32,64},{48,16},{64,96},{80,48},{96,128},{112,80},... | collective-permute-start | bytes 983048 | tf_op jit(solution)/shard_map/ppermute | solution.py:154
  16.5 12.1 %collective-permute-start.3 = (f32[2,64,2560]{2,1,0:T(8,128)S(1)}, f32[2,64,2560]{2,1,0:T(8,128)S(1)}, u32[]{:S(2)}, u32[]{:S(2)}) collective-permute-start(f32[2,64,2560]{2,1,0:T(8,128)S(1)} %get-tuple-element.41), channel_id=1, source_target_pairs={{0,16},{16,0},{32,48},{48,32},{64,80},{80,64},{96,112},{112,96},{1... | collective-permute-start | bytes 3932168 | tf_op jit(solution)/shard_map/ppermute | solution.py:70
  16.6 12.0 %collective-permute-start.5 = (f32[32,2560]{1,0:T(8,128)S(1)}, f32[32,2560]{1,0:T(8,128)S(1)}, u32[]{:S(2)}, u32[]{:S(2)}) collective-permute-start(f32[32,2560]{1,0:T(8,128)S(1)} %get-tuple-element.42), channel_id=1, source_target_pairs={{32,0},{240,16},{64,32},{16,48},{96,64},{48,80},{128,96},{80,112},... | collective-permute-start | bytes 983048 | tf_op jit(solution)/shard_map/ppermute | solution.py:157
  21.9 9.6 %collective-permute-start.10 = (f32[32,2560]{1,0:T(8,128)S(1)}, f32[32,2560]{1,0:T(8,128)S(1)}, u32[]{:S(2)}, u32[]{:S(2)}) collective-permute-start(f32[32,2560]{1,0:T(8,128)S(1)} %get-tuple-element.44.refs_2_), channel_id=1, source_target_pairs={{0,32},{16,240},{32,64},{48,16},{64,96},{80,48},{96,128},{112,80},... | collective-permute-start | bytes 983048 | tf_op jit(solution)/shard_map/ppermute | solution.py:154
  22.0 13.6 %collective-permute-start.11 = (f32[32,2560]{1,0:T(8,128)S(1)}, f32[32,2560]{1,0:T(8,128)S(1)}, u32[]{:S(2)}, u32[]{:S(2)}) collective-permute-start(f32[32,2560]{1,0:T(8,128)S(1)} %get-tuple-element.47), channel_id=1, source_target_pairs={{32,0},{240,16},{64,32},{16,48},{96,64},{48,80},{128,96},{80,112},... | collective-permute-start | bytes 983048 | tf_op jit(solution)/shard_map/ppermute | solution.py:157
  24.4 18.2 %collective-permute-start.2 = (f32[3,64,2560]{2,1,0:T(8,128)S(1)}, f32[3,64,2560]{2,1,0:T(8,128)S(1)}, u32[]{:S(2)}, u32[]{:S(2)}) collective-permute-start(f32[3,64,2560]{2,1,0:T(8,128)S(1)} %get-tuple-element.40), channel_id=1, source_target_pairs={{0,16},{16,0},{32,48},{48,32},{64,80},{80,64},{96,112},{112,96},{1... | collective-permute-start | bytes 5898248 | tf_op jit(solution)/shard_map/ppermute | solution.py:70
  28.6 9.8 %collective-permute-start.8 = (f32[32,2560]{1,0:T(8,128)S(1)}, f32[32,2560]{1,0:T(8,128)S(1)}, u32[]{:S(2)}, u32[]{:S(2)}) collective-permute-start(f32[32,2560]{1,0:T(8,128)S(1)} %get-tuple-element.45.refs_2_), channel_id=1, source_target_pairs={{0,32},{16,240},{32,64},{48,16},{64,96},{80,48},{96,128},{112,80},... | collective-permute-start | bytes 983048 | tf_op jit(solution)/shard_map/ppermute | solution.py:154
  28.9 13.7 %collective-permute-start.9 = (f32[32,2560]{1,0:T(8,128)S(1)}, f32[32,2560]{1,0:T(8,128)S(1)}, u32[]{:S(2)}, u32[]{:S(2)}) collective-permute-start(f32[32,2560]{1,0:T(8,128)S(1)} %get-tuple-element.46), channel_id=1, source_target_pairs={{32,0},{240,16},{64,32},{16,48},{96,64},{48,80},{128,96},{80,112},... | collective-permute-start | bytes 983048 | tf_op jit(solution)/shard_map/ppermute | solution.py:157
  35.7 9.8 %collective-permute-start.14 = (f32[32,2560]{1,0:T(8,128)S(1)}, f32[32,2560]{1,0:T(8,128)S(1)}, u32[]{:S(2)}, u32[]{:S(2)}) collective-permute-start(f32[32,2560]{1,0:T(8,128)S(1)} %get-tuple-element.48.refs_2_), channel_id=1, source_target_pairs={{0,32},{16,240},{32,64},{48,16},{64,96},{80,48},{96,128},{112,80},... | collective-permute-start | bytes 983048 | tf_op jit(solution)/shard_map/ppermute | solution.py:154
  35.7 11.6 %collective-permute-start.15 = (f32[32,2560]{1,0:T(8,128)S(1)}, f32[32,2560]{1,0:T(8,128)S(1)}, u32[]{:S(2)}, u32[]{:S(2)}) collective-permute-start(f32[32,2560]{1,0:T(8,128)S(1)} %get-tuple-element.51), channel_id=1, source_target_pairs={{32,0},{240,16},{64,32},{16,48},{96,64},{48,80},{128,96},{80,112},... | collective-permute-start | bytes 983048 | tf_op jit(solution)/shard_map/ppermute | solution.py:157
  42.7 10.7 %collective-permute-start.12 = (f32[32,2560]{1,0:T(8,128)S(1)}, f32[32,2560]{1,0:T(8,128)S(1)}, u32[]{:S(2)}, u32[]{:S(2)}) collective-permute-start(f32[32,2560]{1,0:T(8,128)S(1)} %get-tuple-element.49), channel_id=1, source_target_pairs={{32,0},{240,16},{64,32},{16,48},{96,64},{48,80},{128,96},{80,112},... | collective-permute-start | bytes 983048 | tf_op jit(solution)/shard_map/ppermute | solution.py:157
  42.8 10.6 %collective-permute-start.13 = (f32[32,2560]{1,0:T(8,128)S(1)}, f32[32,2560]{1,0:T(8,128)S(1)}, u32[]{:S(2)}, u32[]{:S(2)}) collective-permute-start(f32[32,2560]{1,0:T(8,128)S(1)} %get-tuple-element.50.refs_2_), channel_id=1, source_target_pairs={{0,32},{16,240},{32,64},{48,16},{64,96},{80,48},{96,128},{112,80},... | collective-permute-start | bytes 983048 | tf_op jit(solution)/shard_map/ppermute | solution.py:154
  47.5 12.6 %collective-permute-start.16 = (f32[32,2560]{1,0:T(8,128)S(1)}, f32[32,2560]{1,0:T(8,128)S(1)}, u32[]{:S(2)}, u32[]{:S(2)}) collective-permute-start(f32[32,2560]{1,0:T(8,128)S(1)} %get-tuple-element.52.refs_2_), channel_id=1, source_target_pairs={{0,32},{16,240},{32,64},{48,16},{64,96},{80,48},{96,128},{112,80},... | collective-permute-start | bytes 983048 | tf_op jit(solution)/shard_map/ppermute | solution.py:154
  49.4 11.0 %collective-permute-start.17 = (f32[32,2560]{1,0:T(8,128)S(1)}, f32[32,2560]{1,0:T(8,128)S(1)}, u32[]{:S(2)}, u32[]{:S(2)}) collective-permute-start(f32[32,2560]{1,0:T(8,128)S(1)} %get-tuple-element.55), channel_id=1, source_target_pairs={{32,0},{240,16},{64,32},{16,48},{96,64},{48,80},{128,96},{80,112},... | collective-permute-start | bytes 983048 | tf_op jit(solution)/shard_map/ppermute | solution.py:157
  63.7 7.1 %collective-permute-start.22 = (f32[64,2560]{1,0:T(8,128)S(1)}, f32[64,2560]{1,0:T(8,128)S(1)}, u32[]{:S(2)}, u32[]{:S(2)}) collective-permute-start(f32[64,2560]{1,0:T(8,128)S(1)} %pad_maximum_fusion), channel_id=1, source_target_pairs={{0,16},{16,0},{32,48},{48,32},{64,80},{80,64},{96,112},{112,96},{1... | collective-permute-start | bytes 1966088 | tf_op jit(solution)/shard_map/ppermute | solution.py:190
  64.2 3.9 %collective-permute-start.19 = (f32[128]{0:T(128)S(1)}, f32[128]{0:T(128)S(1)}, u32[]{:S(2)}, u32[]{:S(2)}) collective-permute-start(f32[128]{0:T(128)S(1)} %pad_maximum_fusion.4), channel_id=1, source_target_pairs={{0,4},{1,5},{2,6},{3,7},{4,0},{5,1},{6,2},{7,3},{8,12},{9,13},{10,... | collective-permute-start | bytes 1544 | tf_op jit(solution)/shard_map/ppermute | solution.py:137
  71.2 4.6 %collective-permute-start.24 = (f32[5248]{0:T(1024)S(1)}, f32[5248]{0:T(1024)S(1)}, u32[]{:S(2)}, u32[]{:S(2)}) collective-permute-start(f32[5248]{0:T(1024)S(1)} %pad_maximum_fusion.1), channel_id=1, source_target_pairs={{0,1},{1,0},{2,3},{3,2},{4,5},{5,4},{6,7},{7,6},{8,9},{9,8},{10,11... | collective-permute-start | bytes 62984 | tf_op jit(solution)/shard_map/ppermute | solution.py:137
  75.7 4.1 %collective-permute-start.26 = (f32[5248]{0:T(1024)S(1)}, f32[5248]{0:T(1024)S(1)}, u32[]{:S(2)}, u32[]{:S(2)}) collective-permute-start(f32[5248]{0:T(1024)S(1)} %add_add_fusion.1), channel_id=1, source_target_pairs={{0,1},{1,0},{2,3},{3,2},{4,5},{5,4},{6,7},{7,6},{8,9},{9,8},{10,11... | collective-permute-start | bytes 62984 | tf_op jit(solution)/shard_map/ppermute | solution.py:137
  79.8 4.2 %collective-permute-start.27 = (f32[5248]{0:T(1024)S(1)}, f32[5248]{0:T(1024)S(1)}, u32[]{:S(2)}, u32[]{:S(2)}) collective-permute-start(f32[5248]{0:T(1024)S(1)} %add.77), channel_id=1, source_target_pairs={{0,1},{1,0},{2,3},{3,2},{4,5},{5,4},{6,7},{7,6},{8,9},{9,8},{10,11... | collective-permute-start | bytes 62984 | tf_op jit(solution)/shard_map/ppermute | solution.py:137
  86.7 4.0 %collective-permute-start.30 = (f32[128]{0:T(128)S(1)}, f32[128]{0:T(128)S(1)}, u32[]{:S(2)}, u32[]{:S(2)}) collective-permute-start(f32[128]{0:T(128)S(1)} %get-tuple-element.64), channel_id=1, source_target_pairs={{0,4},{1,5},{2,6},{3,7},{4,0},{5,1},{6,2},{7,3},{8,12},{9,13},{10,... | collective-permute-start | bytes 1544 | tf_op jit(solution)/shard_map/ppermute | solution.py:137
  (14 other events, 60.8 us)

commit v4 on v3

--- a/solution.py
+++ b/solution.py
@@ -12,7 +12,6 @@
 HALF = 32
 ROWS = 64
 COLS = 2560
-ORDER = (2, 3, 1)
 
 SWAP = [(i, i ^ 1) for i in range(16)]
 UP = [(2 * z + c, 2 * ((z + 1 - 2 * c) % 8) + c) for z in range(8) for c in range(2)]
@@ -28,8 +27,10 @@
     return pl.CostEstimate(flops=int(micros * 1.15e9), bytes_accessed=0, transcendentals=0)
 
 
-def fetch_kernel(ks, n_in, parts, *refs):
-    own, sent, buf, own_sems, sems = refs[n_in:]
+def fetch_kernel(ks, split, n_in, parts, *refs):
+    own, *sent = refs[n_in:-3]
+    buf, own_sems, sems = refs[-3:]
+    height = ROWS // split
     me = lax.axis_index("dp")
     core = jnp.bitwise_and(me, 1)
     z = lax.shift_right_logical(me, 1) + 8
@@ -44,21 +45,20 @@
         copy.start()
     for i, copy in enumerate(copies):
         copy.wait()
-        sent[i] = buf[i].astype(jnp.float32)
+        for j in range(split):
+            sent[j][i] = buf[i, j * height:(j + 1) * height].astype(jnp.float32)
     for copy in own_copies:
         copy.wait()
 
 
-def fetch(ks, parts, *after, micros=0):
+def fetch(ks, parts, *after, split=1, micros=0):
     n = len(ks)
-    own, sent = pl.pallas_call(
-        functools.partial(fetch_kernel, ks, len(after)),
-        out_shape=[
-            jax.ShapeDtypeStruct((n, ROWS, COLS), jnp.bfloat16),
-            jax.ShapeDtypeStruct((n, ROWS, COLS), jnp.float32),
-        ],
+    own, *sent = pl.pallas_call(
+        functools.partial(fetch_kernel, ks, split, len(after)),
+        out_shape=[jax.ShapeDtypeStruct((n, ROWS, COLS), jnp.bfloat16)]
+        + [jax.ShapeDtypeStruct((n, ROWS // split, COLS), jnp.float32)] * split,
         in_specs=[HBM] + [ANY] * len(after),
-        out_specs=[VMEM, VMEM],
+        out_specs=[VMEM] * (1 + split),
         scratch_shapes=[
             pltpu.VMEM((n, ROWS, COLS), jnp.bfloat16),
             pltpu.SemaphoreType.DMA((n,)),
@@ -67,14 +67,15 @@
         compiler_params=PARAMS,
         cost_estimate=told(micros),
     )(parts, *after)
-    return own, lax.ppermute(sent, "dp", SWAP)
+    return own, *(lax.ppermute(x, "dp", SWAP) for x in sent)
 
 
 def add_kernel(terms, n_in, own, sib, *refs):
     outs = refs[n_in:]
     for i, (block, half, has_state) in enumerate(terms):
         rows = slice(half * HALF, (half + 1) * HALF)
-        total = own[block, rows].astype(jnp.float32) + sib[block, rows]
+        other = sib[block, rows] if sib.shape[1] == ROWS else sib[block]
+        total = own[block, rows].astype(jnp.float32) + other
         if has_state:
             total = total + refs[i][...]
         outs[i][...] = total
@@ -89,6 +90,21 @@
         compiler_params=PARAMS,
         cost_estimate=told(micros),
     )(*blocks, *states, *after)
+
+
+def hold_kernel(x, _, out):
+    out[...] = x[...]
+
+
+def hold(x, after):
+    return pl.pallas_call(
+        hold_kernel,
+        out_shape=jax.ShapeDtypeStruct(x.shape, x.dtype),
+        in_specs=[VMEM, ANY],
+        out_specs=VMEM,
+        compiler_params=PARAMS,
+        cost_estimate=told(0),
+    )(x, after)
 
 
 def final_kernel(scaled, row_sum, total, out, rms, buf, sems):
@@ -137,13 +153,13 @@
     return lax.ppermute(v, ("dp", "row", "col"), pairs)
 
 
-def sum_four(v, axis, idle=None):
+def sum_four(v, axis, idle=None, masks=(2, 3, 1)):
     unit = [0, 0, 0]
-    got = {}
-    for mask in ORDER:
+    got = []
+    for mask in masks:
         unit[axis] = mask
-        got[mask] = exchange(v, tuple(unit), idle)
-    return (got[2] + got[3]) + (got[1] + v)
+        got.append(exchange(v, tuple(unit), idle))
+    return (got[0] + got[1]) + (got[2] + v)
 
 
 def on_device(grad_parts, row_old, col_old):
@@ -156,11 +172,14 @@
     def down(x):
         return lax.ppermute(x, "dp", DOWN)
 
-    far = fetch((4,), parts)
-    third = fetch((3, -3), parts, far[0], micros=40)
-    a, b = add(far, ((0, 0), (0, 1)), after=(third[0],))
-    after = a
-    a, b = up(a), down(b)
+    far, far_up, far_down = fetch((4,), parts, split=2)
+    third = fetch((3, -3), parts, far, micros=40)
+    (a,) = add((far, far_up), ((0, 0),), after=(third[0],))
+    after = a
+    a = up(a)
+    (b,) = add((far, far_down), ((0, 1),), after=(after,))
+    after = b
+    b = down(b)
     c, d = add(third, ((0, 1), (1, 0)), after=(after,))
     second = fetch((2, -2), parts, c)
     near = fetch((1, -1, 0), parts, second[0])
@@ -180,7 +199,8 @@
     a, b = add(near, ((0, 0), (1, 1)), (a, b), after=(after,))
     after = a
     a, b = up(a), down(b)
-    upper, lower = add(near, ((2, 0), (2, 1)), (d, c), after=(after,))
+    row_old = hold(row_old, after)
+    upper, lower = add(near, ((2, 0), (2, 1)), (d, c), after=(row_old,))
     grad = jnp.concatenate([upper + a, lower + b], axis=0)
 
     grad = lax.optimization_barrier(grad)
@@ -199,8 +219,8 @@
         packed.append(sums)
     packed = jnp.concatenate([*packed, row_new])
 
-    packed = sum_four(packed, 0, (0, 0, 1))
-    packed = packed + exchange(packed, (7, 0, 0), (0, 0, 1))
+    packed = sum_four(packed, 0, (0, 0, 1), (6, 7, 1))
+    packed = packed + exchange(packed, (2, 0, 0), (0, 0, 1))
     packed = sum_four(packed, 1, (0, 0, 1))
     col_new = 0.8 * col_old + 0.2 * packed[:COLS] / D
     total = jnp.sum((packed[COLS:2 * COLS] / col_new).reshape(20, 128), axis=0)

time: 95.1 us -> 97 us (1.020)
  starting transfers between devices: 38.1 us -> 44.4 us
  waiting for transfers between devices: 46.6 us -> 42.5 us
    ppermute x7, starting transfers between devices: 11.7 us -> 18.1 us  [up(): return lax.ppermute(x, 'dp', UP)]
    ppermute x7, waiting for transfers between devices: 22.6 us -> 18 us  [down(): return lax.ppermute(x, 'dp', DOWN)]
    ppermute x13, starting transfers between devices: 15.7 us -> 18.6 us  [exchange(): return lax.ppermute(v, ('dp', 'row', 'col'), pairs)]
    ppermute x7, starting transfers between devices: 4.33 us -> 1.97 us  [down(): return lax.ppermute(x, 'dp', DOWN)]
    ppermute x7, waiting for transfers between devices: 10.8 us -> 11.8 us  [up(): return lax.ppermute(x, 'dp', UP)]
    ppermute x4 -> x5, starting transfers between devices: 3.96 us -> 4.02 us  [fetch(): return (own, *(lax.ppermute(x, 'dp', SWAP) for x in sent))]
    pallas_call x4 -> x5, Pallas kernels: 5.24 us -> 5.25 us  [the longest x4 5.24 us: fetch(): pl.pallas_call(functools.partial(fetch_kernel, ks, split, len(after)), ou...]
  transfers between devices with their start and end apart: 34 -> 35, of which waited for: 24 -> 22; matrix products, arithmetic and copies ran while one was open for 1% -> 1% of each run, Pallas kernels for 5% -> 5%
where the time goes in v4:
time: 97 us; the launch traced here: 96.9 us
  starting transfers between devices  44.4 us (46%)
  waiting for transfers between devices  42.5 us (44%)
  Pallas kernels  7.51 us (8%)
  other arithmetic  1.17 us (1%)
  between operations  1.1 us (1%)
    ppermute x13, starting transfers between devices, exchange(): return lax.ppermute(v, ('dp', 'row', 'col'), pairs)  18.6 us
    ppermute x7, starting transfers between devices, up(): return lax.ppermute(x, 'dp', UP)  18.1 us
    ppermute x7, waiting for transfers between devices, down(): return lax.ppermute(x, 'dp', DOWN)  18 us
    ppermute x7, waiting for transfers between devices, up(): return lax.ppermute(x, 'dp', UP)  11.8 us
    ppermute x13, waiting for transfers between devices, exchange(): return lax.ppermute(v, ('dp', 'row', 'col'), pairs)  10.7 us
    pallas_call x4, Pallas kernels, fetch(): pl.pallas_call(functools.partial(fetch_kernel, ks, split, len(after)), ou...  5.24 us
    ppermute x5, starting transfers between devices, fetch(): return (own, *(lax.ppermute(x, 'dp', SWAP) for x in sent))  4.02 us
    ppermute x7, starting transfers between devices, down(): return lax.ppermute(x, 'dp', DOWN)  1.97 us
  transfers between devices with their start and end apart: 35, of which 22 were waited for; matrix products, arithmetic and copies ran while one was open for 1% of the time, Pallas kernels for 5%

profile of v4, /device:TPU:1, one launch (start us, length us, event | category | flops | bytes accessed | tf_op | source)
XLA Modules:
  0.0 96.9 jit_solution(2522673680591625003)
XLA Ops:
  1.7 3.3 %collective-permute-start.2 = (f32[1,32,2560]{2,1,0:T(8,128)S(1)}, f32[1,32,2560]{2,1,0:T(8,128)S(1)}, u32[]{:S(2)}, u32[]{:S(2)}) collective-permute-start(f32[1,32,2560]{2,1,0:T(8,128)S(1)} %get-tuple-element.35), channel_id=1, source_target_pairs={{0,16},{16,0},{32,48},{48,32},{64,80},{80,64},{96,112},{112,96},{1... | collective-permute-start | bytes 983048 | tf_op jit(solution)/shard_map/ppermute | solution.py:70
  7.0 3.9 %collective-permute-start.7 = (f32[32,2560]{1,0:T(8,128)S(1)}, f32[32,2560]{1,0:T(8,128)S(1)}, u32[]{:S(2)}, u32[]{:S(2)}) collective-permute-start(f32[32,2560]{1,0:T(8,128)S(1)} %shard_map.68.refs_0_), channel_id=1, source_target_pairs={{0,32},{16,240},{32,64},{48,16},{64,96},{80,48},{96,128},{112,80},... | collective-permute-start | bytes 983048 | tf_op jit(solution)/shard_map/ppermute | solution.py:170
  12.5 2.7 %collective-permute-start.5 = (f32[32,2560]{1,0:T(8,128)S(1)}, f32[32,2560]{1,0:T(8,128)S(1)}, u32[]{:S(2)}, u32[]{:S(2)}) collective-permute-start(f32[32,2560]{1,0:T(8,128)S(1)} %get-tuple-element.36.refs_0_), channel_id=1, source_target_pairs={{0,32},{16,240},{32,64},{48,16},{64,96},{80,48},{96,128},{112,80},... | collective-permute-start | bytes 983048 | tf_op jit(solution)/shard_map/ppermute | solution.py:170
  15.2 1.5 %shard_map.72 = (bf16[3,64,2560]{2,1,0:T(8,128)(2,1)S(1)}, f32[3,64,2560]{2,1,0:T(8,128)S(1)}) custom-call(bf16[16,64,2560]{2,1,0:T(8,128)(2,1)} %bitcast.19, bf16[2,64,2560]{2,1,0:T(8,128)(2,1)S(1)} %get-tuple-element.37.refs_0_.own), custom_call_target="tpu_custom_call" | custom-call | tf_op jit(solution)/shard_map/pallas_call | solution.py:56
  16.9 4.7 %collective-permute-done.8.refs_1_ = f32[32,2560]{1,0:T(8,128)S(1)} collective-permute-done((f32[32,2560]{1,0:T(8,128)S(1)}, f32[32,2560]{1,0:T(8,128)S(1)}, u32[]{:S(2)}, u32[]{:S(2)}) %collective-permute-start.8) | collective-permute-done | bytes 327712 | tf_op jit(solution)/shard_map/ppermute | solution.py:173
  21.8 1.5 %collective-permute-start.12 = (f32[32,2560]{1,0:T(8,128)S(1)}, f32[32,2560]{1,0:T(8,128)S(1)}, u32[]{:S(2)}, u32[]{:S(2)}) collective-permute-start(f32[32,2560]{1,0:T(8,128)S(1)} %get-tuple-element.45), channel_id=1, source_target_pairs={{32,0},{240,16},{64,32},{16,48},{96,64},{48,80},{128,96},{80,112},... | collective-permute-start | bytes 983048 | tf_op jit(solution)/shard_map/ppermute | solution.py:173
  23.2 1.6 %collective-permute-done.5.refs_0_ = f32[32,2560]{1,0:T(8,128)S(1)} collective-permute-done((f32[32,2560]{1,0:T(8,128)S(1)}, f32[32,2560]{1,0:T(8,128)S(1)}, u32[]{:S(2)}, u32[]{:S(2)}) %collective-permute-start.5) | collective-permute-done | bytes 327712 | tf_op jit(solution)/shard_map/ppermute | solution.py:170
  24.8 3.6 %collective-permute-done.6.refs_1_ = f32[32,2560]{1,0:T(8,128)S(1)} collective-permute-done((f32[32,2560]{1,0:T(8,128)S(1)}, f32[32,2560]{1,0:T(8,128)S(1)}, u32[]{:S(2)}, u32[]{:S(2)}) %collective-permute-start.6) | collective-permute-done | bytes 327712 | tf_op jit(solution)/shard_map/ppermute | solution.py:173
  28.6 2.7 %collective-permute-start.9 = (f32[32,2560]{1,0:T(8,128)S(1)}, f32[32,2560]{1,0:T(8,128)S(1)}, u32[]{:S(2)}, u32[]{:S(2)}) collective-permute-start(f32[32,2560]{1,0:T(8,128)S(1)} %get-tuple-element.43.refs_2_), channel_id=1, source_target_pairs={{0,32},{16,240},{32,64},{48,16},{64,96},{80,48},{96,128},{112,80},... | collective-permute-start | bytes 983048 | tf_op jit(solution)/shard_map/ppermute | solution.py:170
  33.3 2.4 %collective-permute-start.15 = (f32[32,2560]{1,0:T(8,128)S(1)}, f32[32,2560]{1,0:T(8,128)S(1)}, u32[]{:S(2)}, u32[]{:S(2)}) collective-permute-start(f32[32,2560]{1,0:T(8,128)S(1)} %get-tuple-element.46.refs_2_), channel_id=1, source_target_pairs={{0,32},{16,240},{32,64},{48,16},{64,96},{80,48},{96,128},{112,80},... | collective-permute-start | bytes 983048 | tf_op jit(solution)/shard_map/ppermute | solution.py:170
  35.7 3.5 %collective-permute-done.10.refs_1_ = f32[32,2560]{1,0:T(8,128)S(1)} collective-permute-done((f32[32,2560]{1,0:T(8,128)S(1)}, f32[32,2560]{1,0:T(8,128)S(1)}, u32[]{:S(2)}, u32[]{:S(2)}) %collective-permute-start.10) | collective-permute-done | bytes 327712 | tf_op jit(solution)/shard_map/ppermute | solution.py:173
  39.6 3.4 %collective-permute-start.14 = (f32[32,2560]{1,0:T(8,128)S(1)}, f32[32,2560]{1,0:T(8,128)S(1)}, u32[]{:S(2)}, u32[]{:S(2)}) collective-permute-start(f32[32,2560]{1,0:T(8,128)S(1)} %get-tuple-element.48.refs_2_), channel_id=1, source_target_pairs={{0,32},{16,240},{32,64},{48,16},{64,96},{80,48},{96,128},{112,80},... | collective-permute-start | bytes 983048 | tf_op jit(solution)/shard_map/ppermute | solution.py:170
  43.0 2.9 %collective-permute-done.15.refs_0_ = f32[32,2560]{1,0:T(8,128)S(1)} collective-permute-done((f32[32,2560]{1,0:T(8,128)S(1)}, f32[32,2560]{1,0:T(8,128)S(1)}, u32[]{:S(2)}, u32[]{:S(2)}) %collective-permute-start.15) | collective-permute-done | bytes 327712 | tf_op jit(solution)/shard_map/ppermute | solution.py:170
  46.8 2.9 %collective-permute-start.17 = (f32[32,2560]{1,0:T(8,128)S(1)}, f32[32,2560]{1,0:T(8,128)S(1)}, u32[]{:S(2)}, u32[]{:S(2)}) collective-permute-start(f32[32,2560]{1,0:T(8,128)S(1)} %get-tuple-element.50._), channel_id=1, source_target_pairs={{0,32},{16,240},{32,64},{48,16},{64,96},{80,48},{96,128},{112,80},... | collective-permute-start | bytes 983048 | tf_op jit(solution)/shard_map/ppermute | solution.py:170
  49.8 3.3 %collective-permute-done.13.refs_0_ = f32[32,2560]{1,0:T(8,128)S(1)} collective-permute-done((f32[32,2560]{1,0:T(8,128)S(1)}, f32[32,2560]{1,0:T(8,128)S(1)}, u32[]{:S(2)}, u32[]{:S(2)}) %collective-permute-start.13) | collective-permute-done | bytes 327712 | tf_op jit(solution)/shard_map/ppermute | solution.py:173
  53.2 6.8 %collective-permute-done.17 = f32[32,2560]{1,0:T(8,128)S(1)} collective-permute-done((f32[32,2560]{1,0:T(8,128)S(1)}, f32[32,2560]{1,0:T(8,128)S(1)}, u32[]{:S(2)}, u32[]{:S(2)}) %collective-permute-start.17) | collective-permute-done | bytes 327712 | tf_op jit(solution)/shard_map/ppermute | solution.py:170
  63.7 2.7 %collective-permute-start.20 = (f32[128]{0:T(128)S(1)}, f32[128]{0:T(128)S(1)}, u32[]{:S(2)}, u32[]{:S(2)}) collective-permute-start(f32[128]{0:T(128)S(1)} %pad_maximum_fusion.4), channel_id=1, source_target_pairs={{0,4},{1,5},{2,6},{3,7},{4,0},{5,1},{6,2},{7,3},{8,12},{9,13},{10,... | collective-permute-start | bytes 1544 | tf_op jit(solution)/shard_map/ppermute | solution.py:153
  67.6 2.5 %collective-permute-done.21 = f32[128]{0:T(128)S(1)} collective-permute-done((f32[128]{0:T(128)S(1)}, f32[128]{0:T(128)S(1)}, u32[]{:S(2)}, u32[]{:S(2)}) %collective-permute-start.21) | collective-permute-done | bytes 544 | tf_op jit(solution)/shard_map/ppermute | solution.py:153
  70.6 2.0 %collective-permute-start.24 = (f32[5248]{0:T(1024)S(1)}, f32[5248]{0:T(1024)S(1)}, u32[]{:S(2)}, u32[]{:S(2)}) collective-permute-start(f32[5248]{0:T(1024)S(1)} %pad_maximum_fusion.1), channel_id=1, source_target_pairs={{0,1},{1,0},{2,3},{3,2},{4,5},{5,4},{6,7},{7,6},{8,9},{9,8},{10,11... | collective-permute-start | bytes 62984 | tf_op jit(solution)/shard_map/ppermute | solution.py:153
  73.1 2.3 %collective-permute-start.26 = (f32[5248]{0:T(1024)S(1)}, f32[5248]{0:T(1024)S(1)}, u32[]{:S(2)}, u32[]{:S(2)}) collective-permute-start(f32[5248]{0:T(1024)S(1)} %pad_maximum_fusion.1), channel_id=1, source_target_pairs={{0,1},{1,0},{2,3},{3,2},{4,5},{5,4},{6,7},{7,6},{8,9},{9,8},{10,11... | collective-permute-start | bytes 62984 | tf_op jit(solution)/shard_map/ppermute | solution.py:153
  76.9 3.7 %collective-permute-start.27 = (f32[5248]{0:T(1024)S(1)}, f32[5248]{0:T(1024)S(1)}, u32[]{:S(2)}, u32[]{:S(2)}) collective-permute-start(f32[5248]{0:T(1024)S(1)} %add_add_fusion.1), channel_id=1, source_target_pairs={{0,1},{1,0},{2,3},{3,2},{4,5},{5,4},{6,7},{7,6},{8,9},{9,8},{10,11... | collective-permute-start | bytes 62984 | tf_op jit(solution)/shard_map/ppermute | solution.py:153
  81.8 2.9 %collective-permute-start.28 = (f32[5248]{0:T(1024)S(1)}, f32[5248]{0:T(1024)S(1)}, u32[]{:S(2)}, u32[]{:S(2)}) collective-permute-start(f32[5248]{0:T(1024)S(1)} %add.77), channel_id=1, source_target_pairs={{0,1},{1,0},{2,3},{3,2},{4,5},{5,4},{6,7},{7,6},{8,9},{9,8},{10,11... | collective-permute-start | bytes 62984 | tf_op jit(solution)/shard_map/ppermute | solution.py:153
  86.0 2.6 %collective-permute-done.29 = f32[5248]{0:T(1024)S(1)} collective-permute-done((f32[5248]{0:T(1024)S(1)}, f32[5248]{0:T(1024)S(1)}, u32[]{:S(2)}, u32[]{:S(2)}) %collective-permute-start.29) | collective-permute-done | bytes 21024 | tf_op jit(solution)/shard_map/ppermute | solution.py:153
  95.1 1.5 %shard_map.80 = (f32[64,2560]{1,0:T(8,128)}, f32[1,1]{1,0:T(1,128)}) custom-call(f32[64,2560]{1,0:T(8,128)S(1)} %rsqrt_multiply_fusion.scaled, f32[1,128]{1,0:T(1,128)S(1)} %get-tuple-element.67.row_sum, f32[1,128]{1,0:T(1,128)S(1)} %get-tuple-element.66.total), custom_call_target="tpu_custom_call" | custom-call | flops 1150000000 | tf_op jit(solution)/shard_map/pallas_call | solution.py:126
  (94 shorter events, 24.9 us)
Async XLA Ops:
  1.7 5.2 %collective-permute-start.2 = (f32[1,32,2560]{2,1,0:T(8,128)S(1)}, f32[1,32,2560]{2,1,0:T(8,128)S(1)}, u32[]{:S(2)}, u32[]{:S(2)}) collective-permute-start(f32[1,32,2560]{2,1,0:T(8,128)S(1)} %get-tuple-element.35), channel_id=1, source_target_pairs={{0,16},{16,0},{32,48},{48,32},{64,80},{80,64},{96,112},{112,96},{1... | collective-permute-start | bytes 983048 | tf_op jit(solution)/shard_map/ppermute | solution.py:70
  5.1 5.9 %collective-permute-start.1 = (f32[1,32,2560]{2,1,0:T(8,128)S(1)}, f32[1,32,2560]{2,1,0:T(8,128)S(1)}, u32[]{:S(2)}, u32[]{:S(2)}) collective-permute-start(f32[1,32,2560]{2,1,0:T(8,128)S(1)} %get-tuple-element.34), channel_id=1, source_target_pairs={{0,16},{16,0},{32,48},{48,32},{64,80},{80,64},{96,112},{112,96},{1... | collective-permute-start | bytes 983048 | tf_op jit(solution)/shard_map/ppermute | solution.py:70
  6.5 4.6 %collective-permute-start = (f32[2,64,2560]{2,1,0:T(8,128)S(1)}, f32[2,64,2560]{2,1,0:T(8,128)S(1)}, u32[]{:S(2)}, u32[]{:S(2)}) collective-permute-start(f32[2,64,2560]{2,1,0:T(8,128)S(1)} %get-tuple-element.33), channel_id=1, source_target_pairs={{0,16},{16,0},{32,48},{48,32},{64,80},{80,64},{96,112},{112,96},{1... | collective-permute-start | bytes 3932168 | tf_op jit(solution)/shard_map/ppermute | solution.py:70
  7.0 14.6 %collective-permute-start.7 = (f32[32,2560]{1,0:T(8,128)S(1)}, f32[32,2560]{1,0:T(8,128)S(1)}, u32[]{:S(2)}, u32[]{:S(2)}) collective-permute-start(f32[32,2560]{1,0:T(8,128)S(1)} %shard_map.68.refs_0_), channel_id=1, source_target_pairs={{0,32},{16,240},{32,64},{48,16},{64,96},{80,48},{96,128},{112,80},... | collective-permute-start | bytes 983048 | tf_op jit(solution)/shard_map/ppermute | solution.py:170
  11.0 10.6 %collective-permute-start.8 = (f32[32,2560]{1,0:T(8,128)S(1)}, f32[32,2560]{1,0:T(8,128)S(1)}, u32[]{:S(2)}, u32[]{:S(2)}) collective-permute-start(f32[32,2560]{1,0:T(8,128)S(1)} %shard_map.69.refs_0_), channel_id=1, source_target_pairs={{32,0},{240,16},{64,32},{16,48},{96,64},{48,80},{128,96},{80,112},... | collective-permute-start | bytes 983048 | tf_op jit(solution)/shard_map/ppermute | solution.py:173
  12.5 12.4 %collective-permute-start.5 = (f32[32,2560]{1,0:T(8,128)S(1)}, f32[32,2560]{1,0:T(8,128)S(1)}, u32[]{:S(2)}, u32[]{:S(2)}) collective-permute-start(f32[32,2560]{1,0:T(8,128)S(1)} %get-tuple-element.36.refs_0_), channel_id=1, source_target_pairs={{0,32},{16,240},{32,64},{48,16},{64,96},{80,48},{96,128},{112,80},... | collective-permute-start | bytes 983048 | tf_op jit(solution)/shard_map/ppermute | solution.py:170
  16.7 11.7 %collective-permute-start.4 = (f32[2,64,2560]{2,1,0:T(8,128)S(1)}, f32[2,64,2560]{2,1,0:T(8,128)S(1)}, u32[]{:S(2)}, u32[]{:S(2)}) collective-permute-start(f32[2,64,2560]{2,1,0:T(8,128)S(1)} %get-tuple-element.40), channel_id=1, source_target_pairs={{0,16},{16,0},{32,48},{48,32},{64,80},{80,64},{96,112},{112,96},{1... | collective-permute-start | bytes 3932168 | tf_op jit(solution)/shard_map/ppermute | solution.py:70
  16.8 11.6 %collective-permute-start.6 = (f32[32,2560]{1,0:T(8,128)S(1)}, f32[32,2560]{1,0:T(8,128)S(1)}, u32[]{:S(2)}, u32[]{:S(2)}) collective-permute-start(f32[32,2560]{1,0:T(8,128)S(1)} %get-tuple-element.41), channel_id=1, source_target_pairs={{32,0},{240,16},{64,32},{16,48},{96,64},{48,80},{128,96},{80,112},... | collective-permute-start | bytes 983048 | tf_op jit(solution)/shard_map/ppermute | solution.py:173
  21.7 10.1 %collective-permute-start.11 = (f32[32,2560]{1,0:T(8,128)S(1)}, f32[32,2560]{1,0:T(8,128)S(1)}, u32[]{:S(2)}, u32[]{:S(2)}) collective-permute-start(f32[32,2560]{1,0:T(8,128)S(1)} %get-tuple-element.42.refs_2_), channel_id=1, source_target_pairs={{0,32},{16,240},{32,64},{48,16},{64,96},{80,48},{96,128},{112,80},... | collective-permute-start | bytes 983048 | tf_op jit(solution)/shard_map/ppermute | solution.py:170
  21.8 11.4 %collective-permute-start.12 = (f32[32,2560]{1,0:T(8,128)S(1)}, f32[32,2560]{1,0:T(8,128)S(1)}, u32[]{:S(2)}, u32[]{:S(2)}) collective-permute-start(f32[32,2560]{1,0:T(8,128)S(1)} %get-tuple-element.45), channel_id=1, source_target_pairs={{32,0},{240,16},{64,32},{16,48},{96,64},{48,80},{128,96},{80,112},... | collective-permute-start | bytes 983048 | tf_op jit(solution)/shard_map/ppermute | solution.py:173
  24.8 14.4 %collective-permute-start.3 = (f32[3,64,2560]{2,1,0:T(8,128)S(1)}, f32[3,64,2560]{2,1,0:T(8,128)S(1)}, u32[]{:S(2)}, u32[]{:S(2)}) collective-permute-start(f32[3,64,2560]{2,1,0:T(8,128)S(1)} %get-tuple-element.39), channel_id=1, source_target_pairs={{0,16},{16,0},{32,48},{48,32},{64,80},{80,64},{96,112},{112,96},{1... | collective-permute-start | bytes 5898248 | tf_op jit(solution)/shard_map/ppermute | solution.py:70
  28.5 10.7 %collective-permute-start.10 = (f32[32,2560]{1,0:T(8,128)S(1)}, f32[32,2560]{1,0:T(8,128)S(1)}, u32[]{:S(2)}, u32[]{:S(2)}) collective-permute-start(f32[32,2560]{1,0:T(8,128)S(1)} %get-tuple-element.44), channel_id=1, source_target_pairs={{32,0},{240,16},{64,32},{16,48},{96,64},{48,80},{128,96},{80,112},... | collective-permute-start | bytes 983048 | tf_op jit(solution)/shard_map/ppermute | solution.py:173
  28.6 10.6 %collective-permute-start.9 = (f32[32,2560]{1,0:T(8,128)S(1)}, f32[32,2560]{1,0:T(8,128)S(1)}, u32[]{:S(2)}, u32[]{:S(2)}) collective-permute-start(f32[32,2560]{1,0:T(8,128)S(1)} %get-tuple-element.43.refs_2_), channel_id=1, source_target_pairs={{0,32},{16,240},{32,64},{48,16},{64,96},{80,48},{96,128},{112,80},... | collective-permute-start | bytes 983048 | tf_op jit(solution)/shard_map/ppermute | solution.py:170
  33.3 12.6 %collective-permute-start.15 = (f32[32,2560]{1,0:T(8,128)S(1)}, f32[32,2560]{1,0:T(8,128)S(1)}, u32[]{:S(2)}, u32[]{:S(2)}) collective-permute-start(f32[32,2560]{1,0:T(8,128)S(1)} %get-tuple-element.46.refs_2_), channel_id=1, source_target_pairs={{0,32},{16,240},{32,64},{48,16},{64,96},{80,48},{96,128},{112,80},... | collective-permute-start | bytes 983048 | tf_op jit(solution)/shard_map/ppermute | solution.py:170
  35.7 11.0 %collective-permute-start.16 = (f32[32,2560]{1,0:T(8,128)S(1)}, f32[32,2560]{1,0:T(8,128)S(1)}, u32[]{:S(2)}, u32[]{:S(2)}) collective-permute-start(f32[32,2560]{1,0:T(8,128)S(1)} %get-tuple-element.49), channel_id=1, source_target_pairs={{32,0},{240,16},{64,32},{16,48},{96,64},{48,80},{128,96},{80,112},... | collective-permute-start | bytes 983048 | tf_op jit(solution)/shard_map/ppermute | solution.py:173
  39.3 13.7 %collective-permute-start.13 = (f32[32,2560]{1,0:T(8,128)S(1)}, f32[32,2560]{1,0:T(8,128)S(1)}, u32[]{:S(2)}, u32[]{:S(2)}) collective-permute-start(f32[32,2560]{1,0:T(8,128)S(1)} %get-tuple-element.47), channel_id=1, source_target_pairs={{32,0},{240,16},{64,32},{16,48},{96,64},{48,80},{128,96},{80,112},... | collective-permute-start | bytes 983048 | tf_op jit(solution)/shard_map/ppermute | solution.py:173
  39.6 13.5 %collective-permute-start.14 = (f32[32,2560]{1,0:T(8,128)S(1)}, f32[32,2560]{1,0:T(8,128)S(1)}, u32[]{:S(2)}, u32[]{:S(2)}) collective-permute-start(f32[32,2560]{1,0:T(8,128)S(1)} %get-tuple-element.48.refs_2_), channel_id=1, source_target_pairs={{0,32},{16,240},{32,64},{48,16},{64,96},{80,48},{96,128},{112,80},... | collective-permute-start | bytes 983048 | tf_op jit(solution)/shard_map/ppermute | solution.py:170
  46.8 13.1 %collective-permute-start.17 = (f32[32,2560]{1,0:T(8,128)S(1)}, f32[32,2560]{1,0:T(8,128)S(1)}, u32[]{:S(2)}, u32[]{:S(2)}) collective-permute-start(f32[32,2560]{1,0:T(8,128)S(1)} %get-tuple-element.50._), channel_id=1, source_target_pairs={{0,32},{16,240},{32,64},{48,16},{64,96},{80,48},{96,128},{112,80},... | collective-permute-start | bytes 983048 | tf_op jit(solution)/shard_map/ppermute | solution.py:170
  49.8 11.0 %collective-permute-start.18 = (f32[32,2560]{1,0:T(8,128)S(1)}, f32[32,2560]{1,0:T(8,128)S(1)}, u32[]{:S(2)}, u32[]{:S(2)}) collective-permute-start(f32[32,2560]{1,0:T(8,128)S(1)} %get-tuple-element.53), channel_id=1, source_target_pairs={{32,0},{240,16},{64,32},{16,48},{96,64},{48,80},{128,96},{80,112},... | collective-permute-start | bytes 983048 | tf_op jit(solution)/shard_map/ppermute | solution.py:173
  63.3 7.1 %collective-permute-start.23 = (f32[64,2560]{1,0:T(8,128)S(1)}, f32[64,2560]{1,0:T(8,128)S(1)}, u32[]{:S(2)}, u32[]{:S(2)}) collective-permute-start(f32[64,2560]{1,0:T(8,128)S(1)} %pad_maximum_fusion), channel_id=1, source_target_pairs={{0,16},{16,0},{32,48},{48,32},{64,80},{80,64},{96,112},{112,96},{1... | collective-permute-start | bytes 1966088 | tf_op jit(solution)/shard_map/ppermute | solution.py:210
  70.6 4.9 %collective-permute-start.24 = (f32[5248]{0:T(1024)S(1)}, f32[5248]{0:T(1024)S(1)}, u32[]{:S(2)}, u32[]{:S(2)}) collective-permute-start(f32[5248]{0:T(1024)S(1)} %pad_maximum_fusion.1), channel_id=1, source_target_pairs={{0,1},{1,0},{2,3},{3,2},{4,5},{5,4},{6,7},{7,6},{8,9},{9,8},{10,11... | collective-permute-start | bytes 62984 | tf_op jit(solution)/shard_map/ppermute | solution.py:153
  76.9 4.9 %collective-permute-start.27 = (f32[5248]{0:T(1024)S(1)}, f32[5248]{0:T(1024)S(1)}, u32[]{:S(2)}, u32[]{:S(2)}) collective-permute-start(f32[5248]{0:T(1024)S(1)} %add_add_fusion.1), channel_id=1, source_target_pairs={{0,1},{1,0},{2,3},{3,2},{4,5},{5,4},{6,7},{7,6},{8,9},{9,8},{10,11... | collective-permute-start | bytes 62984 | tf_op jit(solution)/shard_map/ppermute | solution.py:153
  81.8 4.2 %collective-permute-start.28 = (f32[5248]{0:T(1024)S(1)}, f32[5248]{0:T(1024)S(1)}, u32[]{:S(2)}, u32[]{:S(2)}) collective-permute-start(f32[5248]{0:T(1024)S(1)} %add.77), channel_id=1, source_target_pairs={{0,1},{1,0},{2,3},{3,2},{4,5},{5,4},{6,7},{7,6},{8,9},{9,8},{10,11... | collective-permute-start | bytes 62984 | tf_op jit(solution)/shard_map/ppermute | solution.py:153
  88.7 4.0 %collective-permute-start.31 = (f32[128]{0:T(128)S(1)}, f32[128]{0:T(128)S(1)}, u32[]{:S(2)}, u32[]{:S(2)}) collective-permute-start(f32[128]{0:T(128)S(1)} %get-tuple-element.62), channel_id=1, source_target_pairs={{0,4},{1,5},{2,6},{3,7},{4,0},{5,1},{6,2},{7,3},{8,12},{9,13},{10,... | collective-permute-start | bytes 1544 | tf_op jit(solution)/shard_map/ppermute | solution.py:153
  (15 other events, 76.2 us)

commit v5 on v4

--- a/solution.py
+++ b/solution.py
@@ -81,7 +81,7 @@
         outs[i][...] = total
 
 
-def add(blocks, terms, states=(), after=(), micros=40):
+def add(blocks, terms, states=(), after=(), micros=12):
     return pl.pallas_call(
         functools.partial(add_kernel, [(*t, bool(states)) for t in terms], len(states) + len(after)),
         out_shape=[jax.ShapeDtypeStruct((HALF, COLS), jnp.float32)] * len(terms),
@@ -153,7 +153,7 @@
     return lax.ppermute(v, ("dp", "row", "col"), pairs)
 
 
-def sum_four(v, axis, idle=None, masks=(2, 3, 1)):
+def sum_four(v, axis, idle=None, masks=(1, 3, 2)):
     unit = [0, 0, 0]
     got = []
     for mask in masks:
@@ -173,32 +173,33 @@
         return lax.ppermute(x, "dp", DOWN)
 
     far, far_up, far_down = fetch((4,), parts, split=2)
-    third = fetch((3, -3), parts, far, micros=40)
+    third = fetch((3, -3), parts, far, micros=12)
     (a,) = add((far, far_up), ((0, 0),), after=(third[0],))
     after = a
     a = up(a)
     (b,) = add((far, far_down), ((0, 1),), after=(after,))
     after = b
     b = down(b)
-    c, d = add(third, ((0, 1), (1, 0)), after=(after,))
-    second = fetch((2, -2), parts, c)
+    (c,) = add(third, ((0, 1),), after=(after,))
+    (d,) = add(third, ((1, 0),), after=(c,))
+    after = d
+    second = fetch((2, -2), parts, after)
     near = fetch((1, -1, 0), parts, second[0])
+    after = near[0]
     c, d = up(c), down(d)
-    a, b = add(third, ((0, 0), (1, 1)), (a, b), after=(near[0],))
-    after = a
-    a, b = up(a), down(b)
-    c, d = add(second, ((0, 1), (1, 0)), (c, d), after=(after,))
-    after = c
-    c, d = up(c), down(d)
-    a, b = add(second, ((0, 0), (1, 1)), (a, b), after=(after,))
-    after = a
-    a, b = up(a), down(b)
-    c, d = add(near, ((0, 1), (1, 0)), (c, d), after=(after,))
-    after = c
-    c, d = up(c), down(d)
-    a, b = add(near, ((0, 0), (1, 1)), (a, b), after=(after,))
-    after = a
-    a, b = up(a), down(b)
+    steps = [
+        (third, (0, 0), (1, 1)),
+        (second, (0, 1), (1, 0)),
+        (second, (0, 0), (1, 1)),
+        (near, (0, 1), (1, 0)),
+        (near, (0, 0), (1, 1)),
+    ]
+    for blocks, first, last in steps:
+        (x,) = add(blocks, (first,), (a,), after=(after,))
+        (y,) = add(blocks, (last,), (b,), after=(x,))
+        after = y
+        a, b, c, d = c, d, up(x), down(y)
+    a, b, c, d = c, d, a, b
     row_old = hold(row_old, after)
     upper, lower = add(near, ((2, 0), (2, 1)), (d, c), after=(row_old,))
     grad = jnp.concatenate([upper + a, lower + b], axis=0)
@@ -219,7 +220,7 @@
         packed.append(sums)
     packed = jnp.concatenate([*packed, row_new])
 
-    packed = sum_four(packed, 0, (0, 0, 1), (6, 7, 1))
+    packed = sum_four(packed, 0, (0, 0, 1), (1, 7, 6))
     packed = packed + exchange(packed, (2, 0, 0), (0, 0, 1))
     packed = sum_four(packed, 1, (0, 0, 1))
     col_new = 0.8 * col_old + 0.2 * packed[:COLS] / D

time: 97 us -> 97 us (level)
  starting transfers between devices: 44.4 us -> 49.2 us
  waiting for transfers between devices: 42.5 us -> 37.7 us
    ppermute x7, starting transfers between devices: 18.1 us -> 24.4 us  [up(): return lax.ppermute(x, 'dp', UP)]
    ppermute x7, waiting for transfers between devices: 18 us -> 11.8 us  [down(): return lax.ppermute(x, 'dp', DOWN)]
    ppermute x7, starting transfers between devices: 1.97 us -> 0.59 us  [down(): return lax.ppermute(x, 'dp', DOWN)]
    ppermute x1, starting transfers between devices: 1.31 us -> 0.02 us  [on_device(): row_other = lax.ppermute(row_own, 'dp', SWAP)]
    ppermute x5, starting transfers between devices: 4.02 us -> 5.03 us  [fetch(): return (own, *(lax.ppermute(x, 'dp', SWAP) for x in sent))]
  transfers between devices with their start and end apart: 35 -> 35, of which waited for: 22 -> 22; matrix products, arithmetic and copies ran while one was open for 1% -> 0% of each run, Pallas kernels for 5% -> 5%
where the time goes in v5:
time: 97 us; the launch traced here: 96.8 us
  starting transfers between devices  49.2 us (51%)
  waiting for transfers between devices  37.7 us (39%)
  Pallas kernels  7.5 us (8%)
  between operations  1.15 us (1%)
  other arithmetic  1.13 us (1%)
    ppermute x7, starting transfers between devices, up(): return lax.ppermute(x, 'dp', UP)  24.4 us
    ppermute x13, starting transfers between devices, exchange(): return lax.ppermute(v, ('dp', 'row', 'col'), pairs)  18.9 us
    ppermute x7, waiting for transfers between devices, up(): return lax.ppermute(x, 'dp', UP)  12.7 us
    ppermute x7, waiting for transfers between devices, down(): return lax.ppermute(x, 'dp', DOWN)  11.8 us
    ppermute x13, waiting for transfers between devices, exchange(): return lax.ppermute(v, ('dp', 'row', 'col'), pairs)  10.9 us
    pallas_call x4, Pallas kernels, fetch(): pl.pallas_call(functools.partial(fetch_kernel, ks, split, len(after)), ou...  5.24 us
    ppermute x5, starting transfers between devices, fetch(): return (own, *(lax.ppermute(x, 'dp', SWAP) for x in sent))  5.03 us
  transfers between devices with their start and end apart: 35, of which 22 were waited for; matrix products, arithmetic and copies ran while one was open for 0% of the time, Pallas kernels for 5%

profile of v5, /device:TPU:1, one launch (start us, length us, event | category | flops | bytes accessed | tf_op | source)
XLA Modules:
  0.0 96.8 jit_solution(7358078186225921364)
XLA Ops:
  1.7 3.3 %collective-permute-start.1 = (f32[1,32,2560]{2,1,0:T(8,128)S(1)}, f32[1,32,2560]{2,1,0:T(8,128)S(1)}, u32[]{:S(2)}, u32[]{:S(2)}) collective-permute-start(f32[1,32,2560]{2,1,0:T(8,128)S(1)} %get-tuple-element.22), channel_id=1, source_target_pairs={{0,16},{16,0},{32,48},{48,32},{64,80},{80,64},{96,112},{112,96},{1... | collective-permute-start | bytes 983048 | tf_op jit(solution)/shard_map/ppermute | solution.py:70
  7.0 3.9 %collective-permute-start.8 = (f32[32,2560]{1,0:T(8,128)S(1)}, f32[32,2560]{1,0:T(8,128)S(1)}, u32[]{:S(2)}, u32[]{:S(2)}) collective-permute-start(f32[32,2560]{1,0:T(8,128)S(1)} %shard_map.68.refs_0_), channel_id=1, source_target_pairs={{0,32},{16,240},{32,64},{48,16},{64,96},{80,48},{96,128},{112,80},... | collective-permute-start | bytes 983048 | tf_op jit(solution)/shard_map/ppermute | solution.py:170
  11.1 2.7 %collective-permute-start.6 = (f32[32,2560]{1,0:T(8,128)S(1)}, f32[32,2560]{1,0:T(8,128)S(1)}, u32[]{:S(2)}, u32[]{:S(2)}) collective-permute-start(f32[32,2560]{1,0:T(8,128)S(1)} %shard_map.70.refs_0_), channel_id=1, source_target_pairs={{0,32},{16,240},{32,64},{48,16},{64,96},{80,48},{96,128},{112,80},... | collective-permute-start | bytes 983048 | tf_op jit(solution)/shard_map/ppermute | solution.py:170
  18.0 3.3 %collective-permute-start.12 = (f32[32,2560]{1,0:T(8,128)S(1)}, f32[32,2560]{1,0:T(8,128)S(1)}, u32[]{:S(2)}, u32[]{:S(2)}) collective-permute-start(f32[32,2560]{1,0:T(8,128)S(1)} %shard_map.74.refs_1_), channel_id=1, source_target_pairs={{0,32},{16,240},{32,64},{48,16},{64,96},{80,48},{96,128},{112,80},... | collective-permute-start | bytes 983048 | tf_op jit(solution)/shard_map/ppermute | solution.py:170
  22.2 2.5 %collective-permute-done.6.refs_0_ = f32[32,2560]{1,0:T(8,128)S(1)} collective-permute-done((f32[32,2560]{1,0:T(8,128)S(1)}, f32[32,2560]{1,0:T(8,128)S(1)}, u32[]{:S(2)}, u32[]{:S(2)}) %collective-permute-start.6) | collective-permute-done | bytes 327712 | tf_op jit(solution)/shard_map/ppermute | solution.py:170
  24.8 3.9 %collective-permute-start.10 = (f32[32,2560]{1,0:T(8,128)S(1)}, f32[32,2560]{1,0:T(8,128)S(1)}, u32[]{:S(2)}, u32[]{:S(2)}) collective-permute-start(f32[32,2560]{1,0:T(8,128)S(1)} %shard_map.76.refs_1_), channel_id=1, source_target_pairs={{0,32},{16,240},{32,64},{48,16},{64,96},{80,48},{96,128},{112,80},... | collective-permute-start | bytes 983048 | tf_op jit(solution)/shard_map/ppermute | solution.py:170
  29.2 2.5 %collective-permute-done.12.refs_0_ = f32[32,2560]{1,0:T(8,128)S(1)} collective-permute-done((f32[32,2560]{1,0:T(8,128)S(1)}, f32[32,2560]{1,0:T(8,128)S(1)}, u32[]{:S(2)}, u32[]{:S(2)}) %collective-permute-start.12) | collective-permute-done | bytes 327712 | tf_op jit(solution)/shard_map/ppermute | solution.py:170
  31.8 3.5 %collective-permute-start.16 = (f32[32,2560]{1,0:T(8,128)S(1)}, f32[32,2560]{1,0:T(8,128)S(1)}, u32[]{:S(2)}, u32[]{:S(2)}) collective-permute-start(f32[32,2560]{1,0:T(8,128)S(1)} %shard_map.78.refs_1_), channel_id=1, source_target_pairs={{0,32},{16,240},{32,64},{48,16},{64,96},{80,48},{96,128},{112,80},... | collective-permute-start | bytes 983048 | tf_op jit(solution)/shard_map/ppermute | solution.py:170
  36.2 2.5 %collective-permute-done.10.refs_0_ = f32[32,2560]{1,0:T(8,128)S(1)} collective-permute-done((f32[32,2560]{1,0:T(8,128)S(1)}, f32[32,2560]{1,0:T(8,128)S(1)}, u32[]{:S(2)}, u32[]{:S(2)}) %collective-permute-start.10) | collective-permute-done | bytes 327712 | tf_op jit(solution)/shard_map/ppermute | solution.py:170
  38.8 3.7 %collective-permute-start.14 = (f32[32,2560]{1,0:T(8,128)S(1)}, f32[32,2560]{1,0:T(8,128)S(1)}, u32[]{:S(2)}, u32[]{:S(2)}) collective-permute-start(f32[32,2560]{1,0:T(8,128)S(1)} %shard_map.80.refs_1_), channel_id=1, source_target_pairs={{0,32},{16,240},{32,64},{48,16},{64,96},{80,48},{96,128},{112,80},... | collective-permute-start | bytes 983048 | tf_op jit(solution)/shard_map/ppermute | solution.py:170
  43.3 2.5 %collective-permute-done.16.refs_0_ = f32[32,2560]{1,0:T(8,128)S(1)} collective-permute-done((f32[32,2560]{1,0:T(8,128)S(1)}, f32[32,2560]{1,0:T(8,128)S(1)}, u32[]{:S(2)}, u32[]{:S(2)}) %collective-permute-start.16) | collective-permute-done | bytes 327712 | tf_op jit(solution)/shard_map/ppermute | solution.py:170
  45.9 3.5 %collective-permute-start.17 = (f32[32,2560]{1,0:T(8,128)S(1)}, f32[32,2560]{1,0:T(8,128)S(1)}, u32[]{:S(2)}, u32[]{:S(2)}) collective-permute-start(f32[32,2560]{1,0:T(8,128)S(1)} %shard_map.82.refs_1_), channel_id=1, source_target_pairs={{0,32},{16,240},{32,64},{48,16},{64,96},{80,48},{96,128},{112,80},... | collective-permute-start | bytes 983048 | tf_op jit(solution)/shard_map/ppermute | solution.py:170
  50.3 6.9 %collective-permute-done.13.refs_0_ = f32[32,2560]{1,0:T(8,128)S(1)} collective-permute-done((f32[32,2560]{1,0:T(8,128)S(1)}, f32[32,2560]{1,0:T(8,128)S(1)}, u32[]{:S(2)}, u32[]{:S(2)}) %collective-permute-start.13) | collective-permute-done | bytes 327712 | tf_op jit(solution)/shard_map/ppermute | solution.py:173
  57.3 2.6 %collective-permute-done.17 = f32[32,2560]{1,0:T(8,128)S(1)} collective-permute-done((f32[32,2560]{1,0:T(8,128)S(1)}, f32[32,2560]{1,0:T(8,128)S(1)}, u32[]{:S(2)}, u32[]{:S(2)}) %collective-permute-start.17) | collective-permute-done | bytes 327712 | tf_op jit(solution)/shard_map/ppermute | solution.py:170
  59.9 1.5 %collective-permute-done.18 = f32[32,2560]{1,0:T(8,128)S(1)} collective-permute-done((f32[32,2560]{1,0:T(8,128)S(1)}, f32[32,2560]{1,0:T(8,128)S(1)}, u32[]{:S(2)}, u32[]{:S(2)}) %collective-permute-start.18) | collective-permute-done | bytes 327712 | tf_op jit(solution)/shard_map/ppermute | solution.py:173
  63.3 2.8 %collective-permute-start.22 = (f32[128]{0:T(128)S(1)}, f32[128]{0:T(128)S(1)}, u32[]{:S(2)}, u32[]{:S(2)}) collective-permute-start(f32[128]{0:T(128)S(1)} %pad_maximum_fusion.4), channel_id=1, source_target_pairs={{0,4},{1,5},{2,6},{3,7},{4,0},{5,1},{6,2},{7,3},{8,12},{9,13},{10,... | collective-permute-start | bytes 1544 | tf_op jit(solution)/shard_map/ppermute | solution.py:153
  67.2 2.5 %collective-permute-done.21 = f32[128]{0:T(128)S(1)} collective-permute-done((f32[128]{0:T(128)S(1)}, f32[128]{0:T(128)S(1)}, u32[]{:S(2)}, u32[]{:S(2)}) %collective-permute-start.21) | collective-permute-done | bytes 544 | tf_op jit(solution)/shard_map/ppermute | solution.py:153
  70.1 2.6 %collective-permute-start.26 = (f32[5248]{0:T(1024)S(1)}, f32[5248]{0:T(1024)S(1)}, u32[]{:S(2)}, u32[]{:S(2)}) collective-permute-start(f32[5248]{0:T(1024)S(1)} %pad_maximum_fusion.1), channel_id=1, source_target_pairs={{0,1},{1,0},{2,3},{3,2},{4,5},{5,4},{6,7},{7,6},{8,9},{9,8},{10,11... | collective-permute-start | bytes 62984 | tf_op jit(solution)/shard_map/ppermute | solution.py:153
  73.1 1.9 %collective-permute-start.24 = (f32[5248]{0:T(1024)S(1)}, f32[5248]{0:T(1024)S(1)}, u32[]{:S(2)}, u32[]{:S(2)}) collective-permute-start(f32[5248]{0:T(1024)S(1)} %pad_maximum_fusion.1), channel_id=1, source_target_pairs={{0,1},{1,0},{2,3},{3,2},{4,5},{5,4},{6,7},{7,6},{8,9},{9,8},{10,11... | collective-permute-start | bytes 62984 | tf_op jit(solution)/shard_map/ppermute | solution.py:153
  75.0 1.6 %collective-permute-done.25 = f32[5248]{0:T(1024)S(1)} collective-permute-done((f32[5248]{0:T(1024)S(1)}, f32[5248]{0:T(1024)S(1)}, u32[]{:S(2)}, u32[]{:S(2)}) %collective-permute-start.25) | collective-permute-done | bytes 21024 | tf_op jit(solution)/shard_map/ppermute | solution.py:153
  76.6 4.0 %collective-permute-start.27 = (f32[5248]{0:T(1024)S(1)}, f32[5248]{0:T(1024)S(1)}, u32[]{:S(2)}, u32[]{:S(2)}) collective-permute-start(f32[5248]{0:T(1024)S(1)} %add_add_fusion.1), channel_id=1, source_target_pairs={{0,1},{1,0},{2,3},{3,2},{4,5},{5,4},{6,7},{7,6},{8,9},{9,8},{10,11... | collective-permute-start | bytes 62984 | tf_op jit(solution)/shard_map/ppermute | solution.py:153
  81.8 2.9 %collective-permute-start.30 = (f32[5248]{0:T(1024)S(1)}, f32[5248]{0:T(1024)S(1)}, u32[]{:S(2)}, u32[]{:S(2)}) collective-permute-start(f32[5248]{0:T(1024)S(1)} %add.77), channel_id=1, source_target_pairs={{0,1},{1,0},{2,3},{3,2},{4,5},{5,4},{6,7},{7,6},{8,9},{9,8},{10,11... | collective-permute-start | bytes 62984 | tf_op jit(solution)/shard_map/ppermute | solution.py:153
  86.0 2.6 %collective-permute-done.29 = f32[5248]{0:T(1024)S(1)} collective-permute-done((f32[5248]{0:T(1024)S(1)}, f32[5248]{0:T(1024)S(1)}, u32[]{:S(2)}, u32[]{:S(2)}) %collective-permute-start.29) | collective-permute-done | bytes 21024 | tf_op jit(solution)/shard_map/ppermute | solution.py:153
  95.1 1.5 %shard_map.86 = (f32[64,2560]{1,0:T(8,128)}, f32[1,1]{1,0:T(1,128)}) custom-call(f32[64,2560]{1,0:T(8,128)S(1)} %rsqrt_multiply_fusion.scaled, f32[1,128]{1,0:T(1,128)S(1)} %get-tuple-element.43.row_sum, f32[1,128]{1,0:T(1,128)S(1)} %get-tuple-element.42.total), custom_call_target="tpu_custom_call" | custom-call | flops 1150000000 | tf_op jit(solution)/shard_map/pallas_call | solution.py:126
  (100 shorter events, 24.5 us)
Async XLA Ops:
  1.7 9.2 %collective-permute-start.1 = (f32[1,32,2560]{2,1,0:T(8,128)S(1)}, f32[1,32,2560]{2,1,0:T(8,128)S(1)}, u32[]{:S(2)}, u32[]{:S(2)}) collective-permute-start(f32[1,32,2560]{2,1,0:T(8,128)S(1)} %get-tuple-element.22), channel_id=1, source_target_pairs={{0,16},{16,0},{32,48},{48,32},{64,80},{80,64},{96,112},{112,96},{1... | collective-permute-start | bytes 983048 | tf_op jit(solution)/shard_map/ppermute | solution.py:70
  6.5 4.6 %collective-permute-start = (f32[2,64,2560]{2,1,0:T(8,128)S(1)}, f32[2,64,2560]{2,1,0:T(8,128)S(1)}, u32[]{:S(2)}, u32[]{:S(2)}) collective-permute-start(f32[2,64,2560]{2,1,0:T(8,128)S(1)} %get-tuple-element.21), channel_id=1, source_target_pairs={{0,16},{16,0},{32,48},{48,32},{64,80},{80,64},{96,112},{112,96},{1... | collective-permute-start | bytes 3932168 | tf_op jit(solution)/shard_map/ppermute | solution.py:70
  7.0 10.9 %collective-permute-start.8 = (f32[32,2560]{1,0:T(8,128)S(1)}, f32[32,2560]{1,0:T(8,128)S(1)}, u32[]{:S(2)}, u32[]{:S(2)}) collective-permute-start(f32[32,2560]{1,0:T(8,128)S(1)} %shard_map.68.refs_0_), channel_id=1, source_target_pairs={{0,32},{16,240},{32,64},{48,16},{64,96},{80,48},{96,128},{112,80},... | collective-permute-start | bytes 983048 | tf_op jit(solution)/shard_map/ppermute | solution.py:170
  11.0 11.1 %collective-permute-start.7 = (f32[32,2560]{1,0:T(8,128)S(1)}, f32[32,2560]{1,0:T(8,128)S(1)}, u32[]{:S(2)}, u32[]{:S(2)}) collective-permute-start(f32[32,2560]{1,0:T(8,128)S(1)} %shard_map.69.refs_0_), channel_id=1, source_target_pairs={{32,0},{240,16},{64,32},{16,48},{96,64},{48,80},{128,96},{80,112},... | collective-permute-start | bytes 983048 | tf_op jit(solution)/shard_map/ppermute | solution.py:173
  11.1 13.6 %collective-permute-start.6 = (f32[32,2560]{1,0:T(8,128)S(1)}, f32[32,2560]{1,0:T(8,128)S(1)}, u32[]{:S(2)}, u32[]{:S(2)}) collective-permute-start(f32[32,2560]{1,0:T(8,128)S(1)} %shard_map.70.refs_0_), channel_id=1, source_target_pairs={{0,32},{16,240},{32,64},{48,16},{64,96},{80,48},{96,128},{112,80},... | collective-permute-start | bytes 983048 | tf_op jit(solution)/shard_map/ppermute | solution.py:170
  13.9 15.2 %collective-permute-start.5 = (f32[32,2560]{1,0:T(8,128)S(1)}, f32[32,2560]{1,0:T(8,128)S(1)}, u32[]{:S(2)}, u32[]{:S(2)}) collective-permute-start(f32[32,2560]{1,0:T(8,128)S(1)} %shard_map.71.refs_0_), channel_id=1, source_target_pairs={{32,0},{240,16},{64,32},{16,48},{96,64},{48,80},{128,96},{80,112},... | collective-permute-start | bytes 983048 | tf_op jit(solution)/shard_map/ppermute | solution.py:173
  15.3 9.4 %collective-permute-start.4 = (f32[2,64,2560]{2,1,0:T(8,128)S(1)}, f32[2,64,2560]{2,1,0:T(8,128)S(1)}, u32[]{:S(2)}, u32[]{:S(2)}) collective-permute-start(f32[2,64,2560]{2,1,0:T(8,128)S(1)} %get-tuple-element.27), channel_id=1, source_target_pairs={{0,16},{16,0},{32,48},{48,32},{64,80},{80,64},{96,112},{112,96},{1... | collective-permute-start | bytes 3932168 | tf_op jit(solution)/shard_map/ppermute | solution.py:70
  18.0 13.8 %collective-permute-start.12 = (f32[32,2560]{1,0:T(8,128)S(1)}, f32[32,2560]{1,0:T(8,128)S(1)}, u32[]{:S(2)}, u32[]{:S(2)}) collective-permute-start(f32[32,2560]{1,0:T(8,128)S(1)} %shard_map.74.refs_1_), channel_id=1, source_target_pairs={{0,32},{16,240},{32,64},{48,16},{64,96},{80,48},{96,128},{112,80},... | collective-permute-start | bytes 983048 | tf_op jit(solution)/shard_map/ppermute | solution.py:170
  22.1 14.0 %collective-permute-start.11 = (f32[32,2560]{1,0:T(8,128)S(1)}, f32[32,2560]{1,0:T(8,128)S(1)}, u32[]{:S(2)}, u32[]{:S(2)}) collective-permute-start(f32[32,2560]{1,0:T(8,128)S(1)} %shard_map.75.refs_1_), channel_id=1, source_target_pairs={{32,0},{240,16},{64,32},{16,48},{96,64},{48,80},{128,96},{80,112},... | collective-permute-start | bytes 983048 | tf_op jit(solution)/shard_map/ppermute | solution.py:173
  24.7 14.0 %collective-permute-start.3 = (f32[3,64,2560]{2,1,0:T(8,128)S(1)}, f32[3,64,2560]{2,1,0:T(8,128)S(1)}, u32[]{:S(2)}, u32[]{:S(2)}) collective-permute-start(f32[3,64,2560]{2,1,0:T(8,128)S(1)} %get-tuple-element.26), channel_id=1, source_target_pairs={{0,16},{16,0},{32,48},{48,32},{64,80},{80,64},{96,112},{112,96},{1... | collective-permute-start | bytes 5898248 | tf_op jit(solution)/shard_map/ppermute | solution.py:70
  24.8 14.0 %collective-permute-start.10 = (f32[32,2560]{1,0:T(8,128)S(1)}, f32[32,2560]{1,0:T(8,128)S(1)}, u32[]{:S(2)}, u32[]{:S(2)}) collective-permute-start(f32[32,2560]{1,0:T(8,128)S(1)} %shard_map.76.refs_1_), channel_id=1, source_target_pairs={{0,32},{16,240},{32,64},{48,16},{64,96},{80,48},{96,128},{112,80},... | collective-permute-start | bytes 983048 | tf_op jit(solution)/shard_map/ppermute | solution.py:170
  29.1 14.0 %collective-permute-start.9 = (f32[32,2560]{1,0:T(8,128)S(1)}, f32[32,2560]{1,0:T(8,128)S(1)}, u32[]{:S(2)}, u32[]{:S(2)}) collective-permute-start(f32[32,2560]{1,0:T(8,128)S(1)} %shard_map.77.refs_1_), channel_id=1, source_target_pairs={{32,0},{240,16},{64,32},{16,48},{96,64},{48,80},{128,96},{80,112},... | collective-permute-start | bytes 983048 | tf_op jit(solution)/shard_map/ppermute | solution.py:173
  31.8 14.0 %collective-permute-start.16 = (f32[32,2560]{1,0:T(8,128)S(1)}, f32[32,2560]{1,0:T(8,128)S(1)}, u32[]{:S(2)}, u32[]{:S(2)}) collective-permute-start(f32[32,2560]{1,0:T(8,128)S(1)} %shard_map.78.refs_1_), channel_id=1, source_target_pairs={{0,32},{16,240},{32,64},{48,16},{64,96},{80,48},{96,128},{112,80},... | collective-permute-start | bytes 983048 | tf_op jit(solution)/shard_map/ppermute | solution.py:170
  36.1 14.0 %collective-permute-start.15 = (f32[32,2560]{1,0:T(8,128)S(1)}, f32[32,2560]{1,0:T(8,128)S(1)}, u32[]{:S(2)}, u32[]{:S(2)}) collective-permute-start(f32[32,2560]{1,0:T(8,128)S(1)} %shard_map.79.refs_1_), channel_id=1, source_target_pairs={{32,0},{240,16},{64,32},{16,48},{96,64},{48,80},{128,96},{80,112},... | collective-permute-start | bytes 983048 | tf_op jit(solution)/shard_map/ppermute | solution.py:173
  38.8 18.3 %collective-permute-start.14 = (f32[32,2560]{1,0:T(8,128)S(1)}, f32[32,2560]{1,0:T(8,128)S(1)}, u32[]{:S(2)}, u32[]{:S(2)}) collective-permute-start(f32[32,2560]{1,0:T(8,128)S(1)} %shard_map.80.refs_1_), channel_id=1, source_target_pairs={{0,32},{16,240},{32,64},{48,16},{64,96},{80,48},{96,128},{112,80},... | collective-permute-start | bytes 983048 | tf_op jit(solution)/shard_map/ppermute | solution.py:170
  43.2 14.0 %collective-permute-start.13 = (f32[32,2560]{1,0:T(8,128)S(1)}, f32[32,2560]{1,0:T(8,128)S(1)}, u32[]{:S(2)}, u32[]{:S(2)}) collective-permute-start(f32[32,2560]{1,0:T(8,128)S(1)} %shard_map.81.refs_1_), channel_id=1, source_target_pairs={{32,0},{240,16},{64,32},{16,48},{96,64},{48,80},{128,96},{80,112},... | collective-permute-start | bytes 983048 | tf_op jit(solution)/shard_map/ppermute | solution.py:173
  45.9 14.0 %collective-permute-start.17 = (f32[32,2560]{1,0:T(8,128)S(1)}, f32[32,2560]{1,0:T(8,128)S(1)}, u32[]{:S(2)}, u32[]{:S(2)}) collective-permute-start(f32[32,2560]{1,0:T(8,128)S(1)} %shard_map.82.refs_1_), channel_id=1, source_target_pairs={{0,32},{16,240},{32,64},{48,16},{64,96},{80,48},{96,128},{112,80},... | collective-permute-start | bytes 983048 | tf_op jit(solution)/shard_map/ppermute | solution.py:170
  50.2 11.2 %collective-permute-start.18 = (f32[32,2560]{1,0:T(8,128)S(1)}, f32[32,2560]{1,0:T(8,128)S(1)}, u32[]{:S(2)}, u32[]{:S(2)}) collective-permute-start(f32[32,2560]{1,0:T(8,128)S(1)} %shard_map.83._), channel_id=1, source_target_pairs={{32,0},{240,16},{64,32},{16,48},{96,64},{48,80},{128,96},{80,112},... | collective-permute-start | bytes 983048 | tf_op jit(solution)/shard_map/ppermute | solution.py:173
  63.0 7.0 %collective-permute-start.23 = (f32[64,2560]{1,0:T(8,128)S(1)}, f32[64,2560]{1,0:T(8,128)S(1)}, u32[]{:S(2)}, u32[]{:S(2)}) collective-permute-start(f32[64,2560]{1,0:T(8,128)S(1)} %pad_maximum_fusion), channel_id=1, source_target_pairs={{0,16},{16,0},{32,48},{48,32},{64,80},{80,64},{96,112},{112,96},{1... | collective-permute-start | bytes 1966088 | tf_op jit(solution)/shard_map/ppermute | solution.py:211
  63.3 3.9 %collective-permute-start.22 = (f32[128]{0:T(128)S(1)}, f32[128]{0:T(128)S(1)}, u32[]{:S(2)}, u32[]{:S(2)}) collective-permute-start(f32[128]{0:T(128)S(1)} %pad_maximum_fusion.4), channel_id=1, source_target_pairs={{0,4},{1,5},{2,6},{3,7},{4,0},{5,1},{6,2},{7,3},{8,12},{9,13},{10,... | collective-permute-start | bytes 1544 | tf_op jit(solution)/shard_map/ppermute | solution.py:153
  70.1 4.9 %collective-permute-start.26 = (f32[5248]{0:T(1024)S(1)}, f32[5248]{0:T(1024)S(1)}, u32[]{:S(2)}, u32[]{:S(2)}) collective-permute-start(f32[5248]{0:T(1024)S(1)} %pad_maximum_fusion.1), channel_id=1, source_target_pairs={{0,1},{1,0},{2,3},{3,2},{4,5},{5,4},{6,7},{7,6},{8,9},{9,8},{10,11... | collective-permute-start | bytes 62984 | tf_op jit(solution)/shard_map/ppermute | solution.py:153
  76.6 5.2 %collective-permute-start.27 = (f32[5248]{0:T(1024)S(1)}, f32[5248]{0:T(1024)S(1)}, u32[]{:S(2)}, u32[]{:S(2)}) collective-permute-start(f32[5248]{0:T(1024)S(1)} %add_add_fusion.1), channel_id=1, source_target_pairs={{0,1},{1,0},{2,3},{3,2},{4,5},{5,4},{6,7},{7,6},{8,9},{9,8},{10,11... | collective-permute-start | bytes 62984 | tf_op jit(solution)/shard_map/ppermute | solution.py:153
  81.8 4.2 %collective-permute-start.30 = (f32[5248]{0:T(1024)S(1)}, f32[5248]{0:T(1024)S(1)}, u32[]{:S(2)}, u32[]{:S(2)}) collective-permute-start(f32[5248]{0:T(1024)S(1)} %add.77), channel_id=1, source_target_pairs={{0,1},{1,0},{2,3},{3,2},{4,5},{5,4},{6,7},{7,6},{8,9},{9,8},{10,11... | collective-permute-start | bytes 62984 | tf_op jit(solution)/shard_map/ppermute | solution.py:153
  88.7 4.0 %collective-permute-start.33 = (f32[128]{0:T(128)S(1)}, f32[128]{0:T(128)S(1)}, u32[]{:S(2)}, u32[]{:S(2)}) collective-permute-start(f32[128]{0:T(128)S(1)} %get-tuple-element.38), channel_id=1, source_target_pairs={{0,4},{1,5},{2,6},{3,7},{4,0},{5,1},{6,2},{7,3},{8,12},{9,13},{10,... | collective-permute-start | bytes 1544 | tf_op jit(solution)/shard_map/ppermute | solution.py:153
  (15 other events, 66.6 us)

commit v6 on v5

--- a/solution.py
+++ b/solution.py
@@ -220,8 +220,8 @@
         packed.append(sums)
     packed = jnp.concatenate([*packed, row_new])
 
-    packed = sum_four(packed, 0, (0, 0, 1), (1, 7, 6))
-    packed = packed + exchange(packed, (2, 0, 0), (0, 0, 1))
+    packed = sum_four(packed, 0, (0, 0, 1))
+    packed = packed + exchange(packed, (7, 0, 0), (0, 0, 1))
     packed = sum_four(packed, 1, (0, 0, 1))
     col_new = 0.8 * col_old + 0.2 * packed[:COLS] / D
     total = jnp.sum((packed[COLS:2 * COLS] / col_new).reshape(20, 128), axis=0)

time: 97 us -> 94.6 us (0.975)
  starting transfers between devices: 49.2 us -> 46.1 us
    ppermute x13, starting transfers between devices: 18.9 us -> 15.7 us  [exchange(): return lax.ppermute(v, ('dp', 'row', 'col'), pairs)]
  transfers between devices with their start and end apart: 35 -> 35, of which waited for: 22 -> 24; matrix products, arithmetic and copies ran while one was open for 0% -> 0% of each run, Pallas kernels for 5% -> 5%
where the time goes in v6:
time: 94.6 us; the launch traced here: 94.4 us
  starting transfers between devices  46.1 us (49%)
  waiting for transfers between devices  38.4 us (41%)
  Pallas kernels  7.5 us (8%)
  between operations  1.15 us (1%)
  other arithmetic  1.13 us (1%)
    ppermute x7, starting transfers between devices, up(): return lax.ppermute(x, 'dp', UP)  24.4 us
    ppermute x13, starting transfers between devices, exchange(): return lax.ppermute(v, ('dp', 'row', 'col'), pairs)  15.7 us
    ppermute x7, waiting for transfers between devices, up(): return lax.ppermute(x, 'dp', UP)  12.7 us
    ppermute x7, waiting for transfers between devices, down(): return lax.ppermute(x, 'dp', DOWN)  11.8 us
    ppermute x13, waiting for transfers between devices, exchange(): return lax.ppermute(v, ('dp', 'row', 'col'), pairs)  11.5 us
    pallas_call x4, Pallas kernels, fetch(): pl.pallas_call(functools.partial(fetch_kernel, ks, split, len(after)), ou...  5.24 us
    ppermute x5, starting transfers between devices, fetch(): return (own, *(lax.ppermute(x, 'dp', SWAP) for x in sent))  5.03 us
  transfers between devices with their start and end apart: 35, of which 24 were waited for; matrix products, arithmetic and copies ran while one was open for 0% of the time, Pallas kernels for 5%

profile of v6, /device:TPU:1, one launch (start us, length us, event | category | flops | bytes accessed | tf_op | source)
XLA Modules:
  0.0 94.4 jit_solution(5907139719133096780)
XLA Ops:
  1.7 3.3 %collective-permute-start.1 = (f32[1,32,2560]{2,1,0:T(8,128)S(1)}, f32[1,32,2560]{2,1,0:T(8,128)S(1)}, u32[]{:S(2)}, u32[]{:S(2)}) collective-permute-start(f32[1,32,2560]{2,1,0:T(8,128)S(1)} %get-tuple-element.22), channel_id=1, source_target_pairs={{0,16},{16,0},{32,48},{48,32},{64,80},{80,64},{96,112},{112,96},{1... | collective-permute-start | bytes 983048 | tf_op jit(solution)/shard_map/ppermute | solution.py:70
  7.0 3.9 %collective-permute-start.8 = (f32[32,2560]{1,0:T(8,128)S(1)}, f32[32,2560]{1,0:T(8,128)S(1)}, u32[]{:S(2)}, u32[]{:S(2)}) collective-permute-start(f32[32,2560]{1,0:T(8,128)S(1)} %shard_map.68.refs_0_), channel_id=1, source_target_pairs={{0,32},{16,240},{32,64},{48,16},{64,96},{80,48},{96,128},{112,80},... | collective-permute-start | bytes 983048 | tf_op jit(solution)/shard_map/ppermute | solution.py:170
  11.1 2.7 %collective-permute-start.6 = (f32[32,2560]{1,0:T(8,128)S(1)}, f32[32,2560]{1,0:T(8,128)S(1)}, u32[]{:S(2)}, u32[]{:S(2)}) collective-permute-start(f32[32,2560]{1,0:T(8,128)S(1)} %shard_map.70.refs_0_), channel_id=1, source_target_pairs={{0,32},{16,240},{32,64},{48,16},{64,96},{80,48},{96,128},{112,80},... | collective-permute-start | bytes 983048 | tf_op jit(solution)/shard_map/ppermute | solution.py:170
  14.0 1.3 %shard_map.72 = (bf16[2,64,2560]{2,1,0:T(8,128)(2,1)S(1)}, f32[2,64,2560]{2,1,0:T(8,128)S(1)}) custom-call(bf16[16,64,2560]{2,1,0:T(8,128)(2,1)} %bitcast.18, f32[32,2560]{1,0:T(8,128)S(1)} %shard_map.71.refs_0_), custom_call_target="tpu_custom_call" | custom-call | tf_op jit(solution)/shard_map/pallas_call | solution.py:56
  16.4 1.5 %shard_map.73 = (bf16[3,64,2560]{2,1,0:T(8,128)(2,1)S(1)}, f32[3,64,2560]{2,1,0:T(8,128)S(1)}) custom-call(bf16[16,64,2560]{2,1,0:T(8,128)(2,1)} %bitcast.19, bf16[2,64,2560]{2,1,0:T(8,128)(2,1)S(1)} %get-tuple-element.24.refs_0_.own), custom_call_target="tpu_custom_call" | custom-call | tf_op jit(solution)/shard_map/pallas_call | solution.py:56
  18.0 3.3 %collective-permute-start.12 = (f32[32,2560]{1,0:T(8,128)S(1)}, f32[32,2560]{1,0:T(8,128)S(1)}, u32[]{:S(2)}, u32[]{:S(2)}) collective-permute-start(f32[32,2560]{1,0:T(8,128)S(1)} %shard_map.74.refs_1_), channel_id=1, source_target_pairs={{0,32},{16,240},{32,64},{48,16},{64,96},{80,48},{96,128},{112,80},... | collective-permute-start | bytes 983048 | tf_op jit(solution)/shard_map/ppermute | solution.py:170
  22.2 2.5 %collective-permute-done.6.refs_0_ = f32[32,2560]{1,0:T(8,128)S(1)} collective-permute-done((f32[32,2560]{1,0:T(8,128)S(1)}, f32[32,2560]{1,0:T(8,128)S(1)}, u32[]{:S(2)}, u32[]{:S(2)}) %collective-permute-start.6) | collective-permute-done | bytes 327712 | tf_op jit(solution)/shard_map/ppermute | solution.py:170
  24.8 3.9 %collective-permute-start.10 = (f32[32,2560]{1,0:T(8,128)S(1)}, f32[32,2560]{1,0:T(8,128)S(1)}, u32[]{:S(2)}, u32[]{:S(2)}) collective-permute-start(f32[32,2560]{1,0:T(8,128)S(1)} %shard_map.76.refs_1_), channel_id=1, source_target_pairs={{0,32},{16,240},{32,64},{48,16},{64,96},{80,48},{96,128},{112,80},... | collective-permute-start | bytes 983048 | tf_op jit(solution)/shard_map/ppermute | solution.py:170
  29.2 2.5 %collective-permute-done.12.refs_0_ = f32[32,2560]{1,0:T(8,128)S(1)} collective-permute-done((f32[32,2560]{1,0:T(8,128)S(1)}, f32[32,2560]{1,0:T(8,128)S(1)}, u32[]{:S(2)}, u32[]{:S(2)}) %collective-permute-start.12) | collective-permute-done | bytes 327712 | tf_op jit(solution)/shard_map/ppermute | solution.py:170
  31.8 3.5 %collective-permute-start.16 = (f32[32,2560]{1,0:T(8,128)S(1)}, f32[32,2560]{1,0:T(8,128)S(1)}, u32[]{:S(2)}, u32[]{:S(2)}) collective-permute-start(f32[32,2560]{1,0:T(8,128)S(1)} %shard_map.78.refs_1_), channel_id=1, source_target_pairs={{0,32},{16,240},{32,64},{48,16},{64,96},{80,48},{96,128},{112,80},... | collective-permute-start | bytes 983048 | tf_op jit(solution)/shard_map/ppermute | solution.py:170
  36.2 2.5 %collective-permute-done.10.refs_0_ = f32[32,2560]{1,0:T(8,128)S(1)} collective-permute-done((f32[32,2560]{1,0:T(8,128)S(1)}, f32[32,2560]{1,0:T(8,128)S(1)}, u32[]{:S(2)}, u32[]{:S(2)}) %collective-permute-start.10) | collective-permute-done | bytes 327712 | tf_op jit(solution)/shard_map/ppermute | solution.py:170
  38.8 3.7 %collective-permute-start.14 = (f32[32,2560]{1,0:T(8,128)S(1)}, f32[32,2560]{1,0:T(8,128)S(1)}, u32[]{:S(2)}, u32[]{:S(2)}) collective-permute-start(f32[32,2560]{1,0:T(8,128)S(1)} %shard_map.80.refs_1_), channel_id=1, source_target_pairs={{0,32},{16,240},{32,64},{48,16},{64,96},{80,48},{96,128},{112,80},... | collective-permute-start | bytes 983048 | tf_op jit(solution)/shard_map/ppermute | solution.py:170
  43.3 2.5 %collective-permute-done.16.refs_0_ = f32[32,2560]{1,0:T(8,128)S(1)} collective-permute-done((f32[32,2560]{1,0:T(8,128)S(1)}, f32[32,2560]{1,0:T(8,128)S(1)}, u32[]{:S(2)}, u32[]{:S(2)}) %collective-permute-start.16) | collective-permute-done | bytes 327712 | tf_op jit(solution)/shard_map/ppermute | solution.py:170
  45.9 3.5 %collective-permute-start.17 = (f32[32,2560]{1,0:T(8,128)S(1)}, f32[32,2560]{1,0:T(8,128)S(1)}, u32[]{:S(2)}, u32[]{:S(2)}) collective-permute-start(f32[32,2560]{1,0:T(8,128)S(1)} %shard_map.82.refs_1_), channel_id=1, source_target_pairs={{0,32},{16,240},{32,64},{48,16},{64,96},{80,48},{96,128},{112,80},... | collective-permute-start | bytes 983048 | tf_op jit(solution)/shard_map/ppermute | solution.py:170
  50.3 6.9 %collective-permute-done.13.refs_0_ = f32[32,2560]{1,0:T(8,128)S(1)} collective-permute-done((f32[32,2560]{1,0:T(8,128)S(1)}, f32[32,2560]{1,0:T(8,128)S(1)}, u32[]{:S(2)}, u32[]{:S(2)}) %collective-permute-start.13) | collective-permute-done | bytes 327712 | tf_op jit(solution)/shard_map/ppermute | solution.py:173
  57.3 2.6 %collective-permute-done.17 = f32[32,2560]{1,0:T(8,128)S(1)} collective-permute-done((f32[32,2560]{1,0:T(8,128)S(1)}, f32[32,2560]{1,0:T(8,128)S(1)}, u32[]{:S(2)}, u32[]{:S(2)}) %collective-permute-start.17) | collective-permute-done | bytes 327712 | tf_op jit(solution)/shard_map/ppermute | solution.py:170
  59.9 1.5 %collective-permute-done.18 = f32[32,2560]{1,0:T(8,128)S(1)} collective-permute-done((f32[32,2560]{1,0:T(8,128)S(1)}, f32[32,2560]{1,0:T(8,128)S(1)}, u32[]{:S(2)}, u32[]{:S(2)}) %collective-permute-start.18) | collective-permute-done | bytes 327712 | tf_op jit(solution)/shard_map/ppermute | solution.py:173
  63.3 2.8 %collective-permute-start.22 = (f32[128]{0:T(128)S(1)}, f32[128]{0:T(128)S(1)}, u32[]{:S(2)}, u32[]{:S(2)}) collective-permute-start(f32[128]{0:T(128)S(1)} %pad_maximum_fusion.4), channel_id=1, source_target_pairs={{0,4},{1,5},{2,6},{3,7},{4,0},{5,1},{6,2},{7,3},{8,12},{9,13},{10,... | collective-permute-start | bytes 1544 | tf_op jit(solution)/shard_map/ppermute | solution.py:153
  67.2 2.5 %collective-permute-done.21 = f32[128]{0:T(128)S(1)} collective-permute-done((f32[128]{0:T(128)S(1)}, f32[128]{0:T(128)S(1)}, u32[]{:S(2)}, u32[]{:S(2)}) %collective-permute-start.21) | collective-permute-done | bytes 544 | tf_op jit(solution)/shard_map/ppermute | solution.py:153
  70.2 1.8 %collective-permute-start.25 = (f32[5248]{0:T(1024)S(1)}, f32[5248]{0:T(1024)S(1)}, u32[]{:S(2)}, u32[]{:S(2)}) collective-permute-start(f32[5248]{0:T(1024)S(1)} %pad_maximum_fusion.1), channel_id=1, source_target_pairs={{0,1},{1,0},{2,3},{3,2},{4,5},{5,4},{6,7},{7,6},{8,9},{9,8},{10,11... | collective-permute-start | bytes 62984 | tf_op jit(solution)/shard_map/ppermute | solution.py:153
  75.2 2.9 %collective-permute-start.27 = (f32[5248]{0:T(1024)S(1)}, f32[5248]{0:T(1024)S(1)}, u32[]{:S(2)}, u32[]{:S(2)}) collective-permute-start(f32[5248]{0:T(1024)S(1)} %add_add_fusion.1), channel_id=1, source_target_pairs={{0,1},{1,0},{2,3},{3,2},{4,5},{5,4},{6,7},{7,6},{8,9},{9,8},{10,11... | collective-permute-start | bytes 62984 | tf_op jit(solution)/shard_map/ppermute | solution.py:153
  79.4 2.9 %collective-permute-start.30 = (f32[5248]{0:T(1024)S(1)}, f32[5248]{0:T(1024)S(1)}, u32[]{:S(2)}, u32[]{:S(2)}) collective-permute-start(f32[5248]{0:T(1024)S(1)} %add.77), channel_id=1, source_target_pairs={{0,1},{1,0},{2,3},{3,2},{4,5},{5,4},{6,7},{7,6},{8,9},{9,8},{10,11... | collective-permute-start | bytes 62984 | tf_op jit(solution)/shard_map/ppermute | solution.py:153
  83.6 2.6 %collective-permute-done.29 = f32[5248]{0:T(1024)S(1)} collective-permute-done((f32[5248]{0:T(1024)S(1)}, f32[5248]{0:T(1024)S(1)}, u32[]{:S(2)}, u32[]{:S(2)}) %collective-permute-start.29) | collective-permute-done | bytes 21024 | tf_op jit(solution)/shard_map/ppermute | solution.py:153
  92.7 1.5 %shard_map.86 = (f32[64,2560]{1,0:T(8,128)}, f32[1,1]{1,0:T(1,128)}) custom-call(f32[64,2560]{1,0:T(8,128)S(1)} %rsqrt_multiply_fusion.scaled, f32[1,128]{1,0:T(1,128)S(1)} %get-tuple-element.43.row_sum, f32[1,128]{1,0:T(1,128)S(1)} %get-tuple-element.42.total), custom_call_target="tpu_custom_call" | custom-call | flops 1150000000 | tf_op jit(solution)/shard_map/pallas_call | solution.py:126
  (100 shorter events, 24.5 us)
Async XLA Ops:
  1.7 9.2 %collective-permute-start.1 = (f32[1,32,2560]{2,1,0:T(8,128)S(1)}, f32[1,32,2560]{2,1,0:T(8,128)S(1)}, u32[]{:S(2)}, u32[]{:S(2)}) collective-permute-start(f32[1,32,2560]{2,1,0:T(8,128)S(1)} %get-tuple-element.22), channel_id=1, source_target_pairs={{0,16},{16,0},{32,48},{48,32},{64,80},{80,64},{96,112},{112,96},{1... | collective-permute-start | bytes 983048 | tf_op jit(solution)/shard_map/ppermute | solution.py:70
  6.5 4.6 %collective-permute-start = (f32[2,64,2560]{2,1,0:T(8,128)S(1)}, f32[2,64,2560]{2,1,0:T(8,128)S(1)}, u32[]{:S(2)}, u32[]{:S(2)}) collective-permute-start(f32[2,64,2560]{2,1,0:T(8,128)S(1)} %get-tuple-element.21), channel_id=1, source_target_pairs={{0,16},{16,0},{32,48},{48,32},{64,80},{80,64},{96,112},{112,96},{1... | collective-permute-start | bytes 3932168 | tf_op jit(solution)/shard_map/ppermute | solution.py:70
  7.0 10.9 %collective-permute-start.8 = (f32[32,2560]{1,0:T(8,128)S(1)}, f32[32,2560]{1,0:T(8,128)S(1)}, u32[]{:S(2)}, u32[]{:S(2)}) collective-permute-start(f32[32,2560]{1,0:T(8,128)S(1)} %shard_map.68.refs_0_), channel_id=1, source_target_pairs={{0,32},{16,240},{32,64},{48,16},{64,96},{80,48},{96,128},{112,80},... | collective-permute-start | bytes 983048 | tf_op jit(solution)/shard_map/ppermute | solution.py:170
  11.0 11.1 %collective-permute-start.7 = (f32[32,2560]{1,0:T(8,128)S(1)}, f32[32,2560]{1,0:T(8,128)S(1)}, u32[]{:S(2)}, u32[]{:S(2)}) collective-permute-start(f32[32,2560]{1,0:T(8,128)S(1)} %shard_map.69.refs_0_), channel_id=1, source_target_pairs={{32,0},{240,16},{64,32},{16,48},{96,64},{48,80},{128,96},{80,112},... | collective-permute-start | bytes 983048 | tf_op jit(solution)/shard_map/ppermute | solution.py:173
  11.1 13.6 %collective-permute-start.6 = (f32[32,2560]{1,0:T(8,128)S(1)}, f32[32,2560]{1,0:T(8,128)S(1)}, u32[]{:S(2)}, u32[]{:S(2)}) collective-permute-start(f32[32,2560]{1,0:T(8,128)S(1)} %shard_map.70.refs_0_), channel_id=1, source_target_pairs={{0,32},{16,240},{32,64},{48,16},{64,96},{80,48},{96,128},{112,80},... | collective-permute-start | bytes 983048 | tf_op jit(solution)/shard_map/ppermute | solution.py:170
  13.9 15.2 %collective-permute-start.5 = (f32[32,2560]{1,0:T(8,128)S(1)}, f32[32,2560]{1,0:T(8,128)S(1)}, u32[]{:S(2)}, u32[]{:S(2)}) collective-permute-start(f32[32,2560]{1,0:T(8,128)S(1)} %shard_map.71.refs_0_), channel_id=1, source_target_pairs={{32,0},{240,16},{64,32},{16,48},{96,64},{48,80},{128,96},{80,112},... | collective-permute-start | bytes 983048 | tf_op jit(solution)/shard_map/ppermute | solution.py:173
  15.3 9.4 %collective-permute-start.4 = (f32[2,64,2560]{2,1,0:T(8,128)S(1)}, f32[2,64,2560]{2,1,0:T(8,128)S(1)}, u32[]{:S(2)}, u32[]{:S(2)}) collective-permute-start(f32[2,64,2560]{2,1,0:T(8,128)S(1)} %get-tuple-element.27), channel_id=1, source_target_pairs={{0,16},{16,0},{32,48},{48,32},{64,80},{80,64},{96,112},{112,96},{1... | collective-permute-start | bytes 3932168 | tf_op jit(solution)/shard_map/ppermute | solution.py:70
  18.0 13.8 %collective-permute-start.12 = (f32[32,2560]{1,0:T(8,128)S(1)}, f32[32,2560]{1,0:T(8,128)S(1)}, u32[]{:S(2)}, u32[]{:S(2)}) collective-permute-start(f32[32,2560]{1,0:T(8,128)S(1)} %shard_map.74.refs_1_), channel_id=1, source_target_pairs={{0,32},{16,240},{32,64},{48,16},{64,96},{80,48},{96,128},{112,80},... | collective-permute-start | bytes 983048 | tf_op jit(solution)/shard_map/ppermute | solution.py:170
  22.1 14.0 %collective-permute-start.11 = (f32[32,2560]{1,0:T(8,128)S(1)}, f32[32,2560]{1,0:T(8,128)S(1)}, u32[]{:S(2)}, u32[]{:S(2)}) collective-permute-start(f32[32,2560]{1,0:T(8,128)S(1)} %shard_map.75.refs_1_), channel_id=1, source_target_pairs={{32,0},{240,16},{64,32},{16,48},{96,64},{48,80},{128,96},{80,112},... | collective-permute-start | bytes 983048 | tf_op jit(solution)/shard_map/ppermute | solution.py:173
  24.7 14.0 %collective-permute-start.3 = (f32[3,64,2560]{2,1,0:T(8,128)S(1)}, f32[3,64,2560]{2,1,0:T(8,128)S(1)}, u32[]{:S(2)}, u32[]{:S(2)}) collective-permute-start(f32[3,64,2560]{2,1,0:T(8,128)S(1)} %get-tuple-element.26), channel_id=1, source_target_pairs={{0,16},{16,0},{32,48},{48,32},{64,80},{80,64},{96,112},{112,96},{1... | collective-permute-start | bytes 5898248 | tf_op jit(solution)/shard_map/ppermute | solution.py:70
  24.8 14.0 %collective-permute-start.10 = (f32[32,2560]{1,0:T(8,128)S(1)}, f32[32,2560]{1,0:T(8,128)S(1)}, u32[]{:S(2)}, u32[]{:S(2)}) collective-permute-start(f32[32,2560]{1,0:T(8,128)S(1)} %shard_map.76.refs_1_), channel_id=1, source_target_pairs={{0,32},{16,240},{32,64},{48,16},{64,96},{80,48},{96,128},{112,80},... | collective-permute-start | bytes 983048 | tf_op jit(solution)/shard_map/ppermute | solution.py:170
  29.1 14.0 %collective-permute-start.9 = (f32[32,2560]{1,0:T(8,128)S(1)}, f32[32,2560]{1,0:T(8,128)S(1)}, u32[]{:S(2)}, u32[]{:S(2)}) collective-permute-start(f32[32,2560]{1,0:T(8,128)S(1)} %shard_map.77.refs_1_), channel_id=1, source_target_pairs={{32,0},{240,16},{64,32},{16,48},{96,64},{48,80},{128,96},{80,112},... | collective-permute-start | bytes 983048 | tf_op jit(solution)/shard_map/ppermute | solution.py:173
  31.8 14.0 %collective-permute-start.16 = (f32[32,2560]{1,0:T(8,128)S(1)}, f32[32,2560]{1,0:T(8,128)S(1)}, u32[]{:S(2)}, u32[]{:S(2)}) collective-permute-start(f32[32,2560]{1,0:T(8,128)S(1)} %shard_map.78.refs_1_), channel_id=1, source_target_pairs={{0,32},{16,240},{32,64},{48,16},{64,96},{80,48},{96,128},{112,80},... | collective-permute-start | bytes 983048 | tf_op jit(solution)/shard_map/ppermute | solution.py:170
  36.1 14.0 %collective-permute-start.15 = (f32[32,2560]{1,0:T(8,128)S(1)}, f32[32,2560]{1,0:T(8,128)S(1)}, u32[]{:S(2)}, u32[]{:S(2)}) collective-permute-start(f32[32,2560]{1,0:T(8,128)S(1)} %shard_map.79.refs_1_), channel_id=1, source_target_pairs={{32,0},{240,16},{64,32},{16,48},{96,64},{48,80},{128,96},{80,112},... | collective-permute-start | bytes 983048 | tf_op jit(solution)/shard_map/ppermute | solution.py:173
  38.8 18.3 %collective-permute-start.14 = (f32[32,2560]{1,0:T(8,128)S(1)}, f32[32,2560]{1,0:T(8,128)S(1)}, u32[]{:S(2)}, u32[]{:S(2)}) collective-permute-start(f32[32,2560]{1,0:T(8,128)S(1)} %shard_map.80.refs_1_), channel_id=1, source_target_pairs={{0,32},{16,240},{32,64},{48,16},{64,96},{80,48},{96,128},{112,80},... | collective-permute-start | bytes 983048 | tf_op jit(solution)/shard_map/ppermute | solution.py:170
  43.2 14.0 %collective-permute-start.13 = (f32[32,2560]{1,0:T(8,128)S(1)}, f32[32,2560]{1,0:T(8,128)S(1)}, u32[]{:S(2)}, u32[]{:S(2)}) collective-permute-start(f32[32,2560]{1,0:T(8,128)S(1)} %shard_map.81.refs_1_), channel_id=1, source_target_pairs={{32,0},{240,16},{64,32},{16,48},{96,64},{48,80},{128,96},{80,112},... | collective-permute-start | bytes 983048 | tf_op jit(solution)/shard_map/ppermute | solution.py:173
  45.9 14.0 %collective-permute-start.17 = (f32[32,2560]{1,0:T(8,128)S(1)}, f32[32,2560]{1,0:T(8,128)S(1)}, u32[]{:S(2)}, u32[]{:S(2)}) collective-permute-start(f32[32,2560]{1,0:T(8,128)S(1)} %shard_map.82.refs_1_), channel_id=1, source_target_pairs={{0,32},{16,240},{32,64},{48,16},{64,96},{80,48},{96,128},{112,80},... | collective-permute-start | bytes 983048 | tf_op jit(solution)/shard_map/ppermute | solution.py:170
  50.2 11.2 %collective-permute-start.18 = (f32[32,2560]{1,0:T(8,128)S(1)}, f32[32,2560]{1,0:T(8,128)S(1)}, u32[]{:S(2)}, u32[]{:S(2)}) collective-permute-start(f32[32,2560]{1,0:T(8,128)S(1)} %shard_map.83._), channel_id=1, source_target_pairs={{32,0},{240,16},{64,32},{16,48},{96,64},{48,80},{128,96},{80,112},... | collective-permute-start | bytes 983048 | tf_op jit(solution)/shard_map/ppermute | solution.py:173
  63.0 7.0 %collective-permute-start.23 = (f32[64,2560]{1,0:T(8,128)S(1)}, f32[64,2560]{1,0:T(8,128)S(1)}, u32[]{:S(2)}, u32[]{:S(2)}) collective-permute-start(f32[64,2560]{1,0:T(8,128)S(1)} %pad_maximum_fusion), channel_id=1, source_target_pairs={{0,16},{16,0},{32,48},{48,32},{64,80},{80,64},{96,112},{112,96},{1... | collective-permute-start | bytes 1966088 | tf_op jit(solution)/shard_map/ppermute | solution.py:211
  63.3 3.9 %collective-permute-start.22 = (f32[128]{0:T(128)S(1)}, f32[128]{0:T(128)S(1)}, u32[]{:S(2)}, u32[]{:S(2)}) collective-permute-start(f32[128]{0:T(128)S(1)} %pad_maximum_fusion.4), channel_id=1, source_target_pairs={{0,4},{1,5},{2,6},{3,7},{4,0},{5,1},{6,2},{7,3},{8,12},{9,13},{10,... | collective-permute-start | bytes 1544 | tf_op jit(solution)/shard_map/ppermute | solution.py:153
  70.2 4.7 %collective-permute-start.25 = (f32[5248]{0:T(1024)S(1)}, f32[5248]{0:T(1024)S(1)}, u32[]{:S(2)}, u32[]{:S(2)}) collective-permute-start(f32[5248]{0:T(1024)S(1)} %pad_maximum_fusion.1), channel_id=1, source_target_pairs={{0,1},{1,0},{2,3},{3,2},{4,5},{5,4},{6,7},{7,6},{8,9},{9,8},{10,11... | collective-permute-start | bytes 62984 | tf_op jit(solution)/shard_map/ppermute | solution.py:153
  75.2 4.2 %collective-permute-start.27 = (f32[5248]{0:T(1024)S(1)}, f32[5248]{0:T(1024)S(1)}, u32[]{:S(2)}, u32[]{:S(2)}) collective-permute-start(f32[5248]{0:T(1024)S(1)} %add_add_fusion.1), channel_id=1, source_target_pairs={{0,1},{1,0},{2,3},{3,2},{4,5},{5,4},{6,7},{7,6},{8,9},{9,8},{10,11... | collective-permute-start | bytes 62984 | tf_op jit(solution)/shard_map/ppermute | solution.py:153
  79.4 4.2 %collective-permute-start.30 = (f32[5248]{0:T(1024)S(1)}, f32[5248]{0:T(1024)S(1)}, u32[]{:S(2)}, u32[]{:S(2)}) collective-permute-start(f32[5248]{0:T(1024)S(1)} %add.77), channel_id=1, source_target_pairs={{0,1},{1,0},{2,3},{3,2},{4,5},{5,4},{6,7},{7,6},{8,9},{9,8},{10,11... | collective-permute-start | bytes 62984 | tf_op jit(solution)/shard_map/ppermute | solution.py:153
  86.2 4.0 %collective-permute-start.33 = (f32[128]{0:T(128)S(1)}, f32[128]{0:T(128)S(1)}, u32[]{:S(2)}, u32[]{:S(2)}) collective-permute-start(f32[128]{0:T(128)S(1)} %get-tuple-element.38), channel_id=1, source_target_pairs={{0,4},{1,5},{2,6},{3,7},{4,0},{5,1},{6,2},{7,3},{8,12},{9,13},{10,... | collective-permute-start | bytes 1544 | tf_op jit(solution)/shard_map/ppermute | solution.py:153
  (15 other events, 63.5 us)

commit v7 on v6

--- a/solution.py
+++ b/solution.py
@@ -220,8 +220,8 @@
         packed.append(sums)
     packed = jnp.concatenate([*packed, row_new])
 
+    packed = packed + exchange(packed, (7, 0, 0), (0, 0, 1))
     packed = sum_four(packed, 0, (0, 0, 1))
-    packed = packed + exchange(packed, (7, 0, 0), (0, 0, 1))
     packed = sum_four(packed, 1, (0, 0, 1))
     col_new = 0.8 * col_old + 0.2 * packed[:COLS] / D
     total = jnp.sum((packed[COLS:2 * COLS] / col_new).reshape(20, 128), axis=0)

time: 94.6 us -> 95.6 us (1.011)
  transfers between devices with their start and end apart: 35 -> 35, of which waited for: 24 -> 23; matrix products, arithmetic and copies ran while one was open for 0% -> 0% of each run, Pallas kernels for 5% -> 5%
where the time goes in v7:
time: 95.6 us; the launch traced here: 95.4 us
  starting transfers between devices  46.4 us (49%)
  waiting for transfers between devices  39 us (41%)
  Pallas kernels  7.5 us (8%)
  between operations  1.15 us (1%)
  other arithmetic  1.14 us (1%)
    ppermute x7, starting transfers between devices, up(): return lax.ppermute(x, 'dp', UP)  24.4 us
    ppermute x13, starting transfers between devices, exchange(): return lax.ppermute(v, ('dp', 'row', 'col'), pairs)  16.1 us
    ppermute x7, waiting for transfers between devices, up(): return lax.ppermute(x, 'dp', UP)  12.7 us
    ppermute x13, waiting for transfers between devices, exchange(): return lax.ppermute(v, ('dp', 'row', 'col'), pairs)  12.1 us
    ppermute x7, waiting for transfers between devices, down(): return lax.ppermute(x, 'dp', DOWN)  11.8 us
    pallas_call x4, Pallas kernels, fetch(): pl.pallas_call(functools.partial(fetch_kernel, ks, split, len(after)), ou...  5.24 us
    ppermute x5, starting transfers between devices, fetch(): return (own, *(lax.ppermute(x, 'dp', SWAP) for x in sent))  5.03 us
  transfers between devices with their start and end apart: 35, of which 23 were waited for; matrix products, arithmetic and copies ran while one was open for 0% of the time, Pallas kernels for 5%

profile of v7, /device:TPU:1, one launch (start us, length us, event | category | flops | bytes accessed | tf_op | source)
XLA Modules:
  0.0 95.4 jit_solution(7787359302723455364)
XLA Ops:
  1.7 3.3 %collective-permute-start.1 = (f32[1,32,2560]{2,1,0:T(8,128)S(1)}, f32[1,32,2560]{2,1,0:T(8,128)S(1)}, u32[]{:S(2)}, u32[]{:S(2)}) collective-permute-start(f32[1,32,2560]{2,1,0:T(8,128)S(1)} %get-tuple-element.22), channel_id=1, source_target_pairs={{0,16},{16,0},{32,48},{48,32},{64,80},{80,64},{96,112},{112,96},{1... | collective-permute-start | bytes 983048 | tf_op jit(solution)/shard_map/ppermute | solution.py:70
  7.0 3.9 %collective-permute-start.8 = (f32[32,2560]{1,0:T(8,128)S(1)}, f32[32,2560]{1,0:T(8,128)S(1)}, u32[]{:S(2)}, u32[]{:S(2)}) collective-permute-start(f32[32,2560]{1,0:T(8,128)S(1)} %shard_map.68.refs_0_), channel_id=1, source_target_pairs={{0,32},{16,240},{32,64},{48,16},{64,96},{80,48},{96,128},{112,80},... | collective-permute-start | bytes 983048 | tf_op jit(solution)/shard_map/ppermute | solution.py:170
  11.1 2.7 %collective-permute-start.6 = (f32[32,2560]{1,0:T(8,128)S(1)}, f32[32,2560]{1,0:T(8,128)S(1)}, u32[]{:S(2)}, u32[]{:S(2)}) collective-permute-start(f32[32,2560]{1,0:T(8,128)S(1)} %shard_map.70.refs_0_), channel_id=1, source_target_pairs={{0,32},{16,240},{32,64},{48,16},{64,96},{80,48},{96,128},{112,80},... | collective-permute-start | bytes 983048 | tf_op jit(solution)/shard_map/ppermute | solution.py:170
  16.4 1.5 %shard_map.73 = (bf16[3,64,2560]{2,1,0:T(8,128)(2,1)S(1)}, f32[3,64,2560]{2,1,0:T(8,128)S(1)}) custom-call(bf16[16,64,2560]{2,1,0:T(8,128)(2,1)} %bitcast.19, bf16[2,64,2560]{2,1,0:T(8,128)(2,1)S(1)} %get-tuple-element.24.refs_0_.own), custom_call_target="tpu_custom_call" | custom-call | tf_op jit(solution)/shard_map/pallas_call | solution.py:56
  18.0 3.3 %collective-permute-start.12 = (f32[32,2560]{1,0:T(8,128)S(1)}, f32[32,2560]{1,0:T(8,128)S(1)}, u32[]{:S(2)}, u32[]{:S(2)}) collective-permute-start(f32[32,2560]{1,0:T(8,128)S(1)} %shard_map.74.refs_1_), channel_id=1, source_target_pairs={{0,32},{16,240},{32,64},{48,16},{64,96},{80,48},{96,128},{112,80},... | collective-permute-start | bytes 983048 | tf_op jit(solution)/shard_map/ppermute | solution.py:170
  22.2 2.5 %collective-permute-done.6.refs_0_ = f32[32,2560]{1,0:T(8,128)S(1)} collective-permute-done((f32[32,2560]{1,0:T(8,128)S(1)}, f32[32,2560]{1,0:T(8,128)S(1)}, u32[]{:S(2)}, u32[]{:S(2)}) %collective-permute-start.6) | collective-permute-done | bytes 327712 | tf_op jit(solution)/shard_map/ppermute | solution.py:170
  24.8 3.9 %collective-permute-start.10 = (f32[32,2560]{1,0:T(8,128)S(1)}, f32[32,2560]{1,0:T(8,128)S(1)}, u32[]{:S(2)}, u32[]{:S(2)}) collective-permute-start(f32[32,2560]{1,0:T(8,128)S(1)} %shard_map.76.refs_1_), channel_id=1, source_target_pairs={{0,32},{16,240},{32,64},{48,16},{64,96},{80,48},{96,128},{112,80},... | collective-permute-start | bytes 983048 | tf_op jit(solution)/shard_map/ppermute | solution.py:170
  29.2 2.5 %collective-permute-done.12.refs_0_ = f32[32,2560]{1,0:T(8,128)S(1)} collective-permute-done((f32[32,2560]{1,0:T(8,128)S(1)}, f32[32,2560]{1,0:T(8,128)S(1)}, u32[]{:S(2)}, u32[]{:S(2)}) %collective-permute-start.12) | collective-permute-done | bytes 327712 | tf_op jit(solution)/shard_map/ppermute | solution.py:170
  31.8 3.5 %collective-permute-start.16 = (f32[32,2560]{1,0:T(8,128)S(1)}, f32[32,2560]{1,0:T(8,128)S(1)}, u32[]{:S(2)}, u32[]{:S(2)}) collective-permute-start(f32[32,2560]{1,0:T(8,128)S(1)} %shard_map.78.refs_1_), channel_id=1, source_target_pairs={{0,32},{16,240},{32,64},{48,16},{64,96},{80,48},{96,128},{112,80},... | collective-permute-start | bytes 983048 | tf_op jit(solution)/shard_map/ppermute | solution.py:170
  36.2 2.5 %collective-permute-done.10.refs_0_ = f32[32,2560]{1,0:T(8,128)S(1)} collective-permute-done((f32[32,2560]{1,0:T(8,128)S(1)}, f32[32,2560]{1,0:T(8,128)S(1)}, u32[]{:S(2)}, u32[]{:S(2)}) %collective-permute-start.10) | collective-permute-done | bytes 327712 | tf_op jit(solution)/shard_map/ppermute | solution.py:170
  38.8 3.7 %collective-permute-start.14 = (f32[32,2560]{1,0:T(8,128)S(1)}, f32[32,2560]{1,0:T(8,128)S(1)}, u32[]{:S(2)}, u32[]{:S(2)}) collective-permute-start(f32[32,2560]{1,0:T(8,128)S(1)} %shard_map.80.refs_1_), channel_id=1, source_target_pairs={{0,32},{16,240},{32,64},{48,16},{64,96},{80,48},{96,128},{112,80},... | collective-permute-start | bytes 983048 | tf_op jit(solution)/shard_map/ppermute | solution.py:170
  43.3 2.5 %collective-permute-done.16.refs_0_ = f32[32,2560]{1,0:T(8,128)S(1)} collective-permute-done((f32[32,2560]{1,0:T(8,128)S(1)}, f32[32,2560]{1,0:T(8,128)S(1)}, u32[]{:S(2)}, u32[]{:S(2)}) %collective-permute-start.16) | collective-permute-done | bytes 327712 | tf_op jit(solution)/shard_map/ppermute | solution.py:170
  45.9 3.5 %collective-permute-start.17 = (f32[32,2560]{1,0:T(8,128)S(1)}, f32[32,2560]{1,0:T(8,128)S(1)}, u32[]{:S(2)}, u32[]{:S(2)}) collective-permute-start(f32[32,2560]{1,0:T(8,128)S(1)} %shard_map.82.refs_1_), channel_id=1, source_target_pairs={{0,32},{16,240},{32,64},{48,16},{64,96},{80,48},{96,128},{112,80},... | collective-permute-start | bytes 983048 | tf_op jit(solution)/shard_map/ppermute | solution.py:170
  50.3 6.9 %collective-permute-done.13.refs_0_ = f32[32,2560]{1,0:T(8,128)S(1)} collective-permute-done((f32[32,2560]{1,0:T(8,128)S(1)}, f32[32,2560]{1,0:T(8,128)S(1)}, u32[]{:S(2)}, u32[]{:S(2)}) %collective-permute-start.13) | collective-permute-done | bytes 327712 | tf_op jit(solution)/shard_map/ppermute | solution.py:173
  57.3 2.6 %collective-permute-done.17 = f32[32,2560]{1,0:T(8,128)S(1)} collective-permute-done((f32[32,2560]{1,0:T(8,128)S(1)}, f32[32,2560]{1,0:T(8,128)S(1)}, u32[]{:S(2)}, u32[]{:S(2)}) %collective-permute-start.17) | collective-permute-done | bytes 327712 | tf_op jit(solution)/shard_map/ppermute | solution.py:170
  59.9 1.5 %collective-permute-done.18 = f32[32,2560]{1,0:T(8,128)S(1)} collective-permute-done((f32[32,2560]{1,0:T(8,128)S(1)}, f32[32,2560]{1,0:T(8,128)S(1)}, u32[]{:S(2)}, u32[]{:S(2)}) %collective-permute-start.18) | collective-permute-done | bytes 327712 | tf_op jit(solution)/shard_map/ppermute | solution.py:173
  63.3 2.8 %collective-permute-start.22 = (f32[128]{0:T(128)S(1)}, f32[128]{0:T(128)S(1)}, u32[]{:S(2)}, u32[]{:S(2)}) collective-permute-start(f32[128]{0:T(128)S(1)} %pad_maximum_fusion.4), channel_id=1, source_target_pairs={{0,4},{1,5},{2,6},{3,7},{4,0},{5,1},{6,2},{7,3},{8,12},{9,13},{10,... | collective-permute-start | bytes 1544 | tf_op jit(solution)/shard_map/ppermute | solution.py:153
  67.2 2.5 %collective-permute-done.21 = f32[128]{0:T(128)S(1)} collective-permute-done((f32[128]{0:T(128)S(1)}, f32[128]{0:T(128)S(1)}, u32[]{:S(2)}, u32[]{:S(2)}) %collective-permute-start.21) | collective-permute-done | bytes 544 | tf_op jit(solution)/shard_map/ppermute | solution.py:153
  70.1 2.9 %collective-permute-start.24 = (f32[5248]{0:T(1024)S(1)}, f32[5248]{0:T(1024)S(1)}, u32[]{:S(2)}, u32[]{:S(2)}) collective-permute-start(f32[5248]{0:T(1024)S(1)} %pad_maximum_fusion.1), channel_id=1, source_target_pairs={{0,1},{1,0},{2,3},{3,2},{4,5},{5,4},{6,7},{7,6},{8,9},{9,8},{10,11... | collective-permute-start | bytes 62984 | tf_op jit(solution)/shard_map/ppermute | solution.py:153
  75.7 1.6 %collective-permute-start.26 = (f32[5248]{0:T(1024)S(1)}, f32[5248]{0:T(1024)S(1)}, u32[]{:S(2)}, u32[]{:S(2)}) collective-permute-start(f32[5248]{0:T(1024)S(1)} %fusion.8), channel_id=1, source_target_pairs={{0,1},{1,0},{2,3},{3,2},{4,5},{5,4},{6,7},{7,6},{8,9},{9,8},{10,11... | collective-permute-start | bytes 62984 | tf_op jit(solution)/shard_map/ppermute | solution.py:153
  77.9 2.4 %collective-permute-done.26 = f32[5248]{0:T(1024)S(1)} collective-permute-done((f32[5248]{0:T(1024)S(1)}, f32[5248]{0:T(1024)S(1)}, u32[]{:S(2)}, u32[]{:S(2)}) %collective-permute-start.26) | collective-permute-done | bytes 21024 | tf_op jit(solution)/shard_map/ppermute | solution.py:153
  80.3 3.0 %collective-permute-start.30 = (f32[5248]{0:T(1024)S(1)}, f32[5248]{0:T(1024)S(1)}, u32[]{:S(2)}, u32[]{:S(2)}) collective-permute-start(f32[5248]{0:T(1024)S(1)} %add_add_fusion.1), channel_id=1, source_target_pairs={{0,1},{1,0},{2,3},{3,2},{4,5},{5,4},{6,7},{7,6},{8,9},{9,8},{10,11... | collective-permute-start | bytes 62984 | tf_op jit(solution)/shard_map/ppermute | solution.py:153
  84.5 2.6 %collective-permute-done.29 = f32[5248]{0:T(1024)S(1)} collective-permute-done((f32[5248]{0:T(1024)S(1)}, f32[5248]{0:T(1024)S(1)}, u32[]{:S(2)}, u32[]{:S(2)}) %collective-permute-start.29) | collective-permute-done | bytes 21024 | tf_op jit(solution)/shard_map/ppermute | solution.py:153
  93.6 1.5 %shard_map.86 = (f32[64,2560]{1,0:T(8,128)}, f32[1,1]{1,0:T(1,128)}) custom-call(f32[64,2560]{1,0:T(8,128)S(1)} %rsqrt_multiply_fusion.scaled, f32[1,128]{1,0:T(1,128)S(1)} %get-tuple-element.43.row_sum, f32[1,128]{1,0:T(1,128)S(1)} %get-tuple-element.42.total), custom_call_target="tpu_custom_call" | custom-call | flops 1150000000 | tf_op jit(solution)/shard_map/pallas_call | solution.py:126
  (100 shorter events, 24.6 us)
Async XLA Ops:
  1.7 9.2 %collective-permute-start.1 = (f32[1,32,2560]{2,1,0:T(8,128)S(1)}, f32[1,32,2560]{2,1,0:T(8,128)S(1)}, u32[]{:S(2)}, u32[]{:S(2)}) collective-permute-start(f32[1,32,2560]{2,1,0:T(8,128)S(1)} %get-tuple-element.22), channel_id=1, source_target_pairs={{0,16},{16,0},{32,48},{48,32},{64,80},{80,64},{96,112},{112,96},{1... | collective-permute-start | bytes 983048 | tf_op jit(solution)/shard_map/ppermute | solution.py:70
  6.5 4.6 %collective-permute-start = (f32[2,64,2560]{2,1,0:T(8,128)S(1)}, f32[2,64,2560]{2,1,0:T(8,128)S(1)}, u32[]{:S(2)}, u32[]{:S(2)}) collective-permute-start(f32[2,64,2560]{2,1,0:T(8,128)S(1)} %get-tuple-element.21), channel_id=1, source_target_pairs={{0,16},{16,0},{32,48},{48,32},{64,80},{80,64},{96,112},{112,96},{1... | collective-permute-start | bytes 3932168 | tf_op jit(solution)/shard_map/ppermute | solution.py:70
  7.0 10.9 %collective-permute-start.8 = (f32[32,2560]{1,0:T(8,128)S(1)}, f32[32,2560]{1,0:T(8,128)S(1)}, u32[]{:S(2)}, u32[]{:S(2)}) collective-permute-start(f32[32,2560]{1,0:T(8,128)S(1)} %shard_map.68.refs_0_), channel_id=1, source_target_pairs={{0,32},{16,240},{32,64},{48,16},{64,96},{80,48},{96,128},{112,80},... | collective-permute-start | bytes 983048 | tf_op jit(solution)/shard_map/ppermute | solution.py:170
  11.0 11.1 %collective-permute-start.7 = (f32[32,2560]{1,0:T(8,128)S(1)}, f32[32,2560]{1,0:T(8,128)S(1)}, u32[]{:S(2)}, u32[]{:S(2)}) collective-permute-start(f32[32,2560]{1,0:T(8,128)S(1)} %shard_map.69.refs_0_), channel_id=1, source_target_pairs={{32,0},{240,16},{64,32},{16,48},{96,64},{48,80},{128,96},{80,112},... | collective-permute-start | bytes 983048 | tf_op jit(solution)/shard_map/ppermute | solution.py:173
  11.1 13.6 %collective-permute-start.6 = (f32[32,2560]{1,0:T(8,128)S(1)}, f32[32,2560]{1,0:T(8,128)S(1)}, u32[]{:S(2)}, u32[]{:S(2)}) collective-permute-start(f32[32,2560]{1,0:T(8,128)S(1)} %shard_map.70.refs_0_), channel_id=1, source_target_pairs={{0,32},{16,240},{32,64},{48,16},{64,96},{80,48},{96,128},{112,80},... | collective-permute-start | bytes 983048 | tf_op jit(solution)/shard_map/ppermute | solution.py:170
  13.9 15.2 %collective-permute-start.5 = (f32[32,2560]{1,0:T(8,128)S(1)}, f32[32,2560]{1,0:T(8,128)S(1)}, u32[]{:S(2)}, u32[]{:S(2)}) collective-permute-start(f32[32,2560]{1,0:T(8,128)S(1)} %shard_map.71.refs_0_), channel_id=1, source_target_pairs={{32,0},{240,16},{64,32},{16,48},{96,64},{48,80},{128,96},{80,112},... | collective-permute-start | bytes 983048 | tf_op jit(solution)/shard_map/ppermute | solution.py:173
  15.3 9.4 %collective-permute-start.4 = (f32[2,64,2560]{2,1,0:T(8,128)S(1)}, f32[2,64,2560]{2,1,0:T(8,128)S(1)}, u32[]{:S(2)}, u32[]{:S(2)}) collective-permute-start(f32[2,64,2560]{2,1,0:T(8,128)S(1)} %get-tuple-element.27), channel_id=1, source_target_pairs={{0,16},{16,0},{32,48},{48,32},{64,80},{80,64},{96,112},{112,96},{1... | collective-permute-start | bytes 3932168 | tf_op jit(solution)/shard_map/ppermute | solution.py:70
  18.0 13.8 %collective-permute-start.12 = (f32[32,2560]{1,0:T(8,128)S(1)}, f32[32,2560]{1,0:T(8,128)S(1)}, u32[]{:S(2)}, u32[]{:S(2)}) collective-permute-start(f32[32,2560]{1,0:T(8,128)S(1)} %shard_map.74.refs_1_), channel_id=1, source_target_pairs={{0,32},{16,240},{32,64},{48,16},{64,96},{80,48},{96,128},{112,80},... | collective-permute-start | bytes 983048 | tf_op jit(solution)/shard_map/ppermute | solution.py:170
  22.1 14.0 %collective-permute-start.11 = (f32[32,2560]{1,0:T(8,128)S(1)}, f32[32,2560]{1,0:T(8,128)S(1)}, u32[]{:S(2)}, u32[]{:S(2)}) collective-permute-start(f32[32,2560]{1,0:T(8,128)S(1)} %shard_map.75.refs_1_), channel_id=1, source_target_pairs={{32,0},{240,16},{64,32},{16,48},{96,64},{48,80},{128,96},{80,112},... | collective-permute-start | bytes 983048 | tf_op jit(solution)/shard_map/ppermute | solution.py:173
  24.7 14.0 %collective-permute-start.3 = (f32[3,64,2560]{2,1,0:T(8,128)S(1)}, f32[3,64,2560]{2,1,0:T(8,128)S(1)}, u32[]{:S(2)}, u32[]{:S(2)}) collective-permute-start(f32[3,64,2560]{2,1,0:T(8,128)S(1)} %get-tuple-element.26), channel_id=1, source_target_pairs={{0,16},{16,0},{32,48},{48,32},{64,80},{80,64},{96,112},{112,96},{1... | collective-permute-start | bytes 5898248 | tf_op jit(solution)/shard_map/ppermute | solution.py:70
  24.8 14.0 %collective-permute-start.10 = (f32[32,2560]{1,0:T(8,128)S(1)}, f32[32,2560]{1,0:T(8,128)S(1)}, u32[]{:S(2)}, u32[]{:S(2)}) collective-permute-start(f32[32,2560]{1,0:T(8,128)S(1)} %shard_map.76.refs_1_), channel_id=1, source_target_pairs={{0,32},{16,240},{32,64},{48,16},{64,96},{80,48},{96,128},{112,80},... | collective-permute-start | bytes 983048 | tf_op jit(solution)/shard_map/ppermute | solution.py:170
  29.1 14.0 %collective-permute-start.9 = (f32[32,2560]{1,0:T(8,128)S(1)}, f32[32,2560]{1,0:T(8,128)S(1)}, u32[]{:S(2)}, u32[]{:S(2)}) collective-permute-start(f32[32,2560]{1,0:T(8,128)S(1)} %shard_map.77.refs_1_), channel_id=1, source_target_pairs={{32,0},{240,16},{64,32},{16,48},{96,64},{48,80},{128,96},{80,112},... | collective-permute-start | bytes 983048 | tf_op jit(solution)/shard_map/ppermute | solution.py:173
  31.8 14.0 %collective-permute-start.16 = (f32[32,2560]{1,0:T(8,128)S(1)}, f32[32,2560]{1,0:T(8,128)S(1)}, u32[]{:S(2)}, u32[]{:S(2)}) collective-permute-start(f32[32,2560]{1,0:T(8,128)S(1)} %shard_map.78.refs_1_), channel_id=1, source_target_pairs={{0,32},{16,240},{32,64},{48,16},{64,96},{80,48},{96,128},{112,80},... | collective-permute-start | bytes 983048 | tf_op jit(solution)/shard_map/ppermute | solution.py:170
  36.1 14.0 %collective-permute-start.15 = (f32[32,2560]{1,0:T(8,128)S(1)}, f32[32,2560]{1,0:T(8,128)S(1)}, u32[]{:S(2)}, u32[]{:S(2)}) collective-permute-start(f32[32,2560]{1,0:T(8,128)S(1)} %shard_map.79.refs_1_), channel_id=1, source_target_pairs={{32,0},{240,16},{64,32},{16,48},{96,64},{48,80},{128,96},{80,112},... | collective-permute-start | bytes 983048 | tf_op jit(solution)/shard_map/ppermute | solution.py:173
  38.8 18.3 %collective-permute-start.14 = (f32[32,2560]{1,0:T(8,128)S(1)}, f32[32,2560]{1,0:T(8,128)S(1)}, u32[]{:S(2)}, u32[]{:S(2)}) collective-permute-start(f32[32,2560]{1,0:T(8,128)S(1)} %shard_map.80.refs_1_), channel_id=1, source_target_pairs={{0,32},{16,240},{32,64},{48,16},{64,96},{80,48},{96,128},{112,80},... | collective-permute-start | bytes 983048 | tf_op jit(solution)/shard_map/ppermute | solution.py:170
  43.2 14.0 %collective-permute-start.13 = (f32[32,2560]{1,0:T(8,128)S(1)}, f32[32,2560]{1,0:T(8,128)S(1)}, u32[]{:S(2)}, u32[]{:S(2)}) collective-permute-start(f32[32,2560]{1,0:T(8,128)S(1)} %shard_map.81.refs_1_), channel_id=1, source_target_pairs={{32,0},{240,16},{64,32},{16,48},{96,64},{48,80},{128,96},{80,112},... | collective-permute-start | bytes 983048 | tf_op jit(solution)/shard_map/ppermute | solution.py:173
  45.9 14.0 %collective-permute-start.17 = (f32[32,2560]{1,0:T(8,128)S(1)}, f32[32,2560]{1,0:T(8,128)S(1)}, u32[]{:S(2)}, u32[]{:S(2)}) collective-permute-start(f32[32,2560]{1,0:T(8,128)S(1)} %shard_map.82.refs_1_), channel_id=1, source_target_pairs={{0,32},{16,240},{32,64},{48,16},{64,96},{80,48},{96,128},{112,80},... | collective-permute-start | bytes 983048 | tf_op jit(solution)/shard_map/ppermute | solution.py:170
  50.2 11.2 %collective-permute-start.18 = (f32[32,2560]{1,0:T(8,128)S(1)}, f32[32,2560]{1,0:T(8,128)S(1)}, u32[]{:S(2)}, u32[]{:S(2)}) collective-permute-start(f32[32,2560]{1,0:T(8,128)S(1)} %shard_map.83._), channel_id=1, source_target_pairs={{32,0},{240,16},{64,32},{16,48},{96,64},{48,80},{128,96},{80,112},... | collective-permute-start | bytes 983048 | tf_op jit(solution)/shard_map/ppermute | solution.py:173
  63.0 7.0 %collective-permute-start.23 = (f32[64,2560]{1,0:T(8,128)S(1)}, f32[64,2560]{1,0:T(8,128)S(1)}, u32[]{:S(2)}, u32[]{:S(2)}) collective-permute-start(f32[64,2560]{1,0:T(8,128)S(1)} %pad_maximum_fusion), channel_id=1, source_target_pairs={{0,16},{16,0},{32,48},{48,32},{64,80},{80,64},{96,112},{112,96},{1... | collective-permute-start | bytes 1966088 | tf_op jit(solution)/shard_map/ppermute | solution.py:211
  63.3 3.9 %collective-permute-start.22 = (f32[128]{0:T(128)S(1)}, f32[128]{0:T(128)S(1)}, u32[]{:S(2)}, u32[]{:S(2)}) collective-permute-start(f32[128]{0:T(128)S(1)} %pad_maximum_fusion.4), channel_id=1, source_target_pairs={{0,4},{1,5},{2,6},{3,7},{4,0},{5,1},{6,2},{7,3},{8,12},{9,13},{10,... | collective-permute-start | bytes 1544 | tf_op jit(solution)/shard_map/ppermute | solution.py:153
  70.1 4.1 %collective-permute-start.24 = (f32[5248]{0:T(1024)S(1)}, f32[5248]{0:T(1024)S(1)}, u32[]{:S(2)}, u32[]{:S(2)}) collective-permute-start(f32[5248]{0:T(1024)S(1)} %pad_maximum_fusion.1), channel_id=1, source_target_pairs={{0,1},{1,0},{2,3},{3,2},{4,5},{5,4},{6,7},{7,6},{8,9},{9,8},{10,11... | collective-permute-start | bytes 62984 | tf_op jit(solution)/shard_map/ppermute | solution.py:153
  75.7 4.6 %collective-permute-start.26 = (f32[5248]{0:T(1024)S(1)}, f32[5248]{0:T(1024)S(1)}, u32[]{:S(2)}, u32[]{:S(2)}) collective-permute-start(f32[5248]{0:T(1024)S(1)} %fusion.8), channel_id=1, source_target_pairs={{0,1},{1,0},{2,3},{3,2},{4,5},{5,4},{6,7},{7,6},{8,9},{9,8},{10,11... | collective-permute-start | bytes 62984 | tf_op jit(solution)/shard_map/ppermute | solution.py:153
  80.3 4.3 %collective-permute-start.30 = (f32[5248]{0:T(1024)S(1)}, f32[5248]{0:T(1024)S(1)}, u32[]{:S(2)}, u32[]{:S(2)}) collective-permute-start(f32[5248]{0:T(1024)S(1)} %add_add_fusion.1), channel_id=1, source_target_pairs={{0,1},{1,0},{2,3},{3,2},{4,5},{5,4},{6,7},{7,6},{8,9},{9,8},{10,11... | collective-permute-start | bytes 62984 | tf_op jit(solution)/shard_map/ppermute | solution.py:153
  87.2 4.0 %collective-permute-start.33 = (f32[128]{0:T(128)S(1)}, f32[128]{0:T(128)S(1)}, u32[]{:S(2)}, u32[]{:S(2)}) collective-permute-start(f32[128]{0:T(128)S(1)} %get-tuple-element.38), channel_id=1, source_target_pairs={{0,4},{1,5},{2,6},{3,7},{4,0},{5,1},{6,2},{7,3},{8,12},{9,13},{10,... | collective-permute-start | bytes 1544 | tf_op jit(solution)/shard_map/ppermute | solution.py:153
  (15 other events, 64.3 us)

commit v8 on v6

--- a/solution.py
+++ b/solution.py
@@ -25,6 +25,10 @@
 
 def told(micros):
     return pl.CostEstimate(flops=int(micros * 1.15e9), bytes_accessed=0, transcendentals=0)
+
+
+def swap(x):
+    return lax.ppermute(x, "dp", SWAP)
 
 
 def fetch_kernel(ks, split, n_in, parts, *refs):
@@ -67,7 +71,7 @@
         compiler_params=PARAMS,
         cost_estimate=told(micros),
     )(parts, *after)
-    return own, *(lax.ppermute(x, "dp", SWAP) for x in sent)
+    return own, *sent
 
 
 def add_kernel(terms, n_in, own, sib, *refs):
@@ -113,8 +117,8 @@
     rms[...] = update_rms
     factor = jnp.sqrt(row_mean) / jnp.maximum(1.0, update_rms)
     copies = []
-    for i in range(4):
-        rows = pl.ds(16 * i, 16)
+    for i in range(8):
+        rows = pl.ds(8 * i, 8)
         buf[rows] = scaled[rows] * factor
         copies.append(pltpu.make_async_copy(buf.at[rows], out.at[rows], sems.at[i]))
         copies[i].start()
@@ -131,7 +135,7 @@
         ],
         in_specs=[VMEM, VMEM, VMEM],
         out_specs=[HBM, VMEM],
-        scratch_shapes=[pltpu.VMEM((ROWS, COLS), jnp.float32), pltpu.SemaphoreType.DMA((4,))],
+        scratch_shapes=[pltpu.VMEM((ROWS, COLS), jnp.float32), pltpu.SemaphoreType.DMA((8,))],
         compiler_params=PARAMS,
         cost_estimate=told(1),
     )(scaled, row_sum, total)
@@ -172,9 +176,12 @@
     def down(x):
         return lax.ppermute(x, "dp", DOWN)
 
-    far, far_up, far_down = fetch((4,), parts, split=2)
+    far, *sent = fetch((4,), parts, split=2)
+    far_up, far_down = (swap(x) for x in sent)
     third = fetch((3, -3), parts, far, micros=12)
     (a,) = add((far, far_up), ((0, 0),), after=(third[0],))
+    sent, a = lax.optimization_barrier((third[1], a))
+    third = third[0], swap(sent)
     after = a
     a = up(a)
     (b,) = add((far, far_down), ((0, 1),), after=(after,))
@@ -183,8 +190,10 @@
     (c,) = add(third, ((0, 1),), after=(after,))
     (d,) = add(third, ((1, 0),), after=(c,))
     after = d
-    second = fetch((2, -2), parts, after)
-    near = fetch((1, -1, 0), parts, second[0])
+    own, sent = fetch((2, -2), parts, after)
+    second = own, swap(sent)
+    own, sent = fetch((1, -1, 0), parts, second[0])
+    near = own, swap(sent)
     after = near[0]
     c, d = up(c), down(d)
     steps = [

time: 94.6 us -> 94.4 us (level)
  no operation moved by 1% of the time
where the time goes in v8:
time: 94.4 us; the launch traced here: 94.2 us
  starting transfers between devices  45.8 us (49%)
  waiting for transfers between devices  38.4 us (41%)
  Pallas kernels  7.53 us (8%)
  between operations  1.15 us (1%)
  other arithmetic  1.13 us (1%)
    ppermute x7, starting transfers between devices, up(): return lax.ppermute(x, 'dp', UP)  24.2 us
    ppermute x13, starting transfers between devices, exchange(): return lax.ppermute(v, ('dp', 'row', 'col'), pairs)  15.6 us
    ppermute x7, waiting for transfers between devices, up(): return lax.ppermute(x, 'dp', UP)  13.1 us
    ppermute x13, waiting for transfers between devices, exchange(): return lax.ppermute(v, ('dp', 'row', 'col'), pairs)  11.5 us
    ppermute x7, waiting for transfers between devices, down(): return lax.ppermute(x, 'dp', DOWN)  11.5 us
    pallas_call x4, Pallas kernels, fetch(): pl.pallas_call(functools.partial(fetch_kernel, ks, split, len(after)), ou...  5.24 us
    ppermute x5, starting transfers between devices, swap(): return lax.ppermute(x, 'dp', SWAP)  4.96 us
  transfers between devices with their start and end apart: 35, of which 24 were waited for; matrix products, arithmetic and copies ran while one was open for 0% of the time, Pallas kernels for 5%

profile of v8, /device:TPU:1, one launch (start us, length us, event | category | flops | bytes accessed | tf_op | source)
XLA Modules:
  0.0 94.2 jit_solution(5338368622105716080)
XLA Ops:
  1.7 3.3 %collective-permute-start = (f32[1,32,2560]{2,1,0:T(8,128)S(1)}, f32[1,32,2560]{2,1,0:T(8,128)S(1)}, u32[]{:S(2)}, u32[]{:S(2)}) collective-permute-start(f32[1,32,2560]{2,1,0:T(8,128)S(1)} %get-tuple-element.24), channel_id=1, source_target_pairs={{0,16},{16,0},{32,48},{48,32},{64,80},{80,64},{96,112},{112,96},{1... | collective-permute-start | bytes 983048 | tf_op jit(solution)/shard_map/ppermute | solution.py:31
  7.0 3.8 %collective-permute-start.8 = (f32[32,2560]{1,0:T(8,128)S(1)}, f32[32,2560]{1,0:T(8,128)S(1)}, u32[]{:S(2)}, u32[]{:S(2)}) collective-permute-start(f32[32,2560]{1,0:T(8,128)S(1)} %shard_map.68.refs_0_), channel_id=1, source_target_pairs={{0,32},{16,240},{32,64},{48,16},{64,96},{80,48},{96,128},{112,80},... | collective-permute-start | bytes 983048 | tf_op jit(solution)/shard_map/ppermute | solution.py:174
  11.0 2.7 %collective-permute-start.6 = (f32[32,2560]{1,0:T(8,128)S(1)}, f32[32,2560]{1,0:T(8,128)S(1)}, u32[]{:S(2)}, u32[]{:S(2)}) collective-permute-start(f32[32,2560]{1,0:T(8,128)S(1)} %shard_map.70.refs_0_), channel_id=1, source_target_pairs={{0,32},{16,240},{32,64},{48,16},{64,96},{80,48},{96,128},{112,80},... | collective-permute-start | bytes 983048 | tf_op jit(solution)/shard_map/ppermute | solution.py:174
  13.9 1.3 %shard_map.72 = (bf16[2,64,2560]{2,1,0:T(8,128)(2,1)S(1)}, f32[2,64,2560]{2,1,0:T(8,128)S(1)}) custom-call(bf16[16,64,2560]{2,1,0:T(8,128)(2,1)} %bitcast.18, f32[32,2560]{1,0:T(8,128)S(1)} %shard_map.71.refs_0_), custom_call_target="tpu_custom_call" | custom-call | tf_op jit(solution)/shard_map/pallas_call | solution.py:60
  16.3 1.5 %shard_map.73 = (bf16[3,64,2560]{2,1,0:T(8,128)(2,1)S(1)}, f32[3,64,2560]{2,1,0:T(8,128)S(1)}) custom-call(bf16[16,64,2560]{2,1,0:T(8,128)(2,1)} %bitcast.19, bf16[2,64,2560]{2,1,0:T(8,128)(2,1)S(1)} %get-tuple-element.28.refs_0_.own), custom_call_target="tpu_custom_call" | custom-call | tf_op jit(solution)/shard_map/pallas_call | solution.py:60
  17.9 3.4 %collective-permute-start.12 = (f32[32,2560]{1,0:T(8,128)S(1)}, f32[32,2560]{1,0:T(8,128)S(1)}, u32[]{:S(2)}, u32[]{:S(2)}) collective-permute-start(f32[32,2560]{1,0:T(8,128)S(1)} %shard_map.74.refs_1_), channel_id=1, source_target_pairs={{0,32},{16,240},{32,64},{48,16},{64,96},{80,48},{96,128},{112,80},... | collective-permute-start | bytes 983048 | tf_op jit(solution)/shard_map/ppermute | solution.py:174
  22.1 2.6 %collective-permute-done.6.refs_0_ = f32[32,2560]{1,0:T(8,128)S(1)} collective-permute-done((f32[32,2560]{1,0:T(8,128)S(1)}, f32[32,2560]{1,0:T(8,128)S(1)}, u32[]{:S(2)}, u32[]{:S(2)}) %collective-permute-start.6) | collective-permute-done | bytes 327712 | tf_op jit(solution)/shard_map/ppermute | solution.py:174
  24.8 3.6 %collective-permute-start.10 = (f32[32,2560]{1,0:T(8,128)S(1)}, f32[32,2560]{1,0:T(8,128)S(1)}, u32[]{:S(2)}, u32[]{:S(2)}) collective-permute-start(f32[32,2560]{1,0:T(8,128)S(1)} %shard_map.76.refs_1_), channel_id=1, source_target_pairs={{0,32},{16,240},{32,64},{48,16},{64,96},{80,48},{96,128},{112,80},... | collective-permute-start | bytes 983048 | tf_op jit(solution)/shard_map/ppermute | solution.py:174
  29.1 2.6 %collective-permute-done.12.refs_0_ = f32[32,2560]{1,0:T(8,128)S(1)} collective-permute-done((f32[32,2560]{1,0:T(8,128)S(1)}, f32[32,2560]{1,0:T(8,128)S(1)}, u32[]{:S(2)}, u32[]{:S(2)}) %collective-permute-start.12) | collective-permute-done | bytes 327712 | tf_op jit(solution)/shard_map/ppermute | solution.py:174
  31.8 3.5 %collective-permute-start.16 = (f32[32,2560]{1,0:T(8,128)S(1)}, f32[32,2560]{1,0:T(8,128)S(1)}, u32[]{:S(2)}, u32[]{:S(2)}) collective-permute-start(f32[32,2560]{1,0:T(8,128)S(1)} %shard_map.78.refs_1_), channel_id=1, source_target_pairs={{0,32},{16,240},{32,64},{48,16},{64,96},{80,48},{96,128},{112,80},... | collective-permute-start | bytes 983048 | tf_op jit(solution)/shard_map/ppermute | solution.py:174
  36.2 2.6 %collective-permute-done.10.refs_0_ = f32[32,2560]{1,0:T(8,128)S(1)} collective-permute-done((f32[32,2560]{1,0:T(8,128)S(1)}, f32[32,2560]{1,0:T(8,128)S(1)}, u32[]{:S(2)}, u32[]{:S(2)}) %collective-permute-start.10) | collective-permute-done | bytes 327712 | tf_op jit(solution)/shard_map/ppermute | solution.py:174
  38.9 3.7 %collective-permute-start.14 = (f32[32,2560]{1,0:T(8,128)S(1)}, f32[32,2560]{1,0:T(8,128)S(1)}, u32[]{:S(2)}, u32[]{:S(2)}) collective-permute-start(f32[32,2560]{1,0:T(8,128)S(1)} %shard_map.80.refs_1_), channel_id=1, source_target_pairs={{0,32},{16,240},{32,64},{48,16},{64,96},{80,48},{96,128},{112,80},... | collective-permute-start | bytes 983048 | tf_op jit(solution)/shard_map/ppermute | solution.py:174
  43.2 2.6 %collective-permute-done.16.refs_0_ = f32[32,2560]{1,0:T(8,128)S(1)} collective-permute-done((f32[32,2560]{1,0:T(8,128)S(1)}, f32[32,2560]{1,0:T(8,128)S(1)}, u32[]{:S(2)}, u32[]{:S(2)}) %collective-permute-start.16) | collective-permute-done | bytes 327712 | tf_op jit(solution)/shard_map/ppermute | solution.py:174
  45.9 3.5 %collective-permute-start.17 = (f32[32,2560]{1,0:T(8,128)S(1)}, f32[32,2560]{1,0:T(8,128)S(1)}, u32[]{:S(2)}, u32[]{:S(2)}) collective-permute-start(f32[32,2560]{1,0:T(8,128)S(1)} %shard_map.82.refs_1_), channel_id=1, source_target_pairs={{0,32},{16,240},{32,64},{48,16},{64,96},{80,48},{96,128},{112,80},... | collective-permute-start | bytes 983048 | tf_op jit(solution)/shard_map/ppermute | solution.py:174
  50.2 6.9 %collective-permute-done.13.refs_0_ = f32[32,2560]{1,0:T(8,128)S(1)} collective-permute-done((f32[32,2560]{1,0:T(8,128)S(1)}, f32[32,2560]{1,0:T(8,128)S(1)}, u32[]{:S(2)}, u32[]{:S(2)}) %collective-permute-start.13) | collective-permute-done | bytes 327712 | tf_op jit(solution)/shard_map/ppermute | solution.py:177
  57.2 2.7 %collective-permute-done.17 = f32[32,2560]{1,0:T(8,128)S(1)} collective-permute-done((f32[32,2560]{1,0:T(8,128)S(1)}, f32[32,2560]{1,0:T(8,128)S(1)}, u32[]{:S(2)}, u32[]{:S(2)}) %collective-permute-start.17) | collective-permute-done | bytes 327712 | tf_op jit(solution)/shard_map/ppermute | solution.py:174
  59.9 1.4 %collective-permute-done.18 = f32[32,2560]{1,0:T(8,128)S(1)} collective-permute-done((f32[32,2560]{1,0:T(8,128)S(1)}, f32[32,2560]{1,0:T(8,128)S(1)}, u32[]{:S(2)}, u32[]{:S(2)}) %collective-permute-start.18) | collective-permute-done | bytes 327712 | tf_op jit(solution)/shard_map/ppermute | solution.py:177
  63.1 2.8 %collective-permute-start.22 = (f32[128]{0:T(128)S(1)}, f32[128]{0:T(128)S(1)}, u32[]{:S(2)}, u32[]{:S(2)}) collective-permute-start(f32[128]{0:T(128)S(1)} %pad_maximum_fusion.4), channel_id=1, source_target_pairs={{0,4},{1,5},{2,6},{3,7},{4,0},{5,1},{6,2},{7,3},{8,12},{9,13},{10,... | collective-permute-start | bytes 1544 | tf_op jit(solution)/shard_map/ppermute | solution.py:157
  67.0 2.5 %collective-permute-done.21 = f32[128]{0:T(128)S(1)} collective-permute-done((f32[128]{0:T(128)S(1)}, f32[128]{0:T(128)S(1)}, u32[]{:S(2)}, u32[]{:S(2)}) %collective-permute-start.21) | collective-permute-done | bytes 544 | tf_op jit(solution)/shard_map/ppermute | solution.py:157
  70.1 1.9 %collective-permute-start.25 = (f32[5248]{0:T(1024)S(1)}, f32[5248]{0:T(1024)S(1)}, u32[]{:S(2)}, u32[]{:S(2)}) collective-permute-start(f32[5248]{0:T(1024)S(1)} %pad_maximum_fusion.1), channel_id=1, source_target_pairs={{0,1},{1,0},{2,3},{3,2},{4,5},{5,4},{6,7},{7,6},{8,9},{9,8},{10,11... | collective-permute-start | bytes 62984 | tf_op jit(solution)/shard_map/ppermute | solution.py:157
  75.1 2.9 %collective-permute-start.27 = (f32[5248]{0:T(1024)S(1)}, f32[5248]{0:T(1024)S(1)}, u32[]{:S(2)}, u32[]{:S(2)}) collective-permute-start(f32[5248]{0:T(1024)S(1)} %add_add_fusion.1), channel_id=1, source_target_pairs={{0,1},{1,0},{2,3},{3,2},{4,5},{5,4},{6,7},{7,6},{8,9},{9,8},{10,11... | collective-permute-start | bytes 62984 | tf_op jit(solution)/shard_map/ppermute | solution.py:157
  79.1 2.9 %collective-permute-start.30 = (f32[5248]{0:T(1024)S(1)}, f32[5248]{0:T(1024)S(1)}, u32[]{:S(2)}, u32[]{:S(2)}) collective-permute-start(f32[5248]{0:T(1024)S(1)} %add.77), channel_id=1, source_target_pairs={{0,1},{1,0},{2,3},{3,2},{4,5},{5,4},{6,7},{7,6},{8,9},{9,8},{10,11... | collective-permute-start | bytes 62984 | tf_op jit(solution)/shard_map/ppermute | solution.py:157
  83.3 2.6 %collective-permute-done.29 = f32[5248]{0:T(1024)S(1)} collective-permute-done((f32[5248]{0:T(1024)S(1)}, f32[5248]{0:T(1024)S(1)}, u32[]{:S(2)}, u32[]{:S(2)}) %collective-permute-start.29) | collective-permute-done | bytes 21024 | tf_op jit(solution)/shard_map/ppermute | solution.py:157
  92.4 1.6 %shard_map.86 = (f32[64,2560]{1,0:T(8,128)}, f32[1,1]{1,0:T(1,128)}) custom-call(f32[64,2560]{1,0:T(8,128)S(1)} %rsqrt_multiply_fusion.scaled, f32[1,128]{1,0:T(1,128)S(1)} %get-tuple-element.47.row_sum, f32[1,128]{1,0:T(1,128)S(1)} %get-tuple-element.46.total), custom_call_target="tpu_custom_call" | custom-call | flops 1150000000 | tf_op jit(solution)/shard_map/pallas_call | solution.py:130
  (100 shorter events, 24.2 us)
Async XLA Ops:
  1.7 4.7 %collective-permute-start = (f32[1,32,2560]{2,1,0:T(8,128)S(1)}, f32[1,32,2560]{2,1,0:T(8,128)S(1)}, u32[]{:S(2)}, u32[]{:S(2)}) collective-permute-start(f32[1,32,2560]{2,1,0:T(8,128)S(1)} %get-tuple-element.24), channel_id=1, source_target_pairs={{0,16},{16,0},{32,48},{48,32},{64,80},{80,64},{96,112},{112,96},{1... | collective-permute-start | bytes 983048 | tf_op jit(solution)/shard_map/ppermute | solution.py:31
  5.1 5.8 %collective-permute-start.2 = (f32[1,32,2560]{2,1,0:T(8,128)S(1)}, f32[1,32,2560]{2,1,0:T(8,128)S(1)}, u32[]{:S(2)}, u32[]{:S(2)}) collective-permute-start(f32[1,32,2560]{2,1,0:T(8,128)S(1)} %get-tuple-element.26), channel_id=1, source_target_pairs={{0,16},{16,0},{32,48},{48,32},{64,80},{80,64},{96,112},{112,96},{1... | collective-permute-start | bytes 983048 | tf_op jit(solution)/shard_map/ppermute | solution.py:31
  6.5 4.5 %collective-permute-start.1 = (f32[2,64,2560]{2,1,0:T(8,128)S(1)}, f32[2,64,2560]{2,1,0:T(8,128)S(1)}, u32[]{:S(2)}, u32[]{:S(2)}) collective-permute-start(f32[2,64,2560]{2,1,0:T(8,128)S(1)} %get-tuple-element.25), channel_id=1, source_target_pairs={{0,16},{16,0},{32,48},{48,32},{64,80},{80,64},{96,112},{112,96},{1... | collective-permute-start | bytes 3932168 | tf_op jit(solution)/shard_map/ppermute | solution.py:31
  7.0 10.8 %collective-permute-start.8 = (f32[32,2560]{1,0:T(8,128)S(1)}, f32[32,2560]{1,0:T(8,128)S(1)}, u32[]{:S(2)}, u32[]{:S(2)}) collective-permute-start(f32[32,2560]{1,0:T(8,128)S(1)} %shard_map.68.refs_0_), channel_id=1, source_target_pairs={{0,32},{16,240},{32,64},{48,16},{64,96},{80,48},{96,128},{112,80},... | collective-permute-start | bytes 983048 | tf_op jit(solution)/shard_map/ppermute | solution.py:174
  10.9 11.1 %collective-permute-start.7 = (f32[32,2560]{1,0:T(8,128)S(1)}, f32[32,2560]{1,0:T(8,128)S(1)}, u32[]{:S(2)}, u32[]{:S(2)}) collective-permute-start(f32[32,2560]{1,0:T(8,128)S(1)} %shard_map.69.refs_0_), channel_id=1, source_target_pairs={{32,0},{240,16},{64,32},{16,48},{96,64},{48,80},{128,96},{80,112},... | collective-permute-start | bytes 983048 | tf_op jit(solution)/shard_map/ppermute | solution.py:177
  11.0 13.7 %collective-permute-start.6 = (f32[32,2560]{1,0:T(8,128)S(1)}, f32[32,2560]{1,0:T(8,128)S(1)}, u32[]{:S(2)}, u32[]{:S(2)}) collective-permute-start(f32[32,2560]{1,0:T(8,128)S(1)} %shard_map.70.refs_0_), channel_id=1, source_target_pairs={{0,32},{16,240},{32,64},{48,16},{64,96},{80,48},{96,128},{112,80},... | collective-permute-start | bytes 983048 | tf_op jit(solution)/shard_map/ppermute | solution.py:174
  13.8 15.2 %collective-permute-start.5 = (f32[32,2560]{1,0:T(8,128)S(1)}, f32[32,2560]{1,0:T(8,128)S(1)}, u32[]{:S(2)}, u32[]{:S(2)}) collective-permute-start(f32[32,2560]{1,0:T(8,128)S(1)} %shard_map.71.refs_0_), channel_id=1, source_target_pairs={{32,0},{240,16},{64,32},{16,48},{96,64},{48,80},{128,96},{80,112},... | collective-permute-start | bytes 983048 | tf_op jit(solution)/shard_map/ppermute | solution.py:177
  15.2 9.5 %collective-permute-start.4 = (f32[2,64,2560]{2,1,0:T(8,128)S(1)}, f32[2,64,2560]{2,1,0:T(8,128)S(1)}, u32[]{:S(2)}, u32[]{:S(2)}) collective-permute-start(f32[2,64,2560]{2,1,0:T(8,128)S(1)} %get-tuple-element.31), channel_id=1, source_target_pairs={{0,16},{16,0},{32,48},{48,32},{64,80},{80,64},{96,112},{112,96},{1... | collective-permute-start | bytes 3932168 | tf_op jit(solution)/shard_map/ppermute | solution.py:31
  17.9 13.9 %collective-permute-start.12 = (f32[32,2560]{1,0:T(8,128)S(1)}, f32[32,2560]{1,0:T(8,128)S(1)}, u32[]{:S(2)}, u32[]{:S(2)}) collective-permute-start(f32[32,2560]{1,0:T(8,128)S(1)} %shard_map.74.refs_1_), channel_id=1, source_target_pairs={{0,32},{16,240},{32,64},{48,16},{64,96},{80,48},{96,128},{112,80},... | collective-permute-start | bytes 983048 | tf_op jit(solution)/shard_map/ppermute | solution.py:174
  22.0 14.0 %collective-permute-start.11 = (f32[32,2560]{1,0:T(8,128)S(1)}, f32[32,2560]{1,0:T(8,128)S(1)}, u32[]{:S(2)}, u32[]{:S(2)}) collective-permute-start(f32[32,2560]{1,0:T(8,128)S(1)} %shard_map.75.refs_1_), channel_id=1, source_target_pairs={{32,0},{240,16},{64,32},{16,48},{96,64},{48,80},{128,96},{80,112},... | collective-permute-start | bytes 983048 | tf_op jit(solution)/shard_map/ppermute | solution.py:177
  24.8 14.0 %collective-permute-start.3 = (f32[3,64,2560]{2,1,0:T(8,128)S(1)}, f32[3,64,2560]{2,1,0:T(8,128)S(1)}, u32[]{:S(2)}, u32[]{:S(2)}) collective-permute-start(f32[3,64,2560]{2,1,0:T(8,128)S(1)} %get-tuple-element.30), channel_id=1, source_target_pairs={{0,16},{16,0},{32,48},{48,32},{64,80},{80,64},{96,112},{112,96},{1... | collective-permute-start | bytes 5898248 | tf_op jit(solution)/shard_map/ppermute | solution.py:31
  24.8 14.0 %collective-permute-start.10 = (f32[32,2560]{1,0:T(8,128)S(1)}, f32[32,2560]{1,0:T(8,128)S(1)}, u32[]{:S(2)}, u32[]{:S(2)}) collective-permute-start(f32[32,2560]{1,0:T(8,128)S(1)} %shard_map.76.refs_1_), channel_id=1, source_target_pairs={{0,32},{16,240},{32,64},{48,16},{64,96},{80,48},{96,128},{112,80},... | collective-permute-start | bytes 983048 | tf_op jit(solution)/shard_map/ppermute | solution.py:174
  29.1 14.0 %collective-permute-start.9 = (f32[32,2560]{1,0:T(8,128)S(1)}, f32[32,2560]{1,0:T(8,128)S(1)}, u32[]{:S(2)}, u32[]{:S(2)}) collective-permute-start(f32[32,2560]{1,0:T(8,128)S(1)} %shard_map.77.refs_1_), channel_id=1, source_target_pairs={{32,0},{240,16},{64,32},{16,48},{96,64},{48,80},{128,96},{80,112},... | collective-permute-start | bytes 983048 | tf_op jit(solution)/shard_map/ppermute | solution.py:177
  31.8 14.0 %collective-permute-start.16 = (f32[32,2560]{1,0:T(8,128)S(1)}, f32[32,2560]{1,0:T(8,128)S(1)}, u32[]{:S(2)}, u32[]{:S(2)}) collective-permute-start(f32[32,2560]{1,0:T(8,128)S(1)} %shard_map.78.refs_1_), channel_id=1, source_target_pairs={{0,32},{16,240},{32,64},{48,16},{64,96},{80,48},{96,128},{112,80},... | collective-permute-start | bytes 983048 | tf_op jit(solution)/shard_map/ppermute | solution.py:174
  36.1 14.0 %collective-permute-start.15 = (f32[32,2560]{1,0:T(8,128)S(1)}, f32[32,2560]{1,0:T(8,128)S(1)}, u32[]{:S(2)}, u32[]{:S(2)}) collective-permute-start(f32[32,2560]{1,0:T(8,128)S(1)} %shard_map.79.refs_1_), channel_id=1, source_target_pairs={{32,0},{240,16},{64,32},{16,48},{96,64},{48,80},{128,96},{80,112},... | collective-permute-start | bytes 983048 | tf_op jit(solution)/shard_map/ppermute | solution.py:177
  38.9 18.2 %collective-permute-start.14 = (f32[32,2560]{1,0:T(8,128)S(1)}, f32[32,2560]{1,0:T(8,128)S(1)}, u32[]{:S(2)}, u32[]{:S(2)}) collective-permute-start(f32[32,2560]{1,0:T(8,128)S(1)} %shard_map.80.refs_1_), channel_id=1, source_target_pairs={{0,32},{16,240},{32,64},{48,16},{64,96},{80,48},{96,128},{112,80},... | collective-permute-start | bytes 983048 | tf_op jit(solution)/shard_map/ppermute | solution.py:174
  43.1 14.0 %collective-permute-start.13 = (f32[32,2560]{1,0:T(8,128)S(1)}, f32[32,2560]{1,0:T(8,128)S(1)}, u32[]{:S(2)}, u32[]{:S(2)}) collective-permute-start(f32[32,2560]{1,0:T(8,128)S(1)} %shard_map.81.refs_1_), channel_id=1, source_target_pairs={{32,0},{240,16},{64,32},{16,48},{96,64},{48,80},{128,96},{80,112},... | collective-permute-start | bytes 983048 | tf_op jit(solution)/shard_map/ppermute | solution.py:177
  45.9 14.0 %collective-permute-start.17 = (f32[32,2560]{1,0:T(8,128)S(1)}, f32[32,2560]{1,0:T(8,128)S(1)}, u32[]{:S(2)}, u32[]{:S(2)}) collective-permute-start(f32[32,2560]{1,0:T(8,128)S(1)} %shard_map.82.refs_1_), channel_id=1, source_target_pairs={{0,32},{16,240},{32,64},{48,16},{64,96},{80,48},{96,128},{112,80},... | collective-permute-start | bytes 983048 | tf_op jit(solution)/shard_map/ppermute | solution.py:174
  50.1 11.1 %collective-permute-start.18 = (f32[32,2560]{1,0:T(8,128)S(1)}, f32[32,2560]{1,0:T(8,128)S(1)}, u32[]{:S(2)}, u32[]{:S(2)}) collective-permute-start(f32[32,2560]{1,0:T(8,128)S(1)} %shard_map.83._), channel_id=1, source_target_pairs={{32,0},{240,16},{64,32},{16,48},{96,64},{48,80},{128,96},{80,112},... | collective-permute-start | bytes 983048 | tf_op jit(solution)/shard_map/ppermute | solution.py:177
  62.8 7.0 %collective-permute-start.23 = (f32[64,2560]{1,0:T(8,128)S(1)}, f32[64,2560]{1,0:T(8,128)S(1)}, u32[]{:S(2)}, u32[]{:S(2)}) collective-permute-start(f32[64,2560]{1,0:T(8,128)S(1)} %pad_maximum_fusion), channel_id=1, source_target_pairs={{0,16},{16,0},{32,48},{48,32},{64,80},{80,64},{96,112},{112,96},{1... | collective-permute-start | bytes 1966088 | tf_op jit(solution)/shard_map/ppermute | solution.py:220
  70.1 4.8 %collective-permute-start.25 = (f32[5248]{0:T(1024)S(1)}, f32[5248]{0:T(1024)S(1)}, u32[]{:S(2)}, u32[]{:S(2)}) collective-permute-start(f32[5248]{0:T(1024)S(1)} %pad_maximum_fusion.1), channel_id=1, source_target_pairs={{0,1},{1,0},{2,3},{3,2},{4,5},{5,4},{6,7},{7,6},{8,9},{9,8},{10,11... | collective-permute-start | bytes 62984 | tf_op jit(solution)/shard_map/ppermute | solution.py:157
  75.1 4.1 %collective-permute-start.27 = (f32[5248]{0:T(1024)S(1)}, f32[5248]{0:T(1024)S(1)}, u32[]{:S(2)}, u32[]{:S(2)}) collective-permute-start(f32[5248]{0:T(1024)S(1)} %add_add_fusion.1), channel_id=1, source_target_pairs={{0,1},{1,0},{2,3},{3,2},{4,5},{5,4},{6,7},{7,6},{8,9},{9,8},{10,11... | collective-permute-start | bytes 62984 | tf_op jit(solution)/shard_map/ppermute | solution.py:157
  79.1 4.2 %collective-permute-start.30 = (f32[5248]{0:T(1024)S(1)}, f32[5248]{0:T(1024)S(1)}, u32[]{:S(2)}, u32[]{:S(2)}) collective-permute-start(f32[5248]{0:T(1024)S(1)} %add.77), channel_id=1, source_target_pairs={{0,1},{1,0},{2,3},{3,2},{4,5},{5,4},{6,7},{7,6},{8,9},{9,8},{10,11... | collective-permute-start | bytes 62984 | tf_op jit(solution)/shard_map/ppermute | solution.py:157
  86.0 4.0 %collective-permute-start.33 = (f32[128]{0:T(128)S(1)}, f32[128]{0:T(128)S(1)}, u32[]{:S(2)}, u32[]{:S(2)}) collective-permute-start(f32[128]{0:T(128)S(1)} %get-tuple-element.42), channel_id=1, source_target_pairs={{0,4},{1,5},{2,6},{3,7},{4,0},{5,1},{6,2},{7,3},{8,12},{9,13},{10,... | collective-permute-start | bytes 1544 | tf_op jit(solution)/shard_map/ppermute | solution.py:157
  (15 other events, 65.3 us)
